TPU v7x, 32 devices: a whole 2x2x4 slice. The times are simulated.
32 devices in a mesh: row: 8 (over z, y), col: 4 (over x, core).
Axes of the slice: x: 2, y: 2, z: 4, core: 2. Of those that a mesh axis runs over, the one named last changes fastest.
Arguments:
- right_sides: bfloat16 [32768, 256], P(('row', 'col')), may hold values from -6 to 6
- tree_order: int32 [32768], P(('row', 'col')), may hold values from 0 to 32767, as said below
- leaf_inverse: bfloat16 [32, 2, 1024, 1024], P(('row', 'col'))
- leaf_basis: bfloat16 [32, 2, 1024, 256], P(('row', 'col')), may hold values from -0.125 to 0.125
- leaf_lift: bfloat16 [32, 2, 1024, 256], P(('row', 'col')), may hold values from -0.1875 to 0.1875
- node_inverse: bfloat16 [32, 5, 2, 512, 512], P(('row', 'col')), as said below
- node_basis: bfloat16 [32, 4, 2, 512, 256], P(('row', 'col')), as said below
- node_lift: bfloat16 [32, 4, 2, 512, 256], P(('row', 'col')), as said below
Outputs:
- solution: float32 [32768, 256], P(('row', 'col'))
Inputs may be any that keep to these rules, and one draw needn't show every extreme that they name: tree_order is a permutation. Initial row i lies on device i div 1024 and goes to device tree_order[i] div 1024; the number of rows that a device sends to the device o places further along row+col (cyclically) depends only on o, is at most 64, and reaches 64 for some o. node_inverse[d, k - 1] is the same for all d with the same d div 2^k. node_basis[d, k - 1] is the same for all d with the same d div 2^k. node_lift[d, k - 1] is the same for all d with the same d div 2^k.
All inputs are finite; a program needn't handle non-finite values.
Results may differ from a plain program's by a relative error of at most 0.0003.
Values may be sent and summed in bfloat16 or wider, within the bound.
No kernel may reach another device: no remote copies, remote signals or barrier semaphores. Data moves between devices by JAX's collectives and lax.ppermute only.
A program may use at most 128 MiB of HBM per device.

v0:
```python
import jax
import jax.numpy as jnp
from jax import lax
from jax.sharding import PartitionSpec as P

exactness = lax.Precision.HIGHEST


def from_partner(shard, axis, apart):
    return lax.ppermute(shard, axis, [(i, i ^ 1 << apart) for i in range(lax.axis_size(axis))])


def rotated(vectors):
    middle = vectors.shape[1] // 2
    return jnp.concatenate([-vectors[:, middle:], vectors[:, :middle]], axis=1)


def apply_complex(matrix, vectors):
    plain = jnp.dot(matrix[0].astype(jnp.float32), vectors, precision=exactness)
    return plain + jnp.dot(matrix[1].astype(jnp.float32), rotated(vectors), precision=exactness)


def apply_narrow(matrix, vectors):
    plain = jnp.dot(matrix[0], vectors, preferred_element_type=jnp.float32)
    return plain + jnp.dot(matrix[1], rotated(vectors), preferred_element_type=jnp.float32)


def apply_transposed(matrix, vectors):
    contract = (((0,), (0,)), ((), ()))
    plain = lax.dot_general(matrix[0].astype(jnp.float32), vectors, contract, precision=exactness)
    return plain + lax.dot_general(
        matrix[1].astype(jnp.float32), rotated(vectors), contract, precision=exactness
    )


def device_bit(height, col_levels):
    if height < col_levels:
        return lax.axis_index("col") >> height & 1
    return lax.axis_index("row") >> height - col_levels & 1


def per_device(
    right_sides,
    tree_order,
    leaf_inverse,
    leaf_basis,
    leaf_lift,
    node_inverse,
    node_basis,
    node_lift,
):
    row_count = lax.axis_size("row")
    col_count = lax.axis_size("col")
    devices = row_count * col_count
    col_levels = col_count.bit_length() - 1
    row_levels = row_count.bit_length() - 1
    levels = col_levels + row_levels
    leaf_rows = right_sides.shape[0]
    vector_width = right_sides.shape[1]
    rank_width = leaf_basis.shape[3]
    capacity = 2 * leaf_rows // min(devices, leaf_rows // 8)
    target = tree_order // leaf_rows
    position = tree_order % leaf_rows
    peer_index = lax.broadcasted_iota(jnp.int32, (leaf_rows, devices), 1)
    onehot = (target[:, None] == peer_index).astype(jnp.bfloat16)
    earlier = (
        lax.broadcasted_iota(jnp.int32, (leaf_rows, leaf_rows), 1)
        < lax.broadcasted_iota(jnp.int32, (leaf_rows, leaf_rows), 0)
    ).astype(jnp.bfloat16)
    before = jnp.dot(earlier, onehot, preferred_element_type=jnp.float32)
    slot_index = jnp.take_along_axis(before, target[:, None], axis=1)[:, 0].astype(jnp.int32)
    flat_slot = target * capacity + slot_index
    send_rows = (
        jnp.zeros((devices * capacity, vector_width), jnp.bfloat16).at[flat_slot].set(right_sides)
    )
    send_place = jnp.full((devices * capacity,), leaf_rows, jnp.int32).at[flat_slot].set(position)
    got_rows, got_place = (
        lax.all_to_all(
            send_rows.reshape(devices, capacity, vector_width),
            ("row", "col"),
            split_axis=0,
            concat_axis=0,
            tiled=True,
        ),
        lax.all_to_all(
            send_place.reshape(devices, capacity),
            ("row", "col"),
            split_axis=0,
            concat_axis=0,
            tiled=True,
        ),
    )
    got_rows = got_rows.reshape(devices * capacity, vector_width)
    got_place = got_place.reshape(devices * capacity)
    placed = (
        jnp.zeros((leaf_rows, vector_width), jnp.bfloat16).at[got_place].set(got_rows, mode="drop")
    )
    leaf_sol = apply_narrow(leaf_inverse[0], placed)
    leaf_coef = apply_transposed(leaf_basis[0], leaf_sol)
    solutions = []
    coefficients = []
    carried = leaf_coef
    for height in range(1, levels + 1):
        if height - 1 < col_levels:
            partner = from_partner(carried, "col", height - 1)
        else:
            partner = from_partner(carried, "row", height - 1 - col_levels)
        upper_half = device_bit(height - 1, col_levels) == 1
        node_rhs = jnp.where(
            upper_half,
            jnp.concatenate([partner, carried], axis=0),
            jnp.concatenate([carried, partner], axis=0),
        )
        node_sol = apply_complex(node_inverse[0, height - 1], node_rhs)
        solutions.append(node_sol)
        if height < levels:
            carried = apply_transposed(node_basis[0, height - 1], node_sol)
            coefficients.append(carried)
    top_down = solutions[levels - 1]
    for height in range(levels - 1, 0, -1):
        upper_half = device_bit(height, col_levels)
        own_half = lax.dynamic_slice_in_dim(top_down, upper_half * rank_width, rank_width, 0)
        top_down = solutions[height - 1] - apply_complex(
            node_lift[0, height - 1], coefficients[height - 1] - own_half
        )
    upper_half = device_bit(0, col_levels)
    own_half = lax.dynamic_slice_in_dim(top_down, upper_half * rank_width, rank_width, 0)
    tree_solution = leaf_sol - apply_complex(leaf_lift[0], leaf_coef - own_half)
    back_rows = jnp.take(tree_solution, got_place, axis=0, mode="fill", fill_value=0.0)
    returned = lax.all_to_all(
        back_rows.reshape(devices, capacity, vector_width),
        ("row", "col"),
        split_axis=0,
        concat_axis=0,
        tiled=True,
    )
    return returned.reshape(devices * capacity, vector_width)[flat_slot]


def solution(mesh):
    in_specs = (
        P(("row", "col"), None),
        P(("row", "col")),
        P(("row", "col"), None, None, None),
        P(("row", "col"), None, None, None),
        P(("row", "col"), None, None, None),
        P(("row", "col"), None, None, None, None),
        P(("row", "col"), None, None, None, None),
        P(("row", "col"), None, None, None, None),
    )
    out_specs = P(("row", "col"), None)
    return jax.shard_map(
        per_device, mesh=mesh, in_specs=in_specs, out_specs=out_specs, check_vma=False
    )
```

profile of v0, /device:TPU:0, one launch (start us, length us, event | category | flops | bytes accessed | tf_op | source)
XLA Modules:
  0.0 213.6 jit_solution(1609894498846892106)
XLA Ops:
  0.0 0.7 compare_select_fusion.3
  1.4 8.6 %gather_fusion.2 = f32[1024]{0:T(1024)S(1)} fusion(f32[1024,32]{0,1:T(8,128)S(1)} %fusion, s32[1024]{0:T(1024)S(1)} %bitcast.159), kind=kCustom, calls=%fused_computation.2 | custom fusion | bytes 16384 | tf_op jit(solution)/shard_map/jit(take_along_axis)/gather | solution.py:71
  10.1 4.3 %scatter_custom_fusion = s32[2048]{0:T(1024)S(1)} fusion(s32[1024]{0:T(1024)S(1)} %get-tuple-element.6, s32[1024]{0:T(1024)S(1)} %get-tuple-element.41, s32[]{:T(128)} %constant.42.clone.1), kind=kCustom, calls=%fused_computation.221 | custom fusion | bytes 8196 | tf_op jit(solution)/shard_map/scatter | solution.py:76
  14.4 0.7 all_to_all.12
  15.1 7.3 %all-to-all-start = ((s32[32,1,64]{2,1,0:T(1,128)}), s32[32,1,64]{2,1,0:T(1,128)S(1)}, u32[]{:S(2)}, u32[]{:S(2)}) async-start(s32[32,1,64]{2,1,0:T(1,128)} %all_to_all.12), calls=%async_computation | async-start | bytes 32768 | tf_op jit(solution)/shard_map/all_to_all | solution.py:85
  22.4 6.4 %scatter_custom_fusion.1 = bf16[2048,256]{1,0:T(8,128)(2,1)} fusion(s32[1024]{0:T(1024)S(1)} %get-tuple-element.6, bf16[1024,256]{1,0:T(8,128)(2,1)} %param.8, bf16[]{:T(256)} %constant.75.clone.1), kind=kCustom, calls=%fused_computation.116 | custom fusion | bytes 1049088 | tf_op jit(solution)/shard_map/scatter | solution.py:74
  28.8 0.7 all-to-all-done
  29.5 5.1 %all-to-all-start.1 = ((bf16[32,64,256]{2,1,0:T(8,128)(2,1)}), bf16[32,64,256]{2,1,0:T(8,128)(2,1)S(1)}, u32[]{:S(2)}, u32[]{:S(2)}) async-start(bf16[32,64,256]{2,1,0:T(8,128)(2,1)} %bitcast.5), calls=%async_computation.1 | async-start | bytes 2097152 | tf_op jit(solution)/shard_map/all_to_all | solution.py:78
  35.1 0.7 reduce.3
  35.9 24.9 %all-to-all-done.1 = bf16[32,64,256]{2,1,0:T(8,128)(2,1)S(1)} async-done(((bf16[32,64,256]{2,1,0:T(8,128)(2,1)}), bf16[32,64,256]{2,1,0:T(8,128)(2,1)S(1)}, u32[]{:S(2)}, u32[]{:S(2)}) %all-to-all-start.1) | async-done | bytes 1048608 | tf_op jit(solution)/shard_map/all_to_all | solution.py:78
  60.9 9.5 %scatter_custom_fusion.2 = bf16[1024,256]{1,0:T(8,128)(2,1)S(1)} fusion(s32[2048]{0:T(1024)S(1)} %bitcast.173, bf16[2048,256]{1,0:T(8,128)(2,1)S(1)} %bitcast.171, bf16[]{:T(256)} %constant.75.clone.1), kind=kCustom, calls=%fused_computation.195 | custom fusion | bytes 524290 | tf_op jit(solution)/shard_map/scatter | solution.py:96
  70.5 2.5 %fusion.1 = f32[256,1024]{1,0:T(8,128)S(1)} fusion(bf16[1,2,1024,1024]{3,2,1,0:T(8,128)(2,1)} %param.10, bf16[1024,128]{1,0:T(8,128)(2,1)S(1)} %get-tuple-element.30, bf16[1024,128]{1,0:T(8,128)(2,1)S(1)} %get-tuple-element.29), kind=kOutput, calls=%fused_computation.8 | convolution fusion | flops 537919488 | bytes 3670016 | tf_op jit(solution)/shard_map/dot_general | solution.py:25
  73.3 0.8 fusion.9
  74.5 0.8 fusion.74
  75.4 0.8 fusion.20
  76.3 1.5 collective-permute-done
  77.9 1.7 fusion.27
  79.6 1.7 convolution_add_fusion.4
  81.3 1.4 fusion.135
  82.8 1.4 fusion.19
  84.2 1.5 collective-permute-start.1
  85.7 6.9 %collective-permute-done.1 = f32[256,256]{1,0:T(8,128)S(1)} collective-permute-done((f32[256,256]{1,0:T(8,128)S(1)}, f32[256,256]{1,0:T(8,128)S(1)}, u32[]{:S(2)}, u32[]{:S(2)}) %collective-permute-start.1) | collective-permute-done | bytes 262176 | tf_op jit(solution)/shard_map/ppermute | solution.py:10
  92.7 1.7 fusion.34
  94.4 1.7 convolution_add_fusion.3
  96.1 1.4 fusion.132
  97.6 1.4 fusion.18
  99.0 1.5 collective-permute-start.2
  100.5 6.0 %collective-permute-done.2 = f32[256,256]{1,0:T(8,128)S(1)} collective-permute-done((f32[256,256]{1,0:T(8,128)S(1)}, f32[256,256]{1,0:T(8,128)S(1)}, u32[]{:S(2)}, u32[]{:S(2)}) %collective-permute-start.2) | collective-permute-done | bytes 262176 | tf_op jit(solution)/shard_map/ppermute | solution.py:10
  106.7 1.7 fusion.41
  108.4 1.7 convolution_add_fusion.2
  110.1 1.4 fusion.129
  111.5 1.4 fusion.17
  113.0 0.9 collective-permute-start.3
  113.9 5.8 %collective-permute-done.3 = f32[256,256]{1,0:T(8,128)} collective-permute-done((f32[256,256]{1,0:T(8,128)S(1)}, f32[256,256]{1,0:T(8,128)}, u32[]{:S(2)}, u32[]{:S(2)}) %collective-permute-start.3) | collective-permute-done | bytes 262176 | tf_op jit(solution)/shard_map/ppermute | solution.py:10
  119.7 1.1 maximum_select_fusion.3
  120.9 1.7 fusion.48
  122.6 1.7 convolution_add_fusion.1
  124.3 1.4 fusion.126
  125.7 1.6 fusion.16
  127.4 2.0 collective-permute-start.4
  129.4 10.3 %collective-permute-done.4 = f32[256,256]{1,0:T(8,128)S(1)} collective-permute-done((f32[256,256]{1,0:T(8,128)S(1)}, f32[256,256]{1,0:T(8,128)S(1)}, u32[]{:S(2)}, u32[]{:S(2)}) %collective-permute-start.4) | collective-permute-done | bytes 262176 | tf_op jit(solution)/shard_map/ppermute | solution.py:10
  139.7 1.7 fusion.63
  141.5 1.8 fusion.55
  147.3 1.1 fusion.60
  148.4 1.0 fusion.8
  149.8 6.6 %gather_fusion = f32[2048,256]{1,0:T(8,128)S(1)} fusion(f32[1024,256]{1,0:T(8,128)S(1)} %copy.65, s32[2048]{0:T(1024)S(1)} %broadcast_clamp_fusion), kind=kCustom, calls=%fused_computation | custom fusion | bytes 4202496 | tf_op jit(solution)/shard_map/jit(_take)/gather | solution.py:129
  156.8 52.1 %all_to_all.19 = f32[32,64,256]{2,1,0:T(8,128)S(1)} all-to-all(f32[32,64,256]{2,1,0:T(8,128)S(1)} %broadcast_select_fusion), channel_id=1, replica_groups=mesh['row'=8,'col'=4] {'row','col'}, dimensions={0} | all-to-all | bytes 4194304 | tf_op jit(solution)/shard_map/all_to_all | solution.py:130
  208.9 4.7 %gather_fusion.1 = f32[1024,256]{1,0:T(8,128)} fusion(f32[2048,256]{1,0:T(8,128)S(1)} %bitcast.160, s32[1024]{0:T(1024)S(1)} %get-tuple-element.5), kind=kCustom, calls=%fused_computation.1 | custom fusion | bytes 2101248 | tf_op jit(solution)/shard_map/gather | solution.py:137
  (58 shorter events, 7.3 us)
Async XLA Ops:
  15.1 14.4 %all-to-all-start = ((s32[32,1,64]{2,1,0:T(1,128)}), s32[32,1,64]{2,1,0:T(1,128)S(1)}, u32[]{:S(2)}, u32[]{:S(2)}) async-start(s32[32,1,64]{2,1,0:T(1,128)} %all_to_all.12), calls=%async_computation | async-start | bytes 32768 | tf_op jit(solution)/shard_map/all_to_all | solution.py:85
  29.5 31.4 %all-to-all-start.1 = ((bf16[32,64,256]{2,1,0:T(8,128)(2,1)}), bf16[32,64,256]{2,1,0:T(8,128)(2,1)S(1)}, u32[]{:S(2)}, u32[]{:S(2)}) async-start(bf16[32,64,256]{2,1,0:T(8,128)(2,1)} %bitcast.5), calls=%async_computation.1 | async-start | bytes 2097152 | tf_op jit(solution)/shard_map/all_to_all | solution.py:78
  70.5 2.8 %copy-start.4 = (bf16[1,2,1024,1024]{3,2,1,0:T(8,128)(2,1)S(1)}, bf16[1,2,1024,1024]{3,2,1,0:T(8,128)(2,1)}, u32[]{:S(2)}) copy-start(bf16[1,2,1024,1024]{3,2,1,0:T(8,128)(2,1)} %param.10) | copy-start | bytes 12582916
  73.3 1.2 copy-start.5
  76.2 1.7 copy-start
  76.2 1.6 collective-permute-start
  84.2 8.4 %collective-permute-start.1 = (f32[256,256]{1,0:T(8,128)S(1)}, f32[256,256]{1,0:T(8,128)S(1)}, u32[]{:S(2)}, u32[]{:S(2)}) collective-permute-start(f32[256,256]{1,0:T(8,128)S(1)} %fusion.19), channel_id=1, source_target_pairs={{0,2},{1,3},{2,0},{3,1},{4,6},{5,7},{6,4},{7,5},{8,10},{9,11},{10,... | collective-permute-start | bytes 786440 | tf_op jit(solution)/shard_map/ppermute | solution.py:10
  99.0 7.6 %collective-permute-start.2 = (f32[256,256]{1,0:T(8,128)S(1)}, f32[256,256]{1,0:T(8,128)S(1)}, u32[]{:S(2)}, u32[]{:S(2)}) collective-permute-start(f32[256,256]{1,0:T(8,128)S(1)} %fusion.18), channel_id=1, source_target_pairs={{0,4},{4,0},{8,12},{12,8},{16,20},{20,16},{24,28},{28,24},{1,5},{5... | collective-permute-start | bytes 786440 | tf_op jit(solution)/shard_map/ppermute | solution.py:10
  113.0 6.8 %collective-permute-start.3 = (f32[256,256]{1,0:T(8,128)S(1)}, f32[256,256]{1,0:T(8,128)}, u32[]{:S(2)}, u32[]{:S(2)}) collective-permute-start(f32[256,256]{1,0:T(8,128)S(1)} %fusion.17), channel_id=1, source_target_pairs={{0,8},{4,12},{8,0},{12,4},{16,24},{20,28},{24,16},{28,20},{1,9},{5... | collective-permute-start | bytes 786440 | tf_op jit(solution)/shard_map/ppermute | solution.py:10
  127.4 12.3 %collective-permute-start.4 = (f32[256,256]{1,0:T(8,128)S(1)}, f32[256,256]{1,0:T(8,128)S(1)}, u32[]{:S(2)}, u32[]{:S(2)}) collective-permute-start(f32[256,256]{1,0:T(8,128)S(1)} %fusion.16), channel_id=1, source_target_pairs={{0,16},{4,20},{8,24},{12,28},{16,0},{20,4},{24,8},{28,12},{1,17},{... | collective-permute-start | bytes 786440 | tf_op jit(solution)/shard_map/ppermute | solution.py:10
  141.4 2.0 copy-start.2
  146.0 1.0 copy-start.1
  146.1 1.2 copy-start.3
where the time goes:
time: 215 us; the launch traced here: 214 us
  waiting for transfers between devices  56.2 us (26%)
  blocking collectives  52.1 us (24%)
  local copies, waits for them, and re-layouts  42.9 us (20%)
  matrix products  39.4 us (18%)
  starting transfers between devices  18.4 us (9%)
  other arithmetic  3.85 us (2%)
    all_to_all x1, blocking collectives, per_device(): lax.all_to_all(back_rows.reshape(devices, capacity, vector_width), ('row'...  52.1 us
    ppermute x5, waiting for transfers between devices, from_partner(): lax.ppermute(shard, axis, [(i, i ^ 1 << apart) for i in range(lax.axis_si...  30.6 us
    all_to_all x1, waiting for transfers between devices, per_device(): lax.all_to_all(send_rows.reshape(devices, capacity, vector_width), ('row'...  24.9 us
    dot_general x10, matrix products, apply_complex(): jnp.dot(matrix[1].astype(jnp.float32), rotated(vectors), precision=exactn...  11.2 us
    dot_general x10, matrix products, apply_complex(): plain = jnp.dot(matrix[0].astype(jnp.float32), vectors, precision=exactness)  11.1 us
    scatter x1, local copies, waits for them, and re-layouts, per_device(): jnp.zeros((leaf_rows, vector_width), jnp.bfloat16).at[got_place]  9.53 us
    gather x1, local copies, waits for them, and re-layouts, per_device(): jnp.take_along_axis(before, target[:, None], axis=1)[:, 0].astype(jnp.int32)  8.65 us
    all_to_all x1, starting transfers between devices, per_device(): lax.all_to_all(send_place.reshape(devices, capacity), ('row', 'col'), spl...  7.3 us
  transfers between devices with their start and end apart: 7, of which 7 were waited for; matrix products, arithmetic and copies ran while one was open for 4% of the time, Pallas kernels for 0%

commit v1 on v0

v1 whole, which is shorter than its diff:
```python
import functools

import jax
import jax.numpy as jnp
from jax import lax
from jax.experimental import pallas as pl
from jax.experimental.pallas import tpu as pltpu
from jax.sharding import PartitionSpec as P

LANES = 128
EXTRA = 16
CODE_BASE = 32
SCALE_STEPS = 64
BF16 = jnp.bfloat16
F32 = jnp.float32


def matmul(a, b):
    return lax.dot_general(a, b, (((1,), (0,)), ((), ())), preferred_element_type=F32)


def matmul_t(a, b):
    return lax.dot_general(a, b, (((0,), (0,)), ((), ())), preferred_element_type=F32)


def matmul_nt(a, b):
    return lax.dot_general(a, b, (((1,), (1,)), ((), ())), preferred_element_type=F32)


def iota(shape, dim):
    return lax.broadcasted_iota(jnp.int32, shape, dim)


def rotated(half):
    low = iota(half.shape, 1) < LANES // 2
    turned = pltpu.roll(half, LANES // 2, 1)
    return jnp.where(low, -turned, turned)


def rotated_all(x):
    return jnp.concatenate(
        [rotated(x[:, at : at + LANES]) for at in range(0, x.shape[1], LANES)], axis=1
    )


def swapped(first, second):
    low = iota(first.shape, 1) < LANES // 2
    return (
        jnp.where(low, first, pltpu.roll(second, LANES // 2, 1)),
        jnp.where(low, pltpu.roll(first, LANES // 2, 1), second),
    )


def two_parts(x):
    high = x.astype(BF16)
    low = (x - high.astype(F32)).astype(BF16)
    return jnp.concatenate([high, low], axis=1)


def folded(both):
    width = both.shape[1] // 2
    return both[:, :width] + both[:, width:]


def apply_complex(real, imag, x):
    turned = rotated_all(x)
    return folded(matmul(real, two_parts(x)) + matmul(imag, two_parts(turned)))


def apply_transposed(real, imag, x):
    turned = rotated_all(x)
    return folded(matmul_t(real, two_parts(x)) + matmul_t(imag, two_parts(turned)))


def unit_of(code):
    return jnp.exp2(code * (1.0 / SCALE_STEPS) - 15.0)


def inverse_unit_of(code):
    return jnp.exp2(15.0 - code * (1.0 / SCALE_STEPS))


def scale_code(x):
    largest = jnp.max(jnp.abs(x), axis=0, keepdims=True)
    return jnp.ceil(jnp.log2(jnp.maximum(largest, 2.0**-110)) * SCALE_STEPS)


def pack_kernel(me_ref, order_ref, rows_ref, send_ref, slot_ref, *, devices, capacity):
    leaf_rows = rows_ref.shape[0]
    order = order_ref[...]
    target = order // leaf_rows
    position = order - target * leaf_rows
    hits = (iota((devices, leaf_rows), 0) == target).astype(F32)
    upper = (iota((leaf_rows, leaf_rows), 0) < iota((leaf_rows, leaf_rows), 1)).astype(F32)
    before = matmul(hits.astype(BF16), upper.astype(BF16))
    rank = jnp.sum(hits * before, axis=0, keepdims=True).astype(jnp.int32)
    slot = target * capacity + rank
    slot_ref[...] = slot
    rows = rows_ref[...].astype(F32)
    first, second = swapped(rows[:, :LANES], rows[:, LANES:])
    rows = jnp.concatenate([first, second], axis=1).astype(BF16)
    chosen = (iota((devices * capacity, leaf_rows), 0) == slot).astype(F32).astype(BF16)
    sent = matmul(chosen, rows).astype(BF16)
    send_ref[:, :capacity, :] = sent[:, :LANES].reshape(devices, capacity, LANES)
    send_ref[:, capacity : 2 * capacity, :] = sent[:, LANES:].reshape(devices, capacity, LANES)
    group = LANES // capacity
    lane = rank + lax.rem(me_ref[0], group) * capacity
    code = position + 1
    high = code // CODE_BASE
    low = code - high * CODE_BASE
    codes = jnp.concatenate([hits * high.astype(F32), hits * low.astype(F32)], axis=0)
    places = (iota((LANES, leaf_rows), 0) == lane).astype(F32).astype(BF16)
    spread = matmul_nt(codes.astype(BF16), places)
    eight = (devices, EXTRA // 2, LANES)
    send_ref[:, 2 * capacity :, :] = jnp.concatenate(
        [
            jnp.broadcast_to(spread[:devices].reshape(devices, 1, LANES), eight),
            jnp.broadcast_to(spread[devices:].reshape(devices, 1, LANES), eight),
        ],
        axis=1,
    ).astype(BF16)


def positions(got_ref, devices, capacity):
    group = LANES // capacity
    extra = got_ref[:, 2 * capacity :, :].astype(F32)
    code = extra[:, 0, :] * CODE_BASE + extra[:, EXTRA // 2, :]
    return jnp.sum(code.reshape(devices // group, group, LANES), axis=1) - 1.0


def leaf_kernel(got_ref, inverse_ref, basis_ref, sol_ref, coef_ref, place_ref, *, devices, capacity):
    leaf_rows = sol_ref.shape[0]
    place = positions(got_ref, devices, capacity)
    place_ref[...] = place
    where_to = iota((leaf_rows, LANES), 0).astype(F32)
    chosen = jnp.concatenate(
        [
            (where_to == place[k : k + 1, :]).astype(F32).astype(BF16)
            for k in range(place.shape[0])
        ],
        axis=1,
    )
    slots = devices * capacity
    got = jnp.concatenate(
        [
            got_ref[:, :capacity, :].reshape(slots, LANES),
            got_ref[:, capacity : 2 * capacity, :].reshape(slots, LANES),
        ],
        axis=1,
    )
    placed = matmul(chosen, got)
    turned = rotated_all(placed)
    sol = matmul(inverse_ref[0], placed.astype(BF16)) + matmul(inverse_ref[1], turned.astype(BF16))
    sol_ref[...] = sol
    coef_ref[...] = apply_transposed(basis_ref[0], basis_ref[1], sol)


def node_rhs(upper, own, partner):
    is_upper = upper == 1
    return jnp.concatenate(
        [jnp.where(is_upper, partner, own), jnp.where(is_upper, own, partner)], axis=0
    )


def node_kernel(bit_ref, own_ref, partner_ref, inverse_ref, basis_ref, sol_ref, coef_ref):
    rhs = node_rhs(bit_ref[0], own_ref[...], partner_ref[...])
    sol = apply_complex(inverse_ref[0], inverse_ref[1], rhs)
    sol_ref[...] = sol
    coef_ref[...] = apply_transposed(basis_ref[0], basis_ref[1], sol)


def half_of(bit, x):
    rank = x.shape[0] // 2
    return jnp.where(bit == 1, x[rank:], x[:rank])


def descent_kernel(bits_ref, own_ref, partner_ref, inverse_ref, lift_ref, *refs):
    levels = bits_ref.shape[0]
    sols = refs[: levels - 1]
    coefs = refs[levels - 1 : 2 * levels - 2]
    mine_ref, other_ref = refs[2 * levels - 2 :]
    rhs = node_rhs(bits_ref[levels - 1], own_ref[...], partner_ref[...])
    down = apply_complex(inverse_ref[0], inverse_ref[1], rhs)
    for height in range(levels - 1, 0, -1):
        gap = coefs[height - 1][...] - half_of(bits_ref[height], down)
        down = sols[height - 1][...] - apply_complex(
            lift_ref[height - 1, 0], lift_ref[height - 1, 1], gap
        )
    mine_ref[...] = half_of(bits_ref[0], down)
    other_ref[...] = half_of(1 - bits_ref[0], down)


def finish_kernel(
    bit_ref, mine_ref, other_ref, coef_ref, sol_ref, lift_ref, place_ref, send_ref, *, devices, capacity
):
    leaf_rows = sol_ref.shape[0]
    swap = bit_ref[0] == 1
    mine, other = mine_ref[...], other_ref[...]
    h = jnp.concatenate([jnp.where(swap, other, mine), jnp.where(swap, mine, other)], axis=1)
    sol = sol_ref[...] - apply_complex(lift_ref[0], lift_ref[1], coef_ref[...] - h)
    code = scale_code(sol)
    level = jnp.clip(jnp.round(sol * inverse_unit_of(code)), -32767.0, 32767.0)
    high = jnp.round(level * (1.0 / 256.0))
    low = level - high * 256.0
    parts = jnp.concatenate([high.astype(BF16), low.astype(BF16)], axis=1)
    place = place_ref[...]
    place = jnp.transpose(place)
    where_from = iota((LANES, leaf_rows), 1).astype(F32)
    chosen = jnp.concatenate(
        [
            (where_from == place[:, k : k + 1]).astype(F32).astype(BF16)
            for k in range(place.shape[1])
        ],
        axis=0,
    )
    both = matmul(chosen, parts)
    width = sol.shape[1]
    level = (both[:, :width] * 256.0 + both[:, width:]).astype(jnp.int32).astype(jnp.int16)
    send_ref[:, :capacity, :] = level[:, :LANES].reshape(devices, capacity, LANES)
    send_ref[:, capacity : 2 * capacity, :] = level[:, LANES:].reshape(devices, capacity, LANES)
    eight = (EXTRA // 2, LANES)
    extra = jnp.concatenate(
        [jnp.broadcast_to(code[:, :LANES], eight), jnp.broadcast_to(code[:, LANES:], eight)], axis=0
    )
    extra = extra.astype(jnp.int32).astype(jnp.int16)
    send_ref[:, 2 * capacity :, :] = jnp.broadcast_to(
        extra.reshape(1, EXTRA, LANES), (devices, EXTRA, LANES)
    )


def unpack_kernel(got_ref, slot_ref, out_ref, *, devices, capacity):
    leaf_rows = out_ref.shape[0]
    slots = devices * capacity
    extra = got_ref[:, 2 * capacity :, :].astype(jnp.int32).astype(F32)
    halves = []
    for half in range(2):
        level = got_ref[:, half * capacity : (half + 1) * capacity, :]
        level = level.astype(jnp.int32).astype(F32)
        unit = unit_of(extra[:, half * (EXTRA // 2) : half * (EXTRA // 2) + 1, :])
        halves.append((level * unit).reshape(slots, LANES))
    both = two_parts(jnp.concatenate(halves, axis=1))
    slot = jnp.transpose(jnp.broadcast_to(slot_ref[...].astype(F32), (LANES, leaf_rows)))[:, :1]
    chosen = (iota((leaf_rows, slots), 1).astype(F32) == slot).astype(F32).astype(BF16)
    result = folded(matmul(chosen, both))
    first, second = swapped(result[:, :LANES], result[:, LANES:])
    out_ref[:, :LANES] = first
    out_ref[:, LANES:] = second


def call(kernel, out_shapes, operands, smem=0, flops=0, moved=0):
    vmem = pl.BlockSpec(memory_space=pltpu.VMEM)
    scalar = pl.BlockSpec(memory_space=pltpu.SMEM)
    return pl.pallas_call(
        kernel,
        out_shape=out_shapes,
        in_specs=[scalar] * smem + [vmem] * (len(operands) - smem),
        out_specs=jax.tree.map(lambda _: vmem, out_shapes),
        compiler_params=pltpu.CompilerParams(vmem_limit_bytes=48 * 2**20),
        cost_estimate=pl.CostEstimate(flops=flops, bytes_accessed=moved, transcendentals=0),
    )(*operands)


def shape(dims, dtype=F32):
    return jax.ShapeDtypeStruct(dims, dtype)


def from_partner(shard, axis, apart):
    return lax.ppermute(shard, axis, [(i, i ^ 1 << apart) for i in range(lax.axis_size(axis))])


def tree_bit(height, col_levels):
    if height < col_levels:
        return lax.axis_index("col") >> height & 1
    return lax.axis_index("row") >> height - col_levels & 1


def per_device(
    right_sides, tree_order, leaf_inverse, leaf_basis, leaf_lift, node_inverse, node_basis, node_lift
):
    row_count = lax.axis_size("row")
    col_count = lax.axis_size("col")
    devices = row_count * col_count
    col_levels = col_count.bit_length() - 1
    levels = col_levels + row_count.bit_length() - 1
    leaf_rows, width = right_sides.shape
    rank = leaf_basis.shape[3]
    capacity = 2 * leaf_rows // min(devices, leaf_rows // 8)
    block = (devices, 2 * capacity + EXTRA, LANES)
    sizes = dict(devices=devices, capacity=capacity)
    me = (lax.axis_index("row") * col_count + lax.axis_index("col")).astype(jnp.int32)
    bits = [tree_bit(height, col_levels).astype(jnp.int32) for height in range(levels)]

    def exchange(blocks):
        return lax.all_to_all(blocks, ("row", "col"), split_axis=0, concat_axis=0, tiled=True)

    def partner_of(shard, height):
        if height < col_levels:
            return from_partner(shard, "col", height)
        return from_partner(shard, "row", height - col_levels)

    send, slot = call(
        functools.partial(pack_kernel, **sizes),
        (shape(block, BF16), shape((1, leaf_rows), jnp.int32)),
        (me.reshape(1), tree_order.reshape(1, leaf_rows), right_sides),
        smem=1,
    )
    got = exchange(send)
    leaf_sol, leaf_coef, place = call(
        functools.partial(leaf_kernel, **sizes),
        (
            shape((leaf_rows, width)),
            shape((rank, width)),
            shape((devices * capacity // LANES, LANES)),
        ),
        (got, leaf_inverse[0], leaf_basis[0]),
    )
    odd = bits[0] == 1
    own = jnp.where(odd, leaf_coef[:, LANES:], leaf_coef[:, :LANES])
    other = jnp.where(odd, leaf_coef[:, :LANES], leaf_coef[:, LANES:])
    sols, coefs = [], []
    for height in range(1, levels):
        partner = partner_of(other if height == 1 else own, height - 1)
        sol, own = call(
            node_kernel,
            (shape((2 * rank, LANES)), shape((rank, LANES))),
            (
                bits[height - 1].reshape(1),
                own,
                partner,
                node_inverse[0, height - 1],
                node_basis[0, height - 1],
            ),
            smem=1,
        )
        sols.append(sol)
        coefs.append(own)
    partner = partner_of(own, levels - 1)
    mine, other = call(
        descent_kernel,
        (shape((rank, LANES)), shape((rank, LANES))),
        (jnp.stack(bits), own, partner, node_inverse[0, levels - 1], node_lift[0], *sols, *coefs),
        smem=1,
    )
    other = partner_of(other, 0)
    back = call(
        functools.partial(finish_kernel, **sizes),
        shape(block, jnp.int16),
        (bits[0].reshape(1), mine, other, leaf_coef, leaf_sol, leaf_lift[0], place),
        smem=1,
    )
    returned = exchange(back)
    return call(
        functools.partial(unpack_kernel, **sizes),
        shape((leaf_rows, width)),
        (returned, slot),
    )


def solution(mesh):
    in_specs = (
        P(("row", "col"), None),
        P(("row", "col")),
        P(("row", "col"), None, None, None),
        P(("row", "col"), None, None, None),
        P(("row", "col"), None, None, None),
        P(("row", "col"), None, None, None, None),
        P(("row", "col"), None, None, None, None),
        P(("row", "col"), None, None, None, None),
    )
    out_specs = P(("row", "col"), None)
    return jax.shard_map(
        per_device, mesh=mesh, in_specs=in_specs, out_specs=out_specs, check_vma=False
    )
```

time: 215 us -> 143 us (0.67)
  matrix products: 39.4 us -> 0 us
  Pallas kernels: 0 us -> 30.6 us
  local copies, waits for them, and re-layouts: 42.9 us -> 20.6 us
  blocking collectives: 52.1 us -> 33.6 us
  waiting for transfers between devices: 56.2 us -> 44.9 us
  starting transfers between devices: 18.4 us -> 12.2 us
  other arithmetic: 3.85 us -> 0.02 us
    dot_general x33 -> x0, matrix products: 39.4 us -> none  [the longest x10 11.2 us: apply_complex(): jnp.dot(matrix[1].astype(jnp.float32), rotated(vectors), precision=exactn...]
    pallas_call x0 -> x9, Pallas kernels: none -> 30.6 us  [call(): pl.pallas_call(kernel, out_shape=out_shapes, in_specs=[scalar] * smem + [...]
    scatter x3 -> x0, local copies, waits for them, and re-layouts: 20.3 us -> none  [the longest x1 9.53 us: per_device(): jnp.zeros((leaf_rows, vector_width), jnp.bfloat16).at[got_place]]
    gather x3 -> x0, local copies, waits for them, and re-layouts: 20 us -> none  [the longest x1 8.65 us: per_device(): jnp.take_along_axis(before, target[:, None], axis=1)[:, 0].astype(jnp.int32)]
    all_to_all x1, blocking collectives: 52.1 us -> 33.6 us  [exchange(): lax.all_to_all(blocks, ('row', 'col'), split_axis=0, concat_axis=0, tiled...]
    unnamed x13 -> x40, local copies, waits for them, and re-layouts: 1.11 us -> 15.1 us
    ppermute x5 -> x6, waiting for transfers between devices: 30.6 us -> 20.1 us  [from_partner(): lax.ppermute(shard, axis, [(i, i ^ 1 << apart) for i in range(lax.axis_si...]
    squeeze x0 -> x2, local copies, waits for them, and re-layouts: none -> 5.49 us  [the longest x1 4.29 us: per_device(): node_inverse[0, levels - 1]]
where the time goes in v1:
time: 143 us; the launch traced here: 142 us
  waiting for transfers between devices  44.9 us (31%)
  blocking collectives  33.6 us (23%)
  Pallas kernels  30.6 us (21%)
  local copies, waits for them, and re-layouts  20.6 us (14%)
  starting transfers between devices  12.2 us (9%)
    all_to_all x1, blocking collectives, exchange(): lax.all_to_all(blocks, ('row', 'col'), split_axis=0, concat_axis=0, tiled...  33.6 us
    pallas_call x9, Pallas kernels, call(): pl.pallas_call(kernel, out_shape=out_shapes, in_specs=[scalar] * smem + [...  30.6 us
    all_to_all x1, waiting for transfers between devices, exchange(): lax.all_to_all(blocks, ('row', 'col'), split_axis=0, concat_axis=0, tiled...  24.8 us
    ppermute x6, waiting for transfers between devices, from_partner(): lax.ppermute(shard, axis, [(i, i ^ 1 << apart) for i in range(lax.axis_si...  20.1 us
    unnamed x40, local copies, waits for them, and re-layouts  15.1 us
    all_to_all x1, starting transfers between devices, exchange(): lax.all_to_all(blocks, ('row', 'col'), split_axis=0, concat_axis=0, tiled...  7.3 us
    ppermute x6, starting transfers between devices, from_partner(): lax.ppermute(shard, axis, [(i, i ^ 1 << apart) for i in range(lax.axis_si...  4.86 us
    squeeze x1, local copies, waits for them, and re-layouts, per_device(): node_inverse[0, levels - 1]  4.29 us
  transfers between devices with their start and end apart: 7, of which 7 were waited for; matrix products, arithmetic and copies ran while one was open for 4% of the time, Pallas kernels for 0%

profile of v1, /device:TPU:0, one launch (start us, length us, event | category | flops | bytes accessed | tf_op | source)
XLA Modules:
  0.0 142.0 jit_solution(11191370599321778739)
XLA Ops:
  0.0 1.0 copy-done.11
  1.0 0.7 copy-done.18
  1.7 2.8 %shard_map.82 = (bf16[32,144,128]{2,1,0:T(8,128)(2,1)}, s32[1,1024]{1,0:T(1,128)S(1)}) custom-call(s32[1]{0:T(128)} %bitcast.5.me_ref, s32[1,1024]{1,0:T(1,128)S(1)} %bitcast.32, bf16[1024,256]{1,0:T(8,128)(2,1)S(1)} %copy-done.11), custom_call_target="tpu_custom_call" | custom-call | tf_op jit(solution)/shard_map/pallas_call | solution.py:253
  4.5 7.3 %all-to-all-start = ((bf16[32,144,128]{2,1,0:T(8,128)(2,1)}), bf16[32,144,128]{2,1,0:T(8,128)(2,1)S(1)}, u32[]{:S(2)}, u32[]{:S(2)}) async-start(bf16[32,144,128]{2,1,0:T(8,128)(2,1)} %get-tuple-element.20), calls=%async_computation | async-start | bytes 2359296 | tf_op jit(solution)/shard_map/all_to_all | solution.py:294
  11.8 4.3 %slice_bitcast_fusion = (bf16[2,512,512]{2,1,0:T(8,128)(2,1)S(1)}, bf16[2,512,512]{2,1,0:T(8,128)(2,1)}, bf16[2,512,512]{2,1,0:T(8,128)(2,1)}, bf16[2,512,512]{2,1,0:T(8,128)(2,1)}, bf16[2,512,512]{2,1,0:T(8,128)(2,1)S(1)}) fusion(bf16[1,5,2,512,512]{4,3,2,1,0:T(8,128)(2,1)} %param.13), kind=kLoop, calls=%fused_computation | loop fusion | bytes 10485760 | tf_op jit(solution)/shard_map/squeeze | solution.py:341
  16.1 24.8 %all-to-all-done.got_ref = bf16[32,144,128]{2,1,0:T(8,128)(2,1)S(1)} async-done(((bf16[32,144,128]{2,1,0:T(8,128)(2,1)}), bf16[32,144,128]{2,1,0:T(8,128)(2,1)S(1)}, u32[]{:S(2)}, u32[]{:S(2)}) %all-to-all-start) | async-done | bytes 1179680 | tf_op jit(solution)/shard_map/all_to_all | solution.py:294
  40.9 1.2 copy-done.7
  42.1 7.3 %shard_map.83 = (f32[1024,256]{1,0:T(8,128)S(1)}, f32[256,256]{1,0:T(8,128)S(1)}, f32[16,128]{1,0:T(8,128)S(1)}) custom-call(bf16[32,144,128]{2,1,0:T(8,128)(2,1)S(1)} %all-to-all-done.got_ref, bf16[2,1024,1024]{2,1,0:T(8,128)(2,1)} %bitcast.33, bf16[2,1024,256]{2,1,0:T(8,128)(2,1)S(1)} %bitcast.30), custom_call_target="tpu_custom_call" | custom-call | tf_op jit(solution)/shard_map/pallas_call | solution.py:253
  49.5 0.0 copy-start.9
  49.5 1.0 copy-done.9
  50.5 0.0 copy-start.2
  50.5 0.1 collective-permute-start
  50.6 0.0 copy-done.19
  50.6 1.2 slice_bitcast_fusion.5
  51.8 0.1 collective-permute-done.partner_ref
  51.9 0.2 copy-done.2
  52.1 1.0 shard_map.84
  53.1 0.0 copy-start.12
  53.1 0.7 copy-done.12
  53.8 1.4 %collective-permute-start.1 = (f32[256,128]{1,0:T(8,128)S(1)}, f32[256,128]{1,0:T(8,128)}, u32[]{:S(2)}, u32[]{:S(2)}) collective-permute-start(f32[256,128]{1,0:T(8,128)S(1)} %get-tuple-element.22.own_ref.refs_4_), channel_id=1, source_target_pairs={{0,2},{1,3},{2,0},{3,1},{4,6},{5,7},{6,4},{7,5},{8,10},{9,11},{10,... | collective-permute-start | bytes 393224 | tf_op jit(solution)/shard_map/ppermute | solution.py:268
  55.3 4.3 %collective-permute-done.1.partner_ref = f32[256,128]{1,0:T(8,128)} collective-permute-done((f32[256,128]{1,0:T(8,128)S(1)}, f32[256,128]{1,0:T(8,128)}, u32[]{:S(2)}, u32[]{:S(2)}) %collective-permute-start.1) | collective-permute-done | bytes 131104 | tf_op jit(solution)/shard_map/ppermute | solution.py:268
  59.5 1.2 copy-done.1
  60.8 1.0 copy-done.6
  61.8 2.6 %shard_map.85 = (f32[512,128]{1,0:T(8,128)S(1)}, f32[256,128]{1,0:T(8,128)}) custom-call(s32[1]{0:T(128)} %bitcast.1.bit_ref, f32[256,128]{1,0:T(8,128)S(1)} %get-tuple-element.22.own_ref.refs_4_, f32[256,128]{1,0:T(8,128)} %collective-permute-done.1.partner_ref, bf16[2,512,512]{2,1,0:T(8,128)(2,1)S(1)} %copy-done.1, bf16[2,512,256]{2,1,0:T(8,128)(2,1)S(1)} %copy-done.6), custom_call_target="tpu_custom_call" | custom-call | tf_op jit(solution)/shard_map/pallas_call | solution.py:253
  64.4 0.7 copy-done.14
  65.1 1.4 %collective-permute-start.2 = (f32[256,128]{1,0:T(8,128)}, f32[256,128]{1,0:T(8,128)}, u32[]{:S(2)}, u32[]{:S(2)}) collective-permute-start(f32[256,128]{1,0:T(8,128)} %get-tuple-element.23.own_ref.refs_5_), channel_id=1, source_target_pairs={{0,4},{4,0},{8,12},{12,8},{16,20},{20,16},{24,28},{28,24},{1,5},{5... | collective-permute-start | bytes 393224 | tf_op jit(solution)/shard_map/ppermute | solution.py:268
  66.6 3.8 %collective-permute-done.2.partner_ref = f32[256,128]{1,0:T(8,128)} collective-permute-done((f32[256,128]{1,0:T(8,128)}, f32[256,128]{1,0:T(8,128)}, u32[]{:S(2)}, u32[]{:S(2)}) %collective-permute-start.2) | collective-permute-done | bytes 131104 | tf_op jit(solution)/shard_map/ppermute | solution.py:268
  70.4 0.0 copy-done
  70.4 1.0 copy-done.5
  71.5 2.6 %shard_map.86 = (f32[512,128]{1,0:T(8,128)S(1)}, f32[256,128]{1,0:T(8,128)}) custom-call(s32[1]{0:T(128)} %bitcast.2.bit_ref, f32[256,128]{1,0:T(8,128)} %get-tuple-element.23.own_ref.refs_5_, f32[256,128]{1,0:T(8,128)} %collective-permute-done.2.partner_ref, bf16[2,512,512]{2,1,0:T(8,128)(2,1)S(1)} %copy-done, bf16[2,512,256]{2,1,0:T(8,128)(2,1)S(1)} %copy-done.5), custom_call_target="tpu_custom_call" | custom-call | tf_op jit(solution)/shard_map/pallas_call | solution.py:253
  74.1 0.7 copy-done.16
  74.8 0.5 collective-permute-start.3
  75.3 4.7 %collective-permute-done.3.partner_ref = f32[256,128]{1,0:T(8,128)S(1)} collective-permute-done((f32[256,128]{1,0:T(8,128)}, f32[256,128]{1,0:T(8,128)S(1)}, u32[]{:S(2)}, u32[]{:S(2)}) %collective-permute-start.3) | collective-permute-done | bytes 131104 | tf_op jit(solution)/shard_map/ppermute | solution.py:268
  80.0 1.0 copy-done.4
  81.0 1.9 %shard_map.87 = (f32[512,128]{1,0:T(8,128)S(1)}, f32[256,128]{1,0:T(8,128)S(1)}) custom-call(s32[1]{0:T(128)} %bitcast.3.bit_ref, f32[256,128]{1,0:T(8,128)} %get-tuple-element.24.own_ref.refs_6_, f32[256,128]{1,0:T(8,128)S(1)} %collective-permute-done.3.partner_ref, bf16[2,512,512]{2,1,0:T(8,128)(2,1)S(1)} %get-tuple-element.39.inverse_ref, ...), custom_call_target="tpu_custom_call" | custom-call | tf_op jit(solution)/shard_map/pallas_call | solution.py:253
  83.0 1.3 collective-permute-start.4
  84.3 0.1 stack.20.bits_ref
  84.4 5.8 %collective-permute-done.4.partner_ref = f32[256,128]{1,0:T(8,128)S(1)} collective-permute-done((f32[256,128]{1,0:T(8,128)S(1)}, f32[256,128]{1,0:T(8,128)S(1)}, u32[]{:S(2)}, u32[]{:S(2)}) %collective-permute-start.4) | collective-permute-done | bytes 131104 | tf_op jit(solution)/shard_map/ppermute | solution.py:268
  90.2 1.6 %copy-done.3 = bf16[1,4,2,512,256]{4,3,2,1,0:T(8,128)(2,1)S(1)} copy-done((bf16[1,4,2,512,256]{4,3,2,1,0:T(8,128)(2,1)S(1)}, bf16[1,4,2,512,256]{4,3,2,1,0:T(8,128)(2,1)}, u32[]{:S(2)}) %copy-start.3) | copy-done | bytes 2097176
  91.8 0.9 copy-done.13
  92.8 0.9 copy-done.15
  93.7 0.9 copy-done.17
  94.7 3.7 %shard_map.88 = (f32[256,128]{1,0:T(8,128)S(1)}, f32[256,128]{1,0:T(8,128)S(1)}) custom-call(s32[5]{0:T(128)S(1)} %stack.20.bits_ref, f32[256,128]{1,0:T(8,128)S(1)} %get-tuple-element.25.own_ref.refs_7_, f32[256,128]{1,0:T(8,128)S(1)} %collective-permute-done.4.partner_ref, bf16[2,512,512]{2,1,0:T(8,128)(2,1)S(1)} %get-tuple-element.35.inverse_ref, ...), custom_call_target="tpu_custom_call" | custom-call | tf_op jit(solution)/shard_map/pallas_call | solution.py:253
  98.5 0.1 collective-permute-start.5
  98.5 1.3 collective-permute-done.5.other_ref
  99.9 4.7 %shard_map.89 = s16[32,144,128]{2,1,0:T(8,128)(2,1)S(1)} custom-call(s32[1]{0:T(128)} %bitcast.bit_ref, f32[256,128]{1,0:T(8,128)S(1)} %get-tuple-element.30.mine_ref, f32[256,128]{1,0:T(8,128)S(1)} %collective-permute-done.5.other_ref, f32[256,256]{1,0:T(8,128)S(1)} %get-tuple-element.21.coef_ref, f32[1024,256]{1,0:T(8,128)S(1)} %copy-done.10, ...), custom_call_target="tpu_custom_call" | custom-call | tf_op jit(solution)/shard_map/pallas_call | solution.py:253
  104.6 33.6 %all_to_all.10.got_ref = s16[32,144,128]{2,1,0:T(8,128)(2,1)S(1)} all-to-all(s16[32,144,128]{2,1,0:T(8,128)(2,1)S(1)} %shard_map.89), channel_id=1, replica_groups=mesh['row'=8,'col'=4] {'row','col'}, dimensions={0} | all-to-all | bytes 2359296 | tf_op jit(solution)/shard_map/all_to_all | solution.py:294
  138.2 3.8 %shard_map.90 = f32[1024,256]{1,0:T(8,128)} custom-call(s16[32,144,128]{2,1,0:T(8,128)(2,1)S(1)} %all_to_all.10.got_ref, s32[1,1024]{1,0:T(1,128)S(1)} %get-tuple-element.34.slot_ref), custom_call_target="tpu_custom_call" | custom-call | tf_op jit(solution)/shard_map/pallas_call | solution.py:253
  (20 shorter events, 0.1 us)
Async XLA Ops:
  0.0 1.0 copy-start.11
  1.0 0.7 copy-start.18
  4.5 36.4 %all-to-all-start = ((bf16[32,144,128]{2,1,0:T(8,128)(2,1)}), bf16[32,144,128]{2,1,0:T(8,128)(2,1)S(1)}, u32[]{:S(2)}, u32[]{:S(2)}) async-start(bf16[32,144,128]{2,1,0:T(8,128)(2,1)} %get-tuple-element.20), calls=%async_computation | async-start | bytes 2359296 | tf_op jit(solution)/shard_map/all_to_all | solution.py:294
  40.9 1.2 copy-start.7
  42.1 8.4 %copy-start.19 = (bf16[1,4,2,512,256]{4,3,2,1,0:T(8,128)(2,1)S(1)}, bf16[1,4,2,512,256]{4,3,2,1,0:T(8,128)(2,1)}, u32[]{:S(2)}) copy-start(bf16[1,4,2,512,256]{4,3,2,1,0:T(8,128)(2,1)} %param.14) | copy-start | bytes 6291460
  49.5 1.0 copy-start.9
  50.5 1.6 %copy-start.2 = (bf16[2,512,512]{2,1,0:T(8,128)(2,1)S(1)}, bf16[2,512,512]{2,1,0:T(8,128)(2,1)}, u32[]{:S(2)}) copy-start(bf16[2,512,512]{2,1,0:T(8,128)(2,1)} %get-tuple-element.38.inverse_ref) | copy-start | bytes 3145732
  50.5 1.4 collective-permute-start
  51.8 18.6 %copy-start = (bf16[2,512,512]{2,1,0:T(8,128)(2,1)S(1)}, bf16[2,512,512]{2,1,0:T(8,128)(2,1)}, u32[]{:S(2)}) copy-start(bf16[2,512,512]{2,1,0:T(8,128)(2,1)} %get-tuple-element.36.inverse_ref) | copy-start | bytes 3145732
  53.1 0.7 copy-start.12
  53.8 5.7 %collective-permute-start.1 = (f32[256,128]{1,0:T(8,128)S(1)}, f32[256,128]{1,0:T(8,128)}, u32[]{:S(2)}, u32[]{:S(2)}) collective-permute-start(f32[256,128]{1,0:T(8,128)S(1)} %get-tuple-element.22.own_ref.refs_4_), channel_id=1, source_target_pairs={{0,2},{1,3},{2,0},{3,1},{4,6},{5,7},{6,4},{7,5},{8,10},{9,11},{10,... | collective-permute-start | bytes 393224 | tf_op jit(solution)/shard_map/ppermute | solution.py:268
  59.5 1.2 copy-start.1
  60.8 1.0 copy-start.6
  64.4 0.7 copy-start.14
  65.1 5.3 %collective-permute-start.2 = (f32[256,128]{1,0:T(8,128)}, f32[256,128]{1,0:T(8,128)}, u32[]{:S(2)}, u32[]{:S(2)}) collective-permute-start(f32[256,128]{1,0:T(8,128)} %get-tuple-element.23.own_ref.refs_5_), channel_id=1, source_target_pairs={{0,4},{4,0},{8,12},{12,8},{16,20},{20,16},{24,28},{28,24},{1,5},{5... | collective-permute-start | bytes 393224 | tf_op jit(solution)/shard_map/ppermute | solution.py:268
  70.4 1.0 copy-start.5
  74.1 0.7 copy-start.16
  74.8 5.2 %collective-permute-start.3 = (f32[256,128]{1,0:T(8,128)}, f32[256,128]{1,0:T(8,128)S(1)}, u32[]{:S(2)}, u32[]{:S(2)}) collective-permute-start(f32[256,128]{1,0:T(8,128)} %get-tuple-element.24.own_ref.refs_6_), channel_id=1, source_target_pairs={{0,8},{4,12},{8,0},{12,4},{16,24},{20,28},{24,16},{28,20},{1,9},{5... | collective-permute-start | bytes 393224 | tf_op jit(solution)/shard_map/ppermute | solution.py:268
  80.0 1.0 copy-start.4
  83.0 7.3 %collective-permute-start.4 = (f32[256,128]{1,0:T(8,128)S(1)}, f32[256,128]{1,0:T(8,128)S(1)}, u32[]{:S(2)}, u32[]{:S(2)}) collective-permute-start(f32[256,128]{1,0:T(8,128)S(1)} %get-tuple-element.25.own_ref.refs_7_), channel_id=1, source_target_pairs={{0,16},{4,20},{8,24},{12,28},{16,0},{20,4},{24,8},{28,12},{1,17},{... | collective-permute-start | bytes 393224 | tf_op jit(solution)/shard_map/ppermute | solution.py:268
  90.2 1.6 %copy-start.3 = (bf16[1,4,2,512,256]{4,3,2,1,0:T(8,128)(2,1)S(1)}, bf16[1,4,2,512,256]{4,3,2,1,0:T(8,128)(2,1)}, u32[]{:S(2)}) copy-start(bf16[1,4,2,512,256]{4,3,2,1,0:T(8,128)(2,1)} %param.15) | copy-start | bytes 6291460
  91.8 0.9 copy-start.13
  92.8 0.9 copy-start.15
  93.7 0.9 copy-start.17
  94.7 5.2 %copy-start.8 = (bf16[1,2,1024,256]{3,2,1,0:T(8,128)(2,1)S(1)}, bf16[1,2,1024,256]{3,2,1,0:T(8,128)(2,1)}, u32[]{:S(2)}) copy-start(bf16[1,2,1024,256]{3,2,1,0:T(8,128)(2,1)} %param.12) | copy-start | bytes 3145732
  94.7 5.2 %copy-start.10 = (f32[1024,256]{1,0:T(8,128)S(1)}, f32[1024,256]{1,0:T(8,128)}, u32[]{:S(2)}) copy-start(f32[1024,256]{1,0:T(8,128)} %copy-done.9) | copy-start | bytes 3145732
  98.5 1.4 collective-permute-start.5

commit v2 on v1

--- a/solution.py
+++ b/solution.py
@@ -85,7 +85,14 @@
     return jnp.ceil(jnp.log2(jnp.maximum(largest, 2.0**-110)) * SCALE_STEPS)
 
 
-def pack_kernel(me_ref, order_ref, rows_ref, send_ref, slot_ref, *, devices, capacity):
+def fetch(source, target, sem):
+    copy = pltpu.make_async_copy(source, target, sem)
+    copy.start()
+    return copy
+
+
+def pack_kernel(me_ref, order_ref, rows_hbm, send_ref, slot_ref, rows_ref, sem, *, devices, capacity):
+    rows_copy = fetch(rows_hbm, rows_ref, sem.at[0])
     leaf_rows = rows_ref.shape[0]
     order = order_ref[...]
     target = order // leaf_rows
@@ -96,13 +103,6 @@
     rank = jnp.sum(hits * before, axis=0, keepdims=True).astype(jnp.int32)
     slot = target * capacity + rank
     slot_ref[...] = slot
-    rows = rows_ref[...].astype(F32)
-    first, second = swapped(rows[:, :LANES], rows[:, LANES:])
-    rows = jnp.concatenate([first, second], axis=1).astype(BF16)
-    chosen = (iota((devices * capacity, leaf_rows), 0) == slot).astype(F32).astype(BF16)
-    sent = matmul(chosen, rows).astype(BF16)
-    send_ref[:, :capacity, :] = sent[:, :LANES].reshape(devices, capacity, LANES)
-    send_ref[:, capacity : 2 * capacity, :] = sent[:, LANES:].reshape(devices, capacity, LANES)
     group = LANES // capacity
     lane = rank + lax.rem(me_ref[0], group) * capacity
     code = position + 1
@@ -119,6 +119,14 @@
         ],
         axis=1,
     ).astype(BF16)
+    chosen = (iota((devices * capacity, leaf_rows), 0) == slot).astype(F32).astype(BF16)
+    rows_copy.wait()
+    rows = rows_ref[...].astype(F32)
+    first, second = swapped(rows[:, :LANES], rows[:, LANES:])
+    rows = jnp.concatenate([first, second], axis=1).astype(BF16)
+    sent = matmul(chosen, rows).astype(BF16)
+    send_ref[:, :capacity, :] = sent[:, :LANES].reshape(devices, capacity, LANES)
+    send_ref[:, capacity : 2 * capacity, :] = sent[:, LANES:].reshape(devices, capacity, LANES)
 
 
 def positions(got_ref, devices, capacity):
@@ -128,7 +136,12 @@
     return jnp.sum(code.reshape(devices // group, group, LANES), axis=1) - 1.0
 
 
-def leaf_kernel(got_ref, inverse_ref, basis_ref, sol_ref, coef_ref, place_ref, *, devices, capacity):
+def leaf_kernel(
+    bit_ref, got_ref, inverse_hbm, basis_hbm, sol_hbm, own_ref, other_ref, place_ref,
+    inverse_ref, basis_ref, sol_ref, sem, *, devices, capacity,
+):
+    inverse_copies = [fetch(inverse_hbm.at[k], inverse_ref.at[k], sem.at[k]) for k in range(2)]
+    basis_copy = fetch(basis_hbm, basis_ref, sem.at[2])
     leaf_rows = sol_ref.shape[0]
     place = positions(got_ref, devices, capacity)
     place_ref[...] = place
@@ -150,9 +163,19 @@
     )
     placed = matmul(chosen, got)
     turned = rotated_all(placed)
-    sol = matmul(inverse_ref[0], placed.astype(BF16)) + matmul(inverse_ref[1], turned.astype(BF16))
+    inverse_copies[0].wait()
+    sol = matmul(inverse_ref[0], placed.astype(BF16))
+    inverse_copies[1].wait()
+    sol = sol + matmul(inverse_ref[1], turned.astype(BF16))
     sol_ref[...] = sol
-    coef_ref[...] = apply_transposed(basis_ref[0], basis_ref[1], sol)
+    sol_copy = fetch(sol_ref, sol_hbm, sem.at[3])
+    basis_copy.wait()
+    coef = apply_transposed(basis_ref[0], basis_ref[1], sol)
+    first, second = coef[:, :LANES], coef[:, LANES:]
+    odd = bit_ref[0] == 1
+    own_ref[...] = jnp.where(odd, second, first)
+    other_ref[...] = jnp.where(odd, first, second)
+    sol_copy.wait()
 
 
 def node_rhs(upper, own, partner):
@@ -162,11 +185,20 @@
     )
 
 
-def node_kernel(bit_ref, own_ref, partner_ref, inverse_ref, basis_ref, sol_ref, coef_ref):
+def node_kernel(
+    bit_ref, own_ref, partner_ref, inverse_hbm, basis_hbm, sol_hbm, coef_ref,
+    inverse_ref, basis_ref, sol_ref, sem, *, level,
+):
+    inverse_copy = fetch(inverse_hbm.at[0, level], inverse_ref, sem.at[0])
+    basis_copy = fetch(basis_hbm.at[0, level], basis_ref, sem.at[1])
     rhs = node_rhs(bit_ref[0], own_ref[...], partner_ref[...])
+    inverse_copy.wait()
     sol = apply_complex(inverse_ref[0], inverse_ref[1], rhs)
     sol_ref[...] = sol
+    sol_copy = fetch(sol_ref, sol_hbm, sem.at[2])
+    basis_copy.wait()
     coef_ref[...] = apply_transposed(basis_ref[0], basis_ref[1], sol)
+    sol_copy.wait()
 
 
 def half_of(bit, x):
@@ -174,45 +206,59 @@
     return jnp.where(bit == 1, x[rank:], x[:rank])
 
 
-def descent_kernel(bits_ref, own_ref, partner_ref, inverse_ref, lift_ref, *refs):
+def descent_kernel(bits_ref, own_ref, partner_ref, inverse_hbm, lift_hbm, *refs):
     levels = bits_ref.shape[0]
-    sols = refs[: levels - 1]
-    coefs = refs[levels - 1 : 2 * levels - 2]
-    mine_ref, other_ref = refs[2 * levels - 2 :]
-    rhs = node_rhs(bits_ref[levels - 1], own_ref[...], partner_ref[...])
+    below = levels - 1
+    sols_hbm, coefs = refs[:below], refs[below : 2 * below]
+    mine_ref, other_ref, inverse_ref, lift_ref, sols_ref, sem = refs[2 * below :]
+    inverse_copy = fetch(inverse_hbm.at[0, below], inverse_ref, sem.at[0])
+    copies = {}
+    for k in range(below - 1, -1, -1):
+        copies[k] = (
+            fetch(lift_hbm.at[0, k], lift_ref.at[k], sem.at[1 + 2 * k]),
+            fetch(sols_hbm[k], sols_ref.at[k], sem.at[2 + 2 * k]),
+        )
+    rhs = node_rhs(bits_ref[below], own_ref[...], partner_ref[...])
+    inverse_copy.wait()
     down = apply_complex(inverse_ref[0], inverse_ref[1], rhs)
-    for height in range(levels - 1, 0, -1):
-        gap = coefs[height - 1][...] - half_of(bits_ref[height], down)
-        down = sols[height - 1][...] - apply_complex(
-            lift_ref[height - 1, 0], lift_ref[height - 1, 1], gap
-        )
+    for k in range(below - 1, -1, -1):
+        gap = coefs[k][...] - half_of(bits_ref[k + 1], down)
+        for copy in copies[k]:
+            copy.wait()
+        down = sols_ref[k] - apply_complex(lift_ref[k, 0], lift_ref[k, 1], gap)
     mine_ref[...] = half_of(bits_ref[0], down)
     other_ref[...] = half_of(1 - bits_ref[0], down)
 
 
 def finish_kernel(
-    bit_ref, mine_ref, other_ref, coef_ref, sol_ref, lift_ref, place_ref, send_ref, *, devices, capacity
+    bit_ref, mine_ref, others_ref, own_ref, other_ref, sol_hbm, lift_hbm, place_ref, send_ref,
+    sol_ref, lift_ref, sem, *, devices, capacity,
 ):
+    lift_copy = fetch(lift_hbm, lift_ref, sem.at[0])
+    sol_copy = fetch(sol_hbm, sol_ref, sem.at[1])
     leaf_rows = sol_ref.shape[0]
+    place = jnp.transpose(place_ref[...])
+    where_from = iota((LANES, leaf_rows), 1).astype(F32)
+    chosen = jnp.concatenate(
+        [
+            (where_from == place[:, k : k + 1]).astype(F32).astype(BF16)
+            for k in range(place.shape[1])
+        ],
+        axis=0,
+    )
     swap = bit_ref[0] == 1
-    mine, other = mine_ref[...], other_ref[...]
-    h = jnp.concatenate([jnp.where(swap, other, mine), jnp.where(swap, mine, other)], axis=1)
-    sol = sol_ref[...] - apply_complex(lift_ref[0], lift_ref[1], coef_ref[...] - h)
+    mine = own_ref[...] - mine_ref[...]
+    other = other_ref[...] - others_ref[...]
+    gap = jnp.concatenate([jnp.where(swap, other, mine), jnp.where(swap, mine, other)], axis=1)
+    lift_copy.wait()
+    change = apply_complex(lift_ref[0], lift_ref[1], gap)
+    sol_copy.wait()
+    sol = sol_ref[...] - change
     code = scale_code(sol)
     level = jnp.clip(jnp.round(sol * inverse_unit_of(code)), -32767.0, 32767.0)
     high = jnp.round(level * (1.0 / 256.0))
     low = level - high * 256.0
     parts = jnp.concatenate([high.astype(BF16), low.astype(BF16)], axis=1)
-    place = place_ref[...]
-    place = jnp.transpose(place)
-    where_from = iota((LANES, leaf_rows), 1).astype(F32)
-    chosen = jnp.concatenate(
-        [
-            (where_from == place[:, k : k + 1]).astype(F32).astype(BF16)
-            for k in range(place.shape[1])
-        ],
-        axis=0,
-    )
     both = matmul(chosen, parts)
     width = sol.shape[1]
     level = (both[:, :width] * 256.0 + both[:, width:]).astype(jnp.int32).astype(jnp.int16)
@@ -247,17 +293,29 @@
     out_ref[:, LANES:] = second
 
 
-def call(kernel, out_shapes, operands, smem=0, flops=0, moved=0):
-    vmem = pl.BlockSpec(memory_space=pltpu.VMEM)
-    scalar = pl.BlockSpec(memory_space=pltpu.SMEM)
-    return pl.pallas_call(
+def call(kernel, outs, operands, scratch=(), vmem=24):
+    specs = {
+        "smem": pl.BlockSpec(memory_space=pltpu.SMEM),
+        "vmem": pl.BlockSpec(memory_space=pltpu.VMEM),
+        "hbm": pl.BlockSpec(memory_space=pl.ANY),
+    }
+    results = pl.pallas_call(
         kernel,
-        out_shape=out_shapes,
-        in_specs=[scalar] * smem + [vmem] * (len(operands) - smem),
-        out_specs=jax.tree.map(lambda _: vmem, out_shapes),
-        compiler_params=pltpu.CompilerParams(vmem_limit_bytes=48 * 2**20),
-        cost_estimate=pl.CostEstimate(flops=flops, bytes_accessed=moved, transcendentals=0),
-    )(*operands)
+        out_shape=[pltpu.HBM(out.shape, out.dtype) if space == "hbm" else out for out, space in outs],
+        in_specs=[specs[space] for _, space in operands],
+        out_specs=[specs[space] for _, space in outs],
+        scratch_shapes=[
+            pltpu.SemaphoreType.DMA((one,)) if isinstance(one, int) else pltpu.VMEM(one.shape, one.dtype)
+            for one in scratch
+        ],
+        compiler_params=pltpu.CompilerParams(vmem_limit_bytes=vmem * 2**20),
+    )(
+        *[
+            pltpu.with_memory_space_constraint(array, pltpu.HBM) if space == "hbm" else array
+            for array, space in operands
+        ]
+    )
+    return results
 
 
 def shape(dims, dtype=F32):
@@ -300,60 +358,87 @@
 
     send, slot = call(
         functools.partial(pack_kernel, **sizes),
-        (shape(block, BF16), shape((1, leaf_rows), jnp.int32)),
-        (me.reshape(1), tree_order.reshape(1, leaf_rows), right_sides),
-        smem=1,
+        [(shape(block, BF16), "vmem"), (shape((1, leaf_rows), jnp.int32), "vmem")],
+        [(me.reshape(1), "smem"), (tree_order.reshape(1, leaf_rows), "vmem"), (right_sides, "hbm")],
+        [shape(right_sides.shape, BF16), 1],
     )
     got = exchange(send)
-    leaf_sol, leaf_coef, place = call(
+    half = shape((rank, LANES))
+    leaf_sol, own, other, place = call(
         functools.partial(leaf_kernel, **sizes),
-        (
+        [
+            (shape((leaf_rows, width)), "hbm"),
+            (half, "vmem"),
+            (half, "vmem"),
+            (shape((devices * capacity // LANES, LANES)), "vmem"),
+        ],
+        [(bits[0].reshape(1), "smem"), (got, "vmem"), (leaf_inverse[0], "hbm"), (leaf_basis[0], "hbm")],
+        [
+            shape(leaf_inverse.shape[1:], BF16),
+            shape(leaf_basis.shape[1:], BF16),
             shape((leaf_rows, width)),
-            shape((rank, width)),
-            shape((devices * capacity // LANES, LANES)),
-        ),
-        (got, leaf_inverse[0], leaf_basis[0]),
-    )
-    odd = bits[0] == 1
-    own = jnp.where(odd, leaf_coef[:, LANES:], leaf_coef[:, :LANES])
-    other = jnp.where(odd, leaf_coef[:, :LANES], leaf_coef[:, LANES:])
+            4,
+        ],
+    )
+    leaf_own, leaf_other = own, other
+    whole = shape((2 * rank, LANES))
+    inverse_shape = shape(node_inverse.shape[2:], BF16)
     sols, coefs = [], []
     for height in range(1, levels):
         partner = partner_of(other if height == 1 else own, height - 1)
         sol, own = call(
-            node_kernel,
-            (shape((2 * rank, LANES)), shape((rank, LANES))),
-            (
-                bits[height - 1].reshape(1),
-                own,
-                partner,
-                node_inverse[0, height - 1],
-                node_basis[0, height - 1],
-            ),
-            smem=1,
+            functools.partial(node_kernel, level=height - 1),
+            [(whole, "hbm"), (half, "vmem")],
+            [
+                (bits[height - 1].reshape(1), "smem"),
+                (own, "vmem"),
+                (partner, "vmem"),
+                (node_inverse, "hbm"),
+                (node_basis, "hbm"),
+            ],
+            [inverse_shape, shape(node_basis.shape[2:], BF16), whole, 3],
+            vmem=12,
         )
         sols.append(sol)
         coefs.append(own)
     partner = partner_of(own, levels - 1)
     mine, other = call(
         descent_kernel,
-        (shape((rank, LANES)), shape((rank, LANES))),
-        (jnp.stack(bits), own, partner, node_inverse[0, levels - 1], node_lift[0], *sols, *coefs),
-        smem=1,
+        [(half, "vmem"), (half, "vmem")],
+        [(jnp.stack(bits), "smem"), (own, "vmem"), (partner, "vmem"), (node_inverse, "hbm"), (node_lift, "hbm")]
+        + [(sol, "hbm") for sol in sols]
+        + [(coef, "vmem") for coef in coefs],
+        [
+            inverse_shape,
+            shape(node_lift.shape[1:], BF16),
+            shape((levels - 1,) + whole.shape),
+            2 * levels - 1,
+        ],
+        vmem=16,
     )
     other = partner_of(other, 0)
-    back = call(
+    (back,) = call(
         functools.partial(finish_kernel, **sizes),
-        shape(block, jnp.int16),
-        (bits[0].reshape(1), mine, other, leaf_coef, leaf_sol, leaf_lift[0], place),
-        smem=1,
+        [(shape(block, jnp.int16), "vmem")],
+        [
+            (bits[0].reshape(1), "smem"),
+            (mine, "vmem"),
+            (other, "vmem"),
+            (leaf_own, "vmem"),
+            (leaf_other, "vmem"),
+            (leaf_sol, "hbm"),
+            (leaf_lift[0], "hbm"),
+            (place, "vmem"),
+        ],
+        [shape((leaf_rows, width)), shape(leaf_lift.shape[1:], BF16), 2],
     )
     returned = exchange(back)
-    return call(
+    (result,) = call(
         functools.partial(unpack_kernel, **sizes),
-        shape((leaf_rows, width)),
-        (returned, slot),
-    )
+        [(shape((leaf_rows, width)), "vmem")],
+        [(returned, "vmem"), (slot, "vmem")],
+    )
+    return result
 
 
 def solution(mesh):

time: 143 us -> 132 us (0.923)
  local copies, waits for them, and re-layouts: 20.6 us -> 0.77 us
  waiting for transfers between devices: 44.9 us -> 49.3 us
  Pallas kernels: 30.6 us -> 34.8 us
    unnamed x40 -> x2, local copies, waits for them, and re-layouts: 15.1 us -> 0.69 us
    squeeze x2 -> x0, local copies, waits for them, and re-layouts: 5.49 us -> none  [the longest x1 4.29 us: per_device(): node_inverse[0, levels - 1]]
    pallas_call x9, Pallas kernels: 30.6 us -> 34.8 us  [call(): pl.pallas_call(kernel, out_shape=[pltpu.HBM(out.shape, out.dtype) if spac...]
    all_to_all x1, waiting for transfers between devices: 24.8 us -> 28.9 us  [exchange(): lax.all_to_all(blocks, ('row', 'col'), split_axis=0, concat_axis=0, tiled...]
  transfers between devices with their start and end apart: 7 -> 7, of which waited for: 7 -> 7; matrix products, arithmetic and copies ran while one was open for 4% -> 0% of each run, Pallas kernels for 0% -> 0%
where the time goes in v2:
time: 132 us; the launch traced here: 131 us
  waiting for transfers between devices  49.3 us (37%)
  Pallas kernels  34.8 us (26%)
  blocking collectives  33.6 us (25%)
  starting transfers between devices  12.8 us (10%)
    pallas_call x9, Pallas kernels, call(): pl.pallas_call(kernel, out_shape=[pltpu.HBM(out.shape, out.dtype) if spac...  34.8 us
    all_to_all x1, blocking collectives, exchange(): lax.all_to_all(blocks, ('row', 'col'), split_axis=0, concat_axis=0, tiled...  33.6 us
    all_to_all x1, waiting for transfers between devices, exchange(): lax.all_to_all(blocks, ('row', 'col'), split_axis=0, concat_axis=0, tiled...  28.9 us
    ppermute x6, waiting for transfers between devices, from_partner(): lax.ppermute(shard, axis, [(i, i ^ 1 << apart) for i in range(lax.axis_si...  20.4 us
    all_to_all x1, starting transfers between devices, exchange(): lax.all_to_all(blocks, ('row', 'col'), split_axis=0, concat_axis=0, tiled...  7.48 us
    ppermute x6, starting transfers between devices, from_partner(): lax.ppermute(shard, axis, [(i, i ^ 1 << apart) for i in range(lax.axis_si...  5.31 us
  transfers between devices with their start and end apart: 7, of which 7 were waited for; matrix products, arithmetic and copies ran while one was open for 0% of the time, Pallas kernels for 0%

profile of v2, /device:TPU:0, one launch (start us, length us, event | category | flops | bytes accessed | tf_op | source)
XLA Modules:
  0.0 131.3 jit_solution(9915093125063157552)
XLA Ops:
  0.0 0.0 copy-start
  0.0 0.7 copy-done
  0.7 4.0 %shard_map.82 = (bf16[32,144,128]{2,1,0:T(8,128)(2,1)}, s32[1,1024]{1,0:T(1,128)S(1)}) custom-call(s32[1]{0:T(128)} %bitcast.5.me_ref, s32[1,1024]{1,0:T(1,128)S(1)} %bitcast.10, bf16[1024,256]{1,0:T(8,128)(2,1)} %rows_hbm.1), custom_call_target="tpu_custom_call" | custom-call | tf_op jit(solution)/shard_map/pallas_call | solution.py:302
  4.7 7.5 %all-to-all-start = ((bf16[32,144,128]{2,1,0:T(8,128)(2,1)}), bf16[32,144,128]{2,1,0:T(8,128)(2,1)S(1)}, u32[]{:S(2)}, u32[]{:S(2)}) async-start(bf16[32,144,128]{2,1,0:T(8,128)(2,1)} %get-tuple-element.21), calls=%async_computation | async-start | bytes 2359296 | tf_op jit(solution)/shard_map/all_to_all | solution.py:352
  12.2 28.9 %all-to-all-done.got_ref = bf16[32,144,128]{2,1,0:T(8,128)(2,1)S(1)} async-done(((bf16[32,144,128]{2,1,0:T(8,128)(2,1)}), bf16[32,144,128]{2,1,0:T(8,128)(2,1)S(1)}, u32[]{:S(2)}, u32[]{:S(2)}) %all-to-all-start) | async-done | bytes 1179680 | tf_op jit(solution)/shard_map/all_to_all | solution.py:352
  41.1 6.0 %shard_map.83 = (f32[1024,256]{1,0:T(8,128)}, f32[256,128]{1,0:T(8,128)S(1)}, f32[256,128]{1,0:T(8,128)S(1)}, f32[16,128]{1,0:T(8,128)S(1)}) custom-call(s32[1]{0:T(128)} %bitcast.bit_ref, bf16[32,144,128]{2,1,0:T(8,128)(2,1)S(1)} %all-to-all-done.got_ref, bf16[2,1024,1024]{2,1,0:T(8,128)(2,1)} %bitcast.11, bf16[2,1024,256]{2,1,0:T(8,128)(2,1)} %bitcast.12), custom_call_target="tpu_custom_call" | custom-call | tf_op jit(solution)/shard_map/pallas_call | solution.py:302
  47.1 0.1 collective-permute-start
  47.2 1.3 %collective-permute-done.partner_ref = f32[256,128]{1,0:T(8,128)S(1)} collective-permute-done((f32[256,128]{1,0:T(8,128)S(1)}, f32[256,128]{1,0:T(8,128)S(1)}, u32[]{:S(2)}, u32[]{:S(2)}) %collective-permute-start) | collective-permute-done | bytes 131104 | tf_op jit(solution)/shard_map/ppermute | solution.py:326
  48.5 2.6 %shard_map.84 = (f32[512,128]{1,0:T(8,128)}, f32[256,128]{1,0:T(8,128)S(1)}) custom-call(s32[1]{0:T(128)} %bitcast.bit_ref, f32[256,128]{1,0:T(8,128)S(1)} %get-tuple-element.22.own_ref, f32[256,128]{1,0:T(8,128)S(1)} %collective-permute-done.partner_ref, bf16[1,5,2,512,512]{4,3,2,1,0:T(8,128)(2,1)} %inverse_hbm.9, bf16[1,4,2,512,256]{4,3,2,1,0:T(8,128)(2,1)} %basis_hbm.7), custom_call_target="tpu_custom_call" | custom-call | tf_op jit(solution)/shard_map/pallas_call | solution.py:302
  51.1 1.5 %collective-permute-start.1 = (f32[256,128]{1,0:T(8,128)S(1)}, f32[256,128]{1,0:T(8,128)S(1)}, u32[]{:S(2)}, u32[]{:S(2)}) collective-permute-start(f32[256,128]{1,0:T(8,128)S(1)} %get-tuple-element.24.own_ref.refs_4_), channel_id=1, source_target_pairs={{0,2},{1,3},{2,0},{3,1},{4,6},{5,7},{6,4},{7,5},{8,10},{9,11},{10,... | collective-permute-start | bytes 393224 | tf_op jit(solution)/shard_map/ppermute | solution.py:326
  52.6 4.1 %collective-permute-done.1.partner_ref = f32[256,128]{1,0:T(8,128)S(1)} collective-permute-done((f32[256,128]{1,0:T(8,128)S(1)}, f32[256,128]{1,0:T(8,128)S(1)}, u32[]{:S(2)}, u32[]{:S(2)}) %collective-permute-start.1) | collective-permute-done | bytes 131104 | tf_op jit(solution)/shard_map/ppermute | solution.py:326
  56.8 2.6 %shard_map.85 = (f32[512,128]{1,0:T(8,128)}, f32[256,128]{1,0:T(8,128)S(1)}) custom-call(s32[1]{0:T(128)} %bitcast.1.bit_ref, f32[256,128]{1,0:T(8,128)S(1)} %get-tuple-element.24.own_ref.refs_4_, f32[256,128]{1,0:T(8,128)S(1)} %collective-permute-done.1.partner_ref, bf16[1,5,2,512,512]{4,3,2,1,0:T(8,128)(2,1)} %inverse_hbm.9, ...), custom_call_target="tpu_custom_call" | custom-call | tf_op jit(solution)/shard_map/pallas_call | solution.py:302
  59.3 1.5 %collective-permute-start.2 = (f32[256,128]{1,0:T(8,128)S(1)}, f32[256,128]{1,0:T(8,128)S(1)}, u32[]{:S(2)}, u32[]{:S(2)}) collective-permute-start(f32[256,128]{1,0:T(8,128)S(1)} %get-tuple-element.25.own_ref.refs_5_), channel_id=1, source_target_pairs={{0,4},{4,0},{8,12},{12,8},{16,20},{20,16},{24,28},{28,24},{1,5},{5... | collective-permute-start | bytes 393224 | tf_op jit(solution)/shard_map/ppermute | solution.py:326
  60.9 3.5 %collective-permute-done.2.partner_ref = f32[256,128]{1,0:T(8,128)S(1)} collective-permute-done((f32[256,128]{1,0:T(8,128)S(1)}, f32[256,128]{1,0:T(8,128)S(1)}, u32[]{:S(2)}, u32[]{:S(2)}) %collective-permute-start.2) | collective-permute-done | bytes 131104 | tf_op jit(solution)/shard_map/ppermute | solution.py:326
  64.4 2.6 %shard_map.86 = (f32[512,128]{1,0:T(8,128)}, f32[256,128]{1,0:T(8,128)S(1)}) custom-call(s32[1]{0:T(128)} %bitcast.2.bit_ref, f32[256,128]{1,0:T(8,128)S(1)} %get-tuple-element.25.own_ref.refs_5_, f32[256,128]{1,0:T(8,128)S(1)} %collective-permute-done.2.partner_ref, bf16[1,5,2,512,512]{4,3,2,1,0:T(8,128)(2,1)} %inverse_hbm.9, ...), custom_call_target="tpu_custom_call" | custom-call | tf_op jit(solution)/shard_map/pallas_call | solution.py:302
  67.0 0.8 collective-permute-start.3
  67.8 4.2 %collective-permute-done.3.partner_ref = f32[256,128]{1,0:T(8,128)S(1)} collective-permute-done((f32[256,128]{1,0:T(8,128)S(1)}, f32[256,128]{1,0:T(8,128)S(1)}, u32[]{:S(2)}, u32[]{:S(2)}) %collective-permute-start.3) | collective-permute-done | bytes 131104 | tf_op jit(solution)/shard_map/ppermute | solution.py:326
  72.0 2.6 %shard_map.87 = (f32[512,128]{1,0:T(8,128)}, f32[256,128]{1,0:T(8,128)S(1)}) custom-call(s32[1]{0:T(128)} %bitcast.3.bit_ref, f32[256,128]{1,0:T(8,128)S(1)} %get-tuple-element.26.own_ref.refs_6_, f32[256,128]{1,0:T(8,128)S(1)} %collective-permute-done.3.partner_ref, bf16[1,5,2,512,512]{4,3,2,1,0:T(8,128)(2,1)} %inverse_hbm.9, ...), custom_call_target="tpu_custom_call" | custom-call | tf_op jit(solution)/shard_map/pallas_call | solution.py:302
  74.6 1.4 %collective-permute-start.4 = (f32[256,128]{1,0:T(8,128)S(1)}, f32[256,128]{1,0:T(8,128)S(1)}, u32[]{:S(2)}, u32[]{:S(2)}) collective-permute-start(f32[256,128]{1,0:T(8,128)S(1)} %get-tuple-element.27.own_ref.refs_7_), channel_id=1, source_target_pairs={{0,16},{4,20},{8,24},{12,28},{16,0},{20,4},{24,8},{28,12},{1,17},{... | collective-permute-start | bytes 393224 | tf_op jit(solution)/shard_map/ppermute | solution.py:326
  76.0 0.1 stack.20.bits_ref
  76.1 5.9 %collective-permute-done.4.partner_ref = f32[256,128]{1,0:T(8,128)S(1)} collective-permute-done((f32[256,128]{1,0:T(8,128)S(1)}, f32[256,128]{1,0:T(8,128)S(1)}, u32[]{:S(2)}, u32[]{:S(2)}) %collective-permute-start.4) | collective-permute-done | bytes 131104 | tf_op jit(solution)/shard_map/ppermute | solution.py:326
  82.0 4.6 %shard_map.88 = (f32[256,128]{1,0:T(8,128)S(1)}, f32[256,128]{1,0:T(8,128)S(1)}) custom-call(s32[5]{0:T(128)S(1)} %stack.20.bits_ref, f32[256,128]{1,0:T(8,128)S(1)} %get-tuple-element.27.own_ref.refs_7_, f32[256,128]{1,0:T(8,128)S(1)} %collective-permute-done.4.partner_ref, bf16[1,5,2,512,512]{4,3,2,1,0:T(8,128)(2,1)} %inverse_hbm.9, ...), custom_call_target="tpu_custom_call" | custom-call | tf_op jit(solution)/shard_map/pallas_call | solution.py:302
  86.6 0.1 collective-permute-start.5
  86.7 1.3 %collective-permute-done.5.others_ref = f32[256,128]{1,0:T(8,128)S(1)} collective-permute-done((f32[256,128]{1,0:T(8,128)S(1)}, f32[256,128]{1,0:T(8,128)S(1)}, u32[]{:S(2)}, u32[]{:S(2)}) %collective-permute-start.5) | collective-permute-done | bytes 131104 | tf_op jit(solution)/shard_map/ppermute | solution.py:326
  88.0 6.0 %shard_map.89 = s16[32,144,128]{2,1,0:T(8,128)(2,1)S(1)} custom-call(s32[1]{0:T(128)} %bitcast.bit_ref, f32[256,128]{1,0:T(8,128)S(1)} %get-tuple-element.32.mine_ref, f32[256,128]{1,0:T(8,128)S(1)} %collective-permute-done.5.others_ref, f32[256,128]{1,0:T(8,128)S(1)} %get-tuple-element.22.own_ref, f32[256,128]{1,0:T(8,128)S(1)} %get-tuple-element.23.other_ref, ...), custom_call_target="tpu_custom_call" | custom-call | tf_op jit(solution)/shard_map/pallas_call | solution.py:302
  94.0 33.6 %all_to_all.10.got_ref = s16[32,144,128]{2,1,0:T(8,128)(2,1)S(1)} all-to-all(s16[32,144,128]{2,1,0:T(8,128)(2,1)S(1)} %shard_map.89), channel_id=1, replica_groups=mesh['row'=8,'col'=4] {'row','col'}, dimensions={0} | all-to-all | bytes 2359296 | tf_op jit(solution)/shard_map/all_to_all | solution.py:352
  127.6 3.8 %shard_map.90 = f32[1024,256]{1,0:T(8,128)} custom-call(s16[32,144,128]{2,1,0:T(8,128)(2,1)S(1)} %all_to_all.10.got_ref, s32[1,1024]{1,0:T(1,128)S(1)} %get-tuple-element.36.slot_ref), custom_call_target="tpu_custom_call" | custom-call | tf_op jit(solution)/shard_map/pallas_call | solution.py:302
Async XLA Ops:
  0.0 0.7 copy-start
  4.7 36.4 %all-to-all-start = ((bf16[32,144,128]{2,1,0:T(8,128)(2,1)}), bf16[32,144,128]{2,1,0:T(8,128)(2,1)S(1)}, u32[]{:S(2)}, u32[]{:S(2)}) async-start(bf16[32,144,128]{2,1,0:T(8,128)(2,1)} %get-tuple-element.21), calls=%async_computation | async-start | bytes 2359296 | tf_op jit(solution)/shard_map/all_to_all | solution.py:352
  47.1 1.4 %collective-permute-start = (f32[256,128]{1,0:T(8,128)S(1)}, f32[256,128]{1,0:T(8,128)S(1)}, u32[]{:S(2)}, u32[]{:S(2)}) collective-permute-start(f32[256,128]{1,0:T(8,128)S(1)} %get-tuple-element.23.other_ref), channel_id=1, source_target_pairs={{0,1},{1,0},{2,3},{3,2},{4,5},{5,4},{6,7},{7,6},{8,9},{9,8},{10,11... | collective-permute-start | bytes 393224 | tf_op jit(solution)/shard_map/ppermute | solution.py:326
  51.1 5.6 %collective-permute-start.1 = (f32[256,128]{1,0:T(8,128)S(1)}, f32[256,128]{1,0:T(8,128)S(1)}, u32[]{:S(2)}, u32[]{:S(2)}) collective-permute-start(f32[256,128]{1,0:T(8,128)S(1)} %get-tuple-element.24.own_ref.refs_4_), channel_id=1, source_target_pairs={{0,2},{1,3},{2,0},{3,1},{4,6},{5,7},{6,4},{7,5},{8,10},{9,11},{10,... | collective-permute-start | bytes 393224 | tf_op jit(solution)/shard_map/ppermute | solution.py:326
  59.3 5.0 %collective-permute-start.2 = (f32[256,128]{1,0:T(8,128)S(1)}, f32[256,128]{1,0:T(8,128)S(1)}, u32[]{:S(2)}, u32[]{:S(2)}) collective-permute-start(f32[256,128]{1,0:T(8,128)S(1)} %get-tuple-element.25.own_ref.refs_5_), channel_id=1, source_target_pairs={{0,4},{4,0},{8,12},{12,8},{16,20},{20,16},{24,28},{28,24},{1,5},{5... | collective-permute-start | bytes 393224 | tf_op jit(solution)/shard_map/ppermute | solution.py:326
  67.0 5.0 %collective-permute-start.3 = (f32[256,128]{1,0:T(8,128)S(1)}, f32[256,128]{1,0:T(8,128)S(1)}, u32[]{:S(2)}, u32[]{:S(2)}) collective-permute-start(f32[256,128]{1,0:T(8,128)S(1)} %get-tuple-element.26.own_ref.refs_6_), channel_id=1, source_target_pairs={{0,8},{4,12},{8,0},{12,4},{16,24},{20,28},{24,16},{28,20},{1,9},{5... | collective-permute-start | bytes 393224 | tf_op jit(solution)/shard_map/ppermute | solution.py:326
  74.6 7.3 %collective-permute-start.4 = (f32[256,128]{1,0:T(8,128)S(1)}, f32[256,128]{1,0:T(8,128)S(1)}, u32[]{:S(2)}, u32[]{:S(2)}) collective-permute-start(f32[256,128]{1,0:T(8,128)S(1)} %get-tuple-element.27.own_ref.refs_7_), channel_id=1, source_target_pairs={{0,16},{4,20},{8,24},{12,28},{16,0},{20,4},{24,8},{28,12},{1,17},{... | collective-permute-start | bytes 393224 | tf_op jit(solution)/shard_map/ppermute | solution.py:326
  86.6 1.4 %collective-permute-start.5 = (f32[256,128]{1,0:T(8,128)S(1)}, f32[256,128]{1,0:T(8,128)S(1)}, u32[]{:S(2)}, u32[]{:S(2)}) collective-permute-start(f32[256,128]{1,0:T(8,128)S(1)} %get-tuple-element.33), channel_id=1, source_target_pairs={{0,1},{1,0},{2,3},{3,2},{4,5},{5,4},{6,7},{7,6},{8,9},{9,8},{10,11... | collective-permute-start | bytes 393224 | tf_op jit(solution)/shard_map/ppermute | solution.py:326

commit v3 on v2

--- a/solution.py
+++ b/solution.py
@@ -8,7 +8,7 @@
 from jax.sharding import PartitionSpec as P
 
 LANES = 128
-EXTRA = 16
+EXTRA = 8
 CODE_BASE = 32
 SCALE_STEPS = 64
 BF16 = jnp.bfloat16
@@ -111,13 +111,11 @@
     codes = jnp.concatenate([hits * high.astype(F32), hits * low.astype(F32)], axis=0)
     places = (iota((LANES, leaf_rows), 0) == lane).astype(F32).astype(BF16)
     spread = matmul_nt(codes.astype(BF16), places)
-    eight = (devices, EXTRA // 2, LANES)
-    send_ref[:, 2 * capacity :, :] = jnp.concatenate(
-        [
-            jnp.broadcast_to(spread[:devices].reshape(devices, 1, LANES), eight),
-            jnp.broadcast_to(spread[devices:].reshape(devices, 1, LANES), eight),
-        ],
-        axis=1,
+    extra = (devices, EXTRA, LANES)
+    send_ref[:, 2 * capacity :, :] = jnp.where(
+        iota(extra, 1) < EXTRA // 2,
+        jnp.broadcast_to(spread[:devices].reshape(devices, 1, LANES), extra),
+        jnp.broadcast_to(spread[devices:].reshape(devices, 1, LANES), extra),
     ).astype(BF16)
     chosen = (iota((devices * capacity, leaf_rows), 0) == slot).astype(F32).astype(BF16)
     rows_copy.wait()
@@ -136,12 +134,22 @@
     return jnp.sum(code.reshape(devices // group, group, LANES), axis=1) - 1.0
 
 
+def load_kernel(after_ref, *refs, picks):
+    count = len(picks)
+    sources, targets, sem = refs[:count], refs[count : 2 * count], refs[2 * count]
+    copies = [
+        fetch(source.at[pick], target, sem.at[k])
+        for k, (source, target, pick) in enumerate(zip(sources, targets, picks))
+    ]
+    for copy in copies:
+        copy.wait()
+
+
 def leaf_kernel(
-    bit_ref, got_ref, inverse_hbm, basis_hbm, sol_hbm, own_ref, other_ref, place_ref,
-    inverse_ref, basis_ref, sol_ref, sem, *, devices, capacity,
+    bit_ref, got_ref, inverse_hbm, basis_ref, sol_hbm, own_ref, other_ref, place_ref,
+    inverse_ref, sol_ref, sem, *, devices, capacity,
 ):
-    inverse_copies = [fetch(inverse_hbm.at[k], inverse_ref.at[k], sem.at[k]) for k in range(2)]
-    basis_copy = fetch(basis_hbm, basis_ref, sem.at[2])
+    copies = [fetch(inverse_hbm.at[0, k], inverse_ref.at[k], sem.at[1 + k]) for k in range(2)]
     leaf_rows = sol_ref.shape[0]
     place = positions(got_ref, devices, capacity)
     place_ref[...] = place
@@ -163,13 +171,12 @@
     )
     placed = matmul(chosen, got)
     turned = rotated_all(placed)
-    inverse_copies[0].wait()
+    copies[0].wait()
     sol = matmul(inverse_ref[0], placed.astype(BF16))
-    inverse_copies[1].wait()
+    copies[1].wait()
     sol = sol + matmul(inverse_ref[1], turned.astype(BF16))
     sol_ref[...] = sol
-    sol_copy = fetch(sol_ref, sol_hbm, sem.at[3])
-    basis_copy.wait()
+    sol_copy = fetch(sol_ref, sol_hbm, sem.at[0])
     coef = apply_transposed(basis_ref[0], basis_ref[1], sol)
     first, second = coef[:, :LANES], coef[:, LANES:]
     odd = bit_ref[0] == 1
@@ -186,17 +193,12 @@
 
 
 def node_kernel(
-    bit_ref, own_ref, partner_ref, inverse_hbm, basis_hbm, sol_hbm, coef_ref,
-    inverse_ref, basis_ref, sol_ref, sem, *, level,
+    bit_ref, own_ref, partner_ref, inverse_ref, basis_ref, sol_hbm, coef_ref, sol_ref, sem
 ):
-    inverse_copy = fetch(inverse_hbm.at[0, level], inverse_ref, sem.at[0])
-    basis_copy = fetch(basis_hbm.at[0, level], basis_ref, sem.at[1])
     rhs = node_rhs(bit_ref[0], own_ref[...], partner_ref[...])
-    inverse_copy.wait()
     sol = apply_complex(inverse_ref[0], inverse_ref[1], rhs)
     sol_ref[...] = sol
-    sol_copy = fetch(sol_ref, sol_hbm, sem.at[2])
-    basis_copy.wait()
+    sol_copy = fetch(sol_ref, sol_hbm, sem.at[0])
     coef_ref[...] = apply_transposed(basis_ref[0], basis_ref[1], sol)
     sol_copy.wait()
 
@@ -206,26 +208,16 @@
     return jnp.where(bit == 1, x[rank:], x[:rank])
 
 
-def descent_kernel(bits_ref, own_ref, partner_ref, inverse_hbm, lift_hbm, *refs):
+def descent_kernel(bits_ref, own_ref, partner_ref, inverse_ref, lift_ref, *refs):
     levels = bits_ref.shape[0]
     below = levels - 1
-    sols_hbm, coefs = refs[:below], refs[below : 2 * below]
-    mine_ref, other_ref, inverse_ref, lift_ref, sols_ref, sem = refs[2 * below :]
-    inverse_copy = fetch(inverse_hbm.at[0, below], inverse_ref, sem.at[0])
-    copies = {}
-    for k in range(below - 1, -1, -1):
-        copies[k] = (
-            fetch(lift_hbm.at[0, k], lift_ref.at[k], sem.at[1 + 2 * k]),
-            fetch(sols_hbm[k], sols_ref.at[k], sem.at[2 + 2 * k]),
-        )
+    sols, coefs = refs[:below], refs[below : 2 * below]
+    mine_ref, other_ref = refs[2 * below :]
     rhs = node_rhs(bits_ref[below], own_ref[...], partner_ref[...])
-    inverse_copy.wait()
     down = apply_complex(inverse_ref[0], inverse_ref[1], rhs)
     for k in range(below - 1, -1, -1):
         gap = coefs[k][...] - half_of(bits_ref[k + 1], down)
-        for copy in copies[k]:
-            copy.wait()
-        down = sols_ref[k] - apply_complex(lift_ref[k, 0], lift_ref[k, 1], gap)
+        down = sols[k][...] - apply_complex(lift_ref[k, 0], lift_ref[k, 1], gap)
     mine_ref[...] = half_of(bits_ref[0], down)
     other_ref[...] = half_of(1 - bits_ref[0], down)
 
@@ -264,9 +256,11 @@
     level = (both[:, :width] * 256.0 + both[:, width:]).astype(jnp.int32).astype(jnp.int16)
     send_ref[:, :capacity, :] = level[:, :LANES].reshape(devices, capacity, LANES)
     send_ref[:, capacity : 2 * capacity, :] = level[:, LANES:].reshape(devices, capacity, LANES)
-    eight = (EXTRA // 2, LANES)
-    extra = jnp.concatenate(
-        [jnp.broadcast_to(code[:, :LANES], eight), jnp.broadcast_to(code[:, LANES:], eight)], axis=0
+    extra = (EXTRA, LANES)
+    extra = jnp.where(
+        iota(extra, 0) < EXTRA // 2,
+        jnp.broadcast_to(code[:, :LANES], extra),
+        jnp.broadcast_to(code[:, LANES:], extra),
     )
     extra = extra.astype(jnp.int32).astype(jnp.int16)
     send_ref[:, 2 * capacity :, :] = jnp.broadcast_to(
@@ -298,6 +292,7 @@
         "smem": pl.BlockSpec(memory_space=pltpu.SMEM),
         "vmem": pl.BlockSpec(memory_space=pltpu.VMEM),
         "hbm": pl.BlockSpec(memory_space=pl.ANY),
+        "any": pl.BlockSpec(memory_space=pl.ANY),
     }
     results = pl.pallas_call(
         kernel,
@@ -362,7 +357,18 @@
         [(me.reshape(1), "smem"), (tree_order.reshape(1, leaf_rows), "vmem"), (right_sides, "hbm")],
         [shape(right_sides.shape, BF16), 1],
     )
+    def load(after, weights, picks):
+        shapes = [jax.eval_shape(lambda w, pick=pick: w[pick], w) for w, pick in zip(weights, picks)]
+        return call(
+            functools.partial(load_kernel, picks=picks),
+            [(shape(one.shape, one.dtype), "vmem") for one in shapes],
+            [(after, "any")] + [(weight, "hbm") for weight in weights],
+            [len(weights)],
+            vmem=4,
+        )
+
     got = exchange(send)
+    (leaf_basis,) = load(slot, (leaf_basis,), (0,))
     half = shape((rank, LANES))
     leaf_sol, own, other, place = call(
         functools.partial(leaf_kernel, **sizes),
@@ -372,48 +378,41 @@
             (half, "vmem"),
             (shape((devices * capacity // LANES, LANES)), "vmem"),
         ],
-        [(bits[0].reshape(1), "smem"), (got, "vmem"), (leaf_inverse[0], "hbm"), (leaf_basis[0], "hbm")],
-        [
-            shape(leaf_inverse.shape[1:], BF16),
-            shape(leaf_basis.shape[1:], BF16),
-            shape((leaf_rows, width)),
-            4,
-        ],
+        [(bits[0].reshape(1), "smem"), (got, "vmem"), (leaf_inverse, "hbm"), (leaf_basis, "vmem")],
+        [shape(leaf_inverse.shape[1:], BF16), shape((leaf_rows, width)), 3],
     )
     leaf_own, leaf_other = own, other
     whole = shape((2 * rank, LANES))
-    inverse_shape = shape(node_inverse.shape[2:], BF16)
     sols, coefs = [], []
     for height in range(1, levels):
         partner = partner_of(other if height == 1 else own, height - 1)
+        pick = (0, height - 1)
+        inverse, basis = load(own, (node_inverse, node_basis), (pick, pick))
         sol, own = call(
-            functools.partial(node_kernel, level=height - 1),
+            node_kernel,
             [(whole, "hbm"), (half, "vmem")],
             [
                 (bits[height - 1].reshape(1), "smem"),
                 (own, "vmem"),
                 (partner, "vmem"),
-                (node_inverse, "hbm"),
-                (node_basis, "hbm"),
+                (inverse, "vmem"),
+                (basis, "vmem"),
             ],
-            [inverse_shape, shape(node_basis.shape[2:], BF16), whole, 3],
+            [whole, 1],
             vmem=12,
         )
         sols.append(sol)
         coefs.append(own)
     partner = partner_of(own, levels - 1)
+    inverse, lift, *sols = load(
+        own, (node_inverse, node_lift, *sols), ((0, levels - 1), 0) + (slice(None),) * (levels - 1)
+    )
     mine, other = call(
         descent_kernel,
         [(half, "vmem"), (half, "vmem")],
-        [(jnp.stack(bits), "smem"), (own, "vmem"), (partner, "vmem"), (node_inverse, "hbm"), (node_lift, "hbm")]
-        + [(sol, "hbm") for sol in sols]
+        [(jnp.stack(bits), "smem"), (own, "vmem"), (partner, "vmem"), (inverse, "vmem"), (lift, "vmem")]
+        + [(sol, "vmem") for sol in sols]
         + [(coef, "vmem") for coef in coefs],
-        [
-            inverse_shape,
-            shape(node_lift.shape[1:], BF16),
-            shape((levels - 1,) + whole.shape),
-            2 * levels - 1,
-        ],
         vmem=16,
     )
     other = partner_of(other, 0)

time: 132 us -> 123 us (0.932)
  waiting for transfers between devices: 49.3 us -> 40 us
  Pallas kernels: 34.8 us -> 37.3 us
    ppermute x6, waiting for transfers between devices: 20.4 us -> 13.8 us  [from_partner(): lax.ppermute(shard, axis, [(i, i ^ 1 << apart) for i in range(lax.axis_si...]
    all_to_all x1, waiting for transfers between devices: 28.9 us -> 26.2 us  [exchange(): lax.all_to_all(blocks, ('row', 'col'), split_axis=0, concat_axis=0, tiled...]
    pallas_call x9 -> x15, Pallas kernels: 34.8 us -> 37.3 us  [call(): pl.pallas_call(kernel, out_shape=[pltpu.HBM(out.shape, out.dtype) if spac...]
  transfers between devices with their start and end apart: 7 -> 7, of which waited for: 7 -> 6; matrix products, arithmetic and copies ran while one was open for 0% -> 0% of each run, Pallas kernels for 0% -> 7%
where the time goes in v3:
time: 123 us
  waiting for transfers between devices  40 us (33%)
  Pallas kernels  37.3 us (30%)
  blocking collectives  32.3 us (26%)
  starting transfers between devices  12.2 us (10%)
    pallas_call x15, Pallas kernels, call(): pl.pallas_call(kernel, out_shape=[pltpu.HBM(out.shape, out.dtype) if spac...  37.3 us
    all_to_all x1, blocking collectives, exchange(): lax.all_to_all(blocks, ('row', 'col'), split_axis=0, concat_axis=0, tiled...  32.3 us
    all_to_all x1, waiting for transfers between devices, exchange(): lax.all_to_all(blocks, ('row', 'col'), split_axis=0, concat_axis=0, tiled...  26.2 us
    ppermute x6, waiting for transfers between devices, from_partner(): lax.ppermute(shard, axis, [(i, i ^ 1 << apart) for i in range(lax.axis_si...  13.8 us
    all_to_all x1, starting transfers between devices, exchange(): lax.all_to_all(blocks, ('row', 'col'), split_axis=0, concat_axis=0, tiled...  7.48 us
    ppermute x6, starting transfers between devices, from_partner(): lax.ppermute(shard, axis, [(i, i ^ 1 << apart) for i in range(lax.axis_si...  4.68 us
  transfers between devices with their start and end apart: 7, of which 6 were waited for; matrix products, arithmetic and copies ran while one was open for 0% of the time, Pallas kernels for 7%

profile of v3, /device:TPU:0, one launch (start us, length us, event | category | flops | bytes accessed | tf_op | source)
XLA Modules:
  0.0 122.8 jit_solution(12781317746284753465)
XLA Ops:
  0.0 0.0 copy-start
  0.0 0.7 copy-done
  0.7 4.0 %shard_map.82 = (bf16[32,136,128]{2,1,0:T(8,128)(2,1)}, s32[1,1024]{1,0:T(1,128)S(1)}) custom-call(s32[1]{0:T(128)} %bitcast.5.me_ref, s32[1,1024]{1,0:T(1,128)S(1)} %bitcast.8, bf16[1024,256]{1,0:T(8,128)(2,1)} %rows_hbm.1), custom_call_target="tpu_custom_call" | custom-call | tf_op jit(solution)/shard_map/pallas_call | solution.py:297
  4.7 7.5 %all-to-all-start = ((bf16[32,136,128]{2,1,0:T(8,128)(2,1)}), bf16[32,136,128]{2,1,0:T(8,128)(2,1)S(1)}, u32[]{:S(2)}, u32[]{:S(2)}) async-start(bf16[32,136,128]{2,1,0:T(8,128)(2,1)} %get-tuple-element.35), calls=%async_computation | async-start | bytes 2228224 | tf_op jit(solution)/shard_map/all_to_all | solution.py:347
  12.2 1.2 %shard_map.83.basis_ref = bf16[2,1024,256]{2,1,0:T(8,128)(2,1)S(1)} custom-call(s32[1,1024]{1,0:T(1,128)S(1)} %get-tuple-element.36.after_ref.slot_ref, bf16[1,2,1024,256]{3,2,1,0:T(8,128)(2,1)} %refs_0_.6), custom_call_target="tpu_custom_call" | custom-call | tf_op jit(solution)/shard_map/pallas_call | solution.py:297
  13.4 26.2 %all-to-all-done.got_ref = bf16[32,136,128]{2,1,0:T(8,128)(2,1)S(1)} async-done(((bf16[32,136,128]{2,1,0:T(8,128)(2,1)}), bf16[32,136,128]{2,1,0:T(8,128)(2,1)S(1)}, u32[]{:S(2)}, u32[]{:S(2)}) %all-to-all-start) | async-done | bytes 1114144 | tf_op jit(solution)/shard_map/all_to_all | solution.py:347
  39.7 5.6 %shard_map.84 = (f32[1024,256]{1,0:T(8,128)}, f32[256,128]{1,0:T(8,128)S(1)}, f32[256,128]{1,0:T(8,128)S(1)}, f32[16,128]{1,0:T(8,128)S(1)}) custom-call(s32[1]{0:T(128)} %bitcast.bit_ref, bf16[32,136,128]{2,1,0:T(8,128)(2,1)S(1)} %all-to-all-done.got_ref, bf16[1,2,1024,1024]{3,2,1,0:T(8,128)(2,1)} %inverse_hbm.1, bf16[2,1024,256]{2,1,0:T(8,128)(2,1)S(1)} %shard_map.83.basis_ref), custom_call_target="tpu_custom_call" | custom-call | tf_op jit(solution)/shard_map/pallas_call | solution.py:297
  45.3 0.1 collective-permute-start
  45.4 1.4 %shard_map.85 = (bf16[2,512,512]{2,1,0:T(8,128)(2,1)S(1)}, bf16[2,512,256]{2,1,0:T(8,128)(2,1)S(1)}) custom-call(f32[256,128]{1,0:T(8,128)S(1)} %get-tuple-element.37.after_ref.own_ref, bf16[1,5,2,512,512]{4,3,2,1,0:T(8,128)(2,1)} %refs_0_.11, bf16[1,4,2,512,256]{4,3,2,1,0:T(8,128)(2,1)} %refs_1_.8), custom_call_target="tpu_custom_call" | custom-call | tf_op jit(solution)/shard_map/pallas_call | solution.py:297
  46.8 0.0 collective-permute-done.partner_ref
  46.8 1.5 %shard_map.86 = (f32[512,128]{1,0:T(8,128)}, f32[256,128]{1,0:T(8,128)S(1)}) custom-call(s32[1]{0:T(128)} %bitcast.bit_ref, f32[256,128]{1,0:T(8,128)S(1)} %get-tuple-element.37.after_ref.own_ref, f32[256,128]{1,0:T(8,128)S(1)} %collective-permute-done.partner_ref, bf16[2,512,512]{2,1,0:T(8,128)(2,1)S(1)} %get-tuple-element.39.inverse_ref, ...), custom_call_target="tpu_custom_call" | custom-call | tf_op jit(solution)/shard_map/pallas_call | solution.py:297
  48.3 1.5 %collective-permute-start.1 = (f32[256,128]{1,0:T(8,128)S(1)}, f32[256,128]{1,0:T(8,128)S(1)}, u32[]{:S(2)}, u32[]{:S(2)}) collective-permute-start(f32[256,128]{1,0:T(8,128)S(1)} %get-tuple-element.41.after_ref.own_ref.refs_4_), channel_id=1, source_target_pairs={{0,2},{1,3},{2,0},{3,1},{4,6},{5,7},{6,4},{7,5},{8,10},{9,11},{10,... | collective-permute-start | bytes 393224 | tf_op jit(solution)/shard_map/ppermute | solution.py:321
  49.8 1.4 %shard_map.87 = (bf16[2,512,512]{2,1,0:T(8,128)(2,1)S(1)}, bf16[2,512,256]{2,1,0:T(8,128)(2,1)S(1)}) custom-call(f32[256,128]{1,0:T(8,128)S(1)} %get-tuple-element.41.after_ref.own_ref.refs_4_, bf16[1,5,2,512,512]{4,3,2,1,0:T(8,128)(2,1)} %refs_0_.11, bf16[1,4,2,512,256]{4,3,2,1,0:T(8,128)(2,1)} %refs_1_.8), custom_call_target="tpu_custom_call" | custom-call | tf_op jit(solution)/shard_map/pallas_call | solution.py:297
  51.2 3.0 %collective-permute-done.1.partner_ref = f32[256,128]{1,0:T(8,128)S(1)} collective-permute-done((f32[256,128]{1,0:T(8,128)S(1)}, f32[256,128]{1,0:T(8,128)S(1)}, u32[]{:S(2)}, u32[]{:S(2)}) %collective-permute-start.1) | collective-permute-done | bytes 131104 | tf_op jit(solution)/shard_map/ppermute | solution.py:321
  54.2 1.4 %shard_map.88 = (f32[512,128]{1,0:T(8,128)}, f32[256,128]{1,0:T(8,128)S(1)}) custom-call(s32[1]{0:T(128)} %bitcast.1.bit_ref, f32[256,128]{1,0:T(8,128)S(1)} %get-tuple-element.41.after_ref.own_ref.refs_4_, f32[256,128]{1,0:T(8,128)S(1)} %collective-permute-done.1.partner_ref, bf16[2,512,512]{2,1,0:T(8,128)(2,1)S(1)} %get-tuple-element.42.inverse_ref, ...), custom_call_target="tpu_custom_call" | custom-call | tf_op jit(solution)/shard_map/pallas_call | solution.py:297
  55.7 1.5 %collective-permute-start.2 = (f32[256,128]{1,0:T(8,128)S(1)}, f32[256,128]{1,0:T(8,128)S(1)}, u32[]{:S(2)}, u32[]{:S(2)}) collective-permute-start(f32[256,128]{1,0:T(8,128)S(1)} %get-tuple-element.44.after_ref.own_ref.refs_5_), channel_id=1, source_target_pairs={{0,4},{4,0},{8,12},{12,8},{16,20},{20,16},{24,28},{28,24},{1,5},{5... | collective-permute-start | bytes 393224 | tf_op jit(solution)/shard_map/ppermute | solution.py:321
  57.2 1.4 %shard_map.89 = (bf16[2,512,512]{2,1,0:T(8,128)(2,1)S(1)}, bf16[2,512,256]{2,1,0:T(8,128)(2,1)S(1)}) custom-call(f32[256,128]{1,0:T(8,128)S(1)} %get-tuple-element.44.after_ref.own_ref.refs_5_, bf16[1,5,2,512,512]{4,3,2,1,0:T(8,128)(2,1)} %refs_0_.11, bf16[1,4,2,512,256]{4,3,2,1,0:T(8,128)(2,1)} %refs_1_.8), custom_call_target="tpu_custom_call" | custom-call | tf_op jit(solution)/shard_map/pallas_call | solution.py:297
  58.6 2.3 %collective-permute-done.2.partner_ref = f32[256,128]{1,0:T(8,128)S(1)} collective-permute-done((f32[256,128]{1,0:T(8,128)S(1)}, f32[256,128]{1,0:T(8,128)S(1)}, u32[]{:S(2)}, u32[]{:S(2)}) %collective-permute-start.2) | collective-permute-done | bytes 131104 | tf_op jit(solution)/shard_map/ppermute | solution.py:321
  60.9 1.5 %shard_map.90 = (f32[512,128]{1,0:T(8,128)}, f32[256,128]{1,0:T(8,128)S(1)}) custom-call(s32[1]{0:T(128)} %bitcast.2.bit_ref, f32[256,128]{1,0:T(8,128)S(1)} %get-tuple-element.44.after_ref.own_ref.refs_5_, f32[256,128]{1,0:T(8,128)S(1)} %collective-permute-done.2.partner_ref, bf16[2,512,512]{2,1,0:T(8,128)(2,1)S(1)} %get-tuple-element.45.inverse_ref, ...), custom_call_target="tpu_custom_call" | custom-call | tf_op jit(solution)/shard_map/pallas_call | solution.py:297
  62.3 0.5 collective-permute-start.3
  62.9 1.4 %shard_map.91 = (bf16[2,512,512]{2,1,0:T(8,128)(2,1)S(1)}, bf16[2,512,256]{2,1,0:T(8,128)(2,1)S(1)}) custom-call(f32[256,128]{1,0:T(8,128)S(1)} %get-tuple-element.47.after_ref.own_ref.refs_6_, bf16[1,5,2,512,512]{4,3,2,1,0:T(8,128)(2,1)} %refs_0_.11, bf16[1,4,2,512,256]{4,3,2,1,0:T(8,128)(2,1)} %refs_1_.8), custom_call_target="tpu_custom_call" | custom-call | tf_op jit(solution)/shard_map/pallas_call | solution.py:297
  64.2 3.1 %collective-permute-done.3.partner_ref = f32[256,128]{1,0:T(8,128)S(1)} collective-permute-done((f32[256,128]{1,0:T(8,128)S(1)}, f32[256,128]{1,0:T(8,128)S(1)}, u32[]{:S(2)}, u32[]{:S(2)}) %collective-permute-start.3) | collective-permute-done | bytes 131104 | tf_op jit(solution)/shard_map/ppermute | solution.py:321
  67.4 1.4 %shard_map.92 = (f32[512,128]{1,0:T(8,128)}, f32[256,128]{1,0:T(8,128)S(1)}) custom-call(s32[1]{0:T(128)} %bitcast.3.bit_ref, f32[256,128]{1,0:T(8,128)S(1)} %get-tuple-element.47.after_ref.own_ref.refs_6_, f32[256,128]{1,0:T(8,128)S(1)} %collective-permute-done.3.partner_ref, bf16[2,512,512]{2,1,0:T(8,128)(2,1)S(1)} %get-tuple-element.48.inverse_ref, ...), custom_call_target="tpu_custom_call" | custom-call | tf_op jit(solution)/shard_map/pallas_call | solution.py:297
  68.8 0.9 collective-permute-start.4
  69.7 0.1 stack.20.bits_ref
  69.8 2.2 %shard_map.93 = (bf16[2,512,512]{2,1,0:T(8,128)(2,1)S(1)}, bf16[4,2,512,256]{3,2,1,0:T(8,128)(2,1)S(1)}, f32[512,128]{1,0:T(8,128)S(1)}, f32[512,128]{1,0:T(8,12...) custom-call(f32[256,128]{1,0:T(8,128)S(1)} %get-tuple-element.50.after_ref.own_ref.refs_7_, ...), custom_call_target="tpu_custom_call" | custom-call | tf_op jit(solution)/shard_map/pallas_call | solution.py:297
  72.0 4.1 %collective-permute-done.4.partner_ref = f32[256,128]{1,0:T(8,128)S(1)} collective-permute-done((f32[256,128]{1,0:T(8,128)S(1)}, f32[256,128]{1,0:T(8,128)S(1)}, u32[]{:S(2)}, u32[]{:S(2)}) %collective-permute-start.4) | collective-permute-done | bytes 131104 | tf_op jit(solution)/shard_map/ppermute | solution.py:321
  76.1 3.2 %shard_map.94 = (f32[256,128]{1,0:T(8,128)S(1)}, f32[256,128]{1,0:T(8,128)S(1)}) custom-call(s32[5]{0:T(128)S(1)} %stack.20.bits_ref, f32[256,128]{1,0:T(8,128)S(1)} %get-tuple-element.50.after_ref.own_ref.refs_7_, f32[256,128]{1,0:T(8,128)S(1)} %collective-permute-done.4.partner_ref, bf16[2,512,512]{2,1,0:T(8,128)(2,1)S(1)} %get-tuple-element.55.inverse_ref, ...), custom_call_target="tpu_custom_call" | custom-call | tf_op jit(solution)/shard_map/pallas_call | solution.py:297
  79.2 0.1 collective-permute-start.5
  79.3 1.3 %collective-permute-done.5.others_ref = f32[256,128]{1,0:T(8,128)S(1)} collective-permute-done((f32[256,128]{1,0:T(8,128)S(1)}, f32[256,128]{1,0:T(8,128)S(1)}, u32[]{:S(2)}, u32[]{:S(2)}) %collective-permute-start.5) | collective-permute-done | bytes 131104 | tf_op jit(solution)/shard_map/ppermute | solution.py:321
  80.6 6.0 %shard_map.95 = s16[32,136,128]{2,1,0:T(8,128)(2,1)S(1)} custom-call(s32[1]{0:T(128)} %bitcast.bit_ref, f32[256,128]{1,0:T(8,128)S(1)} %get-tuple-element.61.mine_ref, f32[256,128]{1,0:T(8,128)S(1)} %collective-permute-done.5.others_ref, f32[256,128]{1,0:T(8,128)S(1)} %get-tuple-element.37.after_ref.own_ref, f32[256,128]{1,0:T(8,128)S(1)} %get-tuple-element.38.other_ref, ...), custom_call_target="tpu_custom_call" | custom-call | tf_op jit(solution)/shard_map/pallas_call | solution.py:297
  86.6 32.3 %all_to_all.10.got_ref = s16[32,136,128]{2,1,0:T(8,128)(2,1)S(1)} all-to-all(s16[32,136,128]{2,1,0:T(8,128)(2,1)S(1)} %shard_map.95), channel_id=1, replica_groups=mesh['row'=8,'col'=4] {'row','col'}, dimensions={0} | all-to-all | bytes 2228224 | tf_op jit(solution)/shard_map/all_to_all | solution.py:347
  119.0 3.8 %shard_map.96 = f32[1024,256]{1,0:T(8,128)} custom-call(s16[32,136,128]{2,1,0:T(8,128)(2,1)S(1)} %all_to_all.10.got_ref, s32[1,1024]{1,0:T(1,128)S(1)} %get-tuple-element.36.after_ref.slot_ref), custom_call_target="tpu_custom_call" | custom-call | tf_op jit(solution)/shard_map/pallas_call | solution.py:297
Async XLA Ops:
  0.0 0.7 copy-start
  4.7 35.0 %all-to-all-start = ((bf16[32,136,128]{2,1,0:T(8,128)(2,1)}), bf16[32,136,128]{2,1,0:T(8,128)(2,1)S(1)}, u32[]{:S(2)}, u32[]{:S(2)}) async-start(bf16[32,136,128]{2,1,0:T(8,128)(2,1)} %get-tuple-element.35), calls=%async_computation | async-start | bytes 2228224 | tf_op jit(solution)/shard_map/all_to_all | solution.py:347
  45.3 1.5 %collective-permute-start = (f32[256,128]{1,0:T(8,128)S(1)}, f32[256,128]{1,0:T(8,128)S(1)}, u32[]{:S(2)}, u32[]{:S(2)}) collective-permute-start(f32[256,128]{1,0:T(8,128)S(1)} %get-tuple-element.38.other_ref), channel_id=1, source_target_pairs={{0,1},{1,0},{2,3},{3,2},{4,5},{5,4},{6,7},{7,6},{8,9},{9,8},{10,11... | collective-permute-start | bytes 393224 | tf_op jit(solution)/shard_map/ppermute | solution.py:321
  48.3 6.0 %collective-permute-start.1 = (f32[256,128]{1,0:T(8,128)S(1)}, f32[256,128]{1,0:T(8,128)S(1)}, u32[]{:S(2)}, u32[]{:S(2)}) collective-permute-start(f32[256,128]{1,0:T(8,128)S(1)} %get-tuple-element.41.after_ref.own_ref.refs_4_), channel_id=1, source_target_pairs={{0,2},{1,3},{2,0},{3,1},{4,6},{5,7},{6,4},{7,5},{8,10},{9,11},{10,... | collective-permute-start | bytes 393224 | tf_op jit(solution)/shard_map/ppermute | solution.py:321
  55.7 5.2 %collective-permute-start.2 = (f32[256,128]{1,0:T(8,128)S(1)}, f32[256,128]{1,0:T(8,128)S(1)}, u32[]{:S(2)}, u32[]{:S(2)}) collective-permute-start(f32[256,128]{1,0:T(8,128)S(1)} %get-tuple-element.44.after_ref.own_ref.refs_5_), channel_id=1, source_target_pairs={{0,4},{4,0},{8,12},{12,8},{16,20},{20,16},{24,28},{28,24},{1,5},{5... | collective-permute-start | bytes 393224 | tf_op jit(solution)/shard_map/ppermute | solution.py:321
  62.3 5.0 %collective-permute-start.3 = (f32[256,128]{1,0:T(8,128)S(1)}, f32[256,128]{1,0:T(8,128)S(1)}, u32[]{:S(2)}, u32[]{:S(2)}) collective-permute-start(f32[256,128]{1,0:T(8,128)S(1)} %get-tuple-element.47.after_ref.own_ref.refs_6_), channel_id=1, source_target_pairs={{0,8},{4,12},{8,0},{12,4},{16,24},{20,28},{24,16},{28,20},{1,9},{5... | collective-permute-start | bytes 393224 | tf_op jit(solution)/shard_map/ppermute | solution.py:321
  68.8 7.3 %collective-permute-start.4 = (f32[256,128]{1,0:T(8,128)S(1)}, f32[256,128]{1,0:T(8,128)S(1)}, u32[]{:S(2)}, u32[]{:S(2)}) collective-permute-start(f32[256,128]{1,0:T(8,128)S(1)} %get-tuple-element.50.after_ref.own_ref.refs_7_), channel_id=1, source_target_pairs={{0,16},{4,20},{8,24},{12,28},{16,0},{20,4},{24,8},{28,12},{1,17},{... | collective-permute-start | bytes 393224 | tf_op jit(solution)/shard_map/ppermute | solution.py:321
  79.2 1.4 %collective-permute-start.5 = (f32[256,128]{1,0:T(8,128)S(1)}, f32[256,128]{1,0:T(8,128)S(1)}, u32[]{:S(2)}, u32[]{:S(2)}) collective-permute-start(f32[256,128]{1,0:T(8,128)S(1)} %get-tuple-element.62), channel_id=1, source_target_pairs={{0,1},{1,0},{2,3},{3,2},{4,5},{5,4},{6,7},{7,6},{8,9},{9,8},{10,11... | collective-permute-start | bytes 393224 | tf_op jit(solution)/shard_map/ppermute | solution.py:321

commit v4 on v3

--- a/solution.py
+++ b/solution.py
@@ -91,24 +91,59 @@
     return copy
 
 
-def pack_kernel(me_ref, order_ref, rows_hbm, send_ref, slot_ref, rows_ref, sem, *, devices, capacity):
-    rows_copy = fetch(rows_hbm, rows_ref, sem.at[0])
+def wide_one_hot(index, blocks):
+    turned = jnp.transpose(index)
+    lane = iota((LANES, LANES), 1).astype(F32)
+    parts = []
+    for k in range(index.shape[0]):
+        entry = turned[:, k : k + 1]
+        block = jnp.floor(entry * (1.0 / LANES))
+        parts.append(jnp.where(lane == entry - block * LANES, block, -1.0))
+    chosen = jnp.concatenate(parts, axis=0).astype(BF16)
+    one, zero = jnp.ones((), BF16), jnp.zeros((), BF16)
+    return jnp.concatenate(
+        [jnp.where(chosen == jnp.array(g, BF16), one, zero) for g in range(blocks)], axis=1
+    )
+
+
+def row_blocks(x):
+    return jnp.concatenate([x[:, at : at + LANES] for at in range(0, x.shape[1], LANES)], axis=0)
+
+
+def ranks(hits):
+    rows, width = hits.shape
+    upper = (iota((LANES, LANES), 0) < iota((LANES, LANES), 1)).astype(F32).astype(BF16)
+    pieces = jnp.concatenate(
+        [hits[:, at : at + LANES] for at in range(0, width, LANES)], axis=0
+    ).astype(BF16)
+    inside = matmul(pieces, upper)
+    totals = matmul(pieces, jnp.ones((LANES, LANES), BF16))
+    ahead = jnp.zeros((rows, LANES), F32)
+    parts = []
+    for k in range(width // LANES):
+        parts.append(inside[k * rows : (k + 1) * rows] + ahead)
+        ahead = ahead + totals[k * rows : (k + 1) * rows]
+    return jnp.concatenate(parts, axis=1)
+
+
+def pack_kernel(
+    me_ref, order_hbm, rows_hbm, send_ref, slot_ref, order_ref, rows_ref, sem, *, devices, capacity
+):
+    order_copy = fetch(order_hbm, order_ref, sem.at[0])
+    rows_copy = fetch(rows_hbm, rows_ref, sem.at[1])
     leaf_rows = rows_ref.shape[0]
+    order_copy.wait()
     order = order_ref[...]
     target = order // leaf_rows
     position = order - target * leaf_rows
     hits = (iota((devices, leaf_rows), 0) == target).astype(F32)
-    upper = (iota((leaf_rows, leaf_rows), 0) < iota((leaf_rows, leaf_rows), 1)).astype(F32)
-    before = matmul(hits.astype(BF16), upper.astype(BF16))
-    rank = jnp.sum(hits * before, axis=0, keepdims=True).astype(jnp.int32)
-    slot = target * capacity + rank
-    slot_ref[...] = slot
+    rank = jnp.sum(hits * ranks(hits), axis=0, keepdims=True).astype(jnp.int32)
+    slot_ref[...] = row_blocks((target * capacity + rank).astype(F32))
     group = LANES // capacity
     lane = rank + lax.rem(me_ref[0], group) * capacity
-    code = position + 1
-    high = code // CODE_BASE
-    low = code - high * CODE_BASE
-    codes = jnp.concatenate([hits * high.astype(F32), hits * low.astype(F32)], axis=0)
+    high = position // CODE_BASE
+    low = position - high * CODE_BASE
+    codes = jnp.concatenate([hits * (high + 1).astype(F32), hits * low.astype(F32)], axis=0)
     places = (iota((LANES, leaf_rows), 0) == lane).astype(F32).astype(BF16)
     spread = matmul_nt(codes.astype(BF16), places)
     extra = (devices, EXTRA, LANES)
@@ -117,7 +152,9 @@
         jnp.broadcast_to(spread[:devices].reshape(devices, 1, LANES), extra),
         jnp.broadcast_to(spread[devices:].reshape(devices, 1, LANES), extra),
     ).astype(BF16)
-    chosen = (iota((devices * capacity, leaf_rows), 0) == slot).astype(F32).astype(BF16)
+    in_slot = (iota((capacity, leaf_rows), 0) == rank).astype(F32).astype(BF16)
+    hits = hits.astype(BF16)
+    chosen = jnp.concatenate([in_slot * hits[t : t + 1, :] for t in range(devices)], axis=0)
     rows_copy.wait()
     rows = rows_ref[...].astype(F32)
     first, second = swapped(rows[:, :LANES], rows[:, LANES:])
@@ -127,22 +164,35 @@
     send_ref[:, capacity : 2 * capacity, :] = sent[:, LANES:].reshape(devices, capacity, LANES)
 
 
-def positions(got_ref, devices, capacity):
+def codes_of(got_ref, devices, capacity):
     group = LANES // capacity
     extra = got_ref[:, 2 * capacity :, :].astype(F32)
-    code = extra[:, 0, :] * CODE_BASE + extra[:, EXTRA // 2, :]
-    return jnp.sum(code.reshape(devices // group, group, LANES), axis=1) - 1.0
-
-
-def load_kernel(after_ref, *refs, picks):
+    grouped = (devices // group, group, LANES)
+    high = jnp.sum(extra[:, 0, :].reshape(grouped), axis=1)
+    low = jnp.sum(extra[:, EXTRA // 2, :].reshape(grouped), axis=1)
+    return high, low
+
+
+def load_kernel(after_ref, *refs, picks, turned, stores):
     count = len(picks)
-    sources, targets, sem = refs[:count], refs[count : 2 * count], refs[2 * count]
+    sources, stored = refs[:count], refs[count : count + stores]
+    targets = refs[count + stores : 2 * count + stores]
+    kept = refs[2 * count + stores : 2 * count + 2 * stores]
+    scratch, sem = refs[2 * count + 2 * stores : -1], refs[-1]
+    plain = count - turned
+    landing = targets[:plain] + scratch
     copies = [
         fetch(source.at[pick], target, sem.at[k])
-        for k, (source, target, pick) in enumerate(zip(sources, targets, picks))
+        for k, (source, target, pick) in enumerate(zip(sources, landing, picks))
     ]
-    for copy in copies:
-        copy.wait()
+    copies += [fetch(stored[k], kept[k], sem.at[count + k]) for k in range(stores)]
+    for k in range(turned):
+        copies[plain + k].wait()
+        for part in range(2):
+            targets[plain + k][part] = jnp.transpose(scratch[k][part])
+    for k, copy in enumerate(copies):
+        if not plain <= k < count:
+            copy.wait()
 
 
 def leaf_kernel(
@@ -151,15 +201,18 @@
 ):
     copies = [fetch(inverse_hbm.at[0, k], inverse_ref.at[k], sem.at[1 + k]) for k in range(2)]
     leaf_rows = sol_ref.shape[0]
-    place = positions(got_ref, devices, capacity)
-    place_ref[...] = place
-    where_to = iota((leaf_rows, LANES), 0).astype(F32)
+    high, low = codes_of(got_ref, devices, capacity)
+    place_ref[...] = (high - 1.0) * CODE_BASE + low
+    code = iota((CODE_BASE, LANES), 0).astype(F32)
+    groups = high.shape[0]
+    is_low = jnp.concatenate(
+        [(code == low[k : k + 1]).astype(F32) for k in range(groups)], axis=1
+    ).astype(BF16)
+    is_high = jnp.concatenate(
+        [(code == high[k : k + 1] - 1.0).astype(F32) for k in range(groups)], axis=1
+    ).astype(BF16)
     chosen = jnp.concatenate(
-        [
-            (where_to == place[k : k + 1, :]).astype(F32).astype(BF16)
-            for k in range(place.shape[0])
-        ],
-        axis=1,
+        [is_low * is_high[h : h + 1, :] for h in range(leaf_rows // CODE_BASE)], axis=0
     )
     slots = devices * capacity
     got = jnp.concatenate(
@@ -177,7 +230,7 @@
     sol = sol + matmul(inverse_ref[1], turned.astype(BF16))
     sol_ref[...] = sol
     sol_copy = fetch(sol_ref, sol_hbm, sem.at[0])
-    coef = apply_transposed(basis_ref[0], basis_ref[1], sol)
+    coef = apply_complex(basis_ref[0], basis_ref[1], sol)
     first, second = coef[:, :LANES], coef[:, LANES:]
     odd = bit_ref[0] == 1
     own_ref[...] = jnp.where(odd, second, first)
@@ -192,20 +245,11 @@
     )
 
 
-def node_kernel(
-    bit_ref, own_ref, partner_ref, inverse_ref, basis_ref, sol_hbm, coef_ref, sol_ref, sem
-):
+def node_kernel(bit_ref, own_ref, partner_ref, inverse_ref, basis_ref, sol_ref, coef_ref):
     rhs = node_rhs(bit_ref[0], own_ref[...], partner_ref[...])
     sol = apply_complex(inverse_ref[0], inverse_ref[1], rhs)
     sol_ref[...] = sol
-    sol_copy = fetch(sol_ref, sol_hbm, sem.at[0])
-    coef_ref[...] = apply_transposed(basis_ref[0], basis_ref[1], sol)
-    sol_copy.wait()
-
-
-def half_of(bit, x):
-    rank = x.shape[0] // 2
-    return jnp.where(bit == 1, x[rank:], x[:rank])
+    coef_ref[...] = apply_complex(basis_ref[0], basis_ref[1], sol)
 
 
 def descent_kernel(bits_ref, own_ref, partner_ref, inverse_ref, lift_ref, *refs):
@@ -213,13 +257,23 @@
     below = levels - 1
     sols, coefs = refs[:below], refs[below : 2 * below]
     mine_ref, other_ref = refs[2 * below :]
+    rank = own_ref.shape[0]
+
+    def half(bit):
+        return pl.ds(pl.multiple_of(bit * rank, rank), rank)
+
     rhs = node_rhs(bits_ref[below], own_ref[...], partner_ref[...])
-    down = apply_complex(inverse_ref[0], inverse_ref[1], rhs)
-    for k in range(below - 1, -1, -1):
-        gap = coefs[k][...] - half_of(bits_ref[k + 1], down)
-        down = sols[k][...] - apply_complex(lift_ref[k, 0], lift_ref[k, 1], gap)
-    mine_ref[...] = half_of(bits_ref[0], down)
-    other_ref[...] = half_of(1 - bits_ref[0], down)
+    rows = half(bits_ref[below])
+    down = apply_complex(inverse_ref[0, rows, :], inverse_ref[1, rows, :], rhs)
+    for k in range(below - 1, 0, -1):
+        gap = coefs[k][...] - down
+        rows = half(bits_ref[k])
+        down = sols[k][rows, :] - apply_complex(lift_ref[k, 0, rows, :], lift_ref[k, 1, rows, :], gap)
+    gap = coefs[0][...] - down
+    down = sols[0][...] - apply_complex(lift_ref[0, 0], lift_ref[0, 1], gap)
+    swap = bits_ref[0] == 1
+    mine_ref[...] = jnp.where(swap, down[rank:], down[:rank])
+    other_ref[...] = jnp.where(swap, down[:rank], down[rank:])
 
 
 def finish_kernel(
@@ -229,15 +283,7 @@
     lift_copy = fetch(lift_hbm, lift_ref, sem.at[0])
     sol_copy = fetch(sol_hbm, sol_ref, sem.at[1])
     leaf_rows = sol_ref.shape[0]
-    place = jnp.transpose(place_ref[...])
-    where_from = iota((LANES, leaf_rows), 1).astype(F32)
-    chosen = jnp.concatenate(
-        [
-            (where_from == place[:, k : k + 1]).astype(F32).astype(BF16)
-            for k in range(place.shape[1])
-        ],
-        axis=0,
-    )
+    chosen = wide_one_hot(place_ref[...], leaf_rows // LANES)
     swap = bit_ref[0] == 1
     mine = own_ref[...] - mine_ref[...]
     other = other_ref[...] - others_ref[...]
@@ -279,8 +325,7 @@
         unit = unit_of(extra[:, half * (EXTRA // 2) : half * (EXTRA // 2) + 1, :])
         halves.append((level * unit).reshape(slots, LANES))
     both = two_parts(jnp.concatenate(halves, axis=1))
-    slot = jnp.transpose(jnp.broadcast_to(slot_ref[...].astype(F32), (LANES, leaf_rows)))[:, :1]
-    chosen = (iota((leaf_rows, slots), 1).astype(F32) == slot).astype(F32).astype(BF16)
+    chosen = wide_one_hot(slot_ref[...], slots // LANES)
     result = folded(matmul(chosen, both))
     first, second = swapped(result[:, :LANES], result[:, LANES:])
     out_ref[:, :LANES] = first
@@ -353,22 +398,25 @@
 
     send, slot = call(
         functools.partial(pack_kernel, **sizes),
-        [(shape(block, BF16), "vmem"), (shape((1, leaf_rows), jnp.int32), "vmem")],
-        [(me.reshape(1), "smem"), (tree_order.reshape(1, leaf_rows), "vmem"), (right_sides, "hbm")],
-        [shape(right_sides.shape, BF16), 1],
-    )
-    def load(after, weights, picks):
+        [(shape(block, BF16), "vmem"), (shape((leaf_rows // LANES, LANES)), "vmem")],
+        [(me.reshape(1), "smem"), (tree_order.reshape(1, leaf_rows), "hbm"), (right_sides, "hbm")],
+        [shape((1, leaf_rows), jnp.int32), shape(right_sides.shape, BF16), 2],
+    )
+    def load(after, weights, picks, turned=0, stores=()):
         shapes = [jax.eval_shape(lambda w, pick=pick: w[pick], w) for w, pick in zip(weights, picks)]
+        plain = len(weights) - turned
+        outs = [shape(one.shape, one.dtype) for one in shapes[:plain]]
+        outs += [shape((2, one.shape[2], one.shape[1]), one.dtype) for one in shapes[plain:]]
         return call(
-            functools.partial(load_kernel, picks=picks),
-            [(shape(one.shape, one.dtype), "vmem") for one in shapes],
-            [(after, "any")] + [(weight, "hbm") for weight in weights],
-            [len(weights)],
-            vmem=4,
+            functools.partial(load_kernel, picks=picks, turned=turned, stores=len(stores)),
+            [(out, "vmem") for out in outs] + [(shape(one.shape), "hbm") for one in stores],
+            [(after, "any")] + [(weight, "hbm") for weight in weights] + [(one, "any") for one in stores],
+            [shape(one.shape, one.dtype) for one in shapes[plain:]] + [len(weights) + len(stores)],
+            vmem=6,
         )
 
     got = exchange(send)
-    (leaf_basis,) = load(slot, (leaf_basis,), (0,))
+    (leaf_basis,) = load(slot, (leaf_basis,), (0,), turned=1)
     half = shape((rank, LANES))
     leaf_sol, own, other, place = call(
         functools.partial(leaf_kernel, **sizes),
@@ -383,14 +431,15 @@
     )
     leaf_own, leaf_other = own, other
     whole = shape((2 * rank, LANES))
-    sols, coefs = [], []
+    sols, stored, coefs = [], [], []
     for height in range(1, levels):
         partner = partner_of(other if height == 1 else own, height - 1)
         pick = (0, height - 1)
-        inverse, basis = load(own, (node_inverse, node_basis), (pick, pick))
+        inverse, basis, *kept = load(own, (node_inverse, node_basis), (pick, pick), 1, sols[-1:])
+        stored += kept
         sol, own = call(
             node_kernel,
-            [(whole, "hbm"), (half, "vmem")],
+            [(whole, "vmem"), (half, "vmem")],
             [
                 (bits[height - 1].reshape(1), "smem"),
                 (own, "vmem"),
@@ -398,22 +447,22 @@
                 (inverse, "vmem"),
                 (basis, "vmem"),
             ],
-            [whole, 1],
-            vmem=12,
+            vmem=8,
         )
         sols.append(sol)
         coefs.append(own)
     partner = partner_of(own, levels - 1)
-    inverse, lift, *sols = load(
-        own, (node_inverse, node_lift, *sols), ((0, levels - 1), 0) + (slice(None),) * (levels - 1)
-    )
+    inverse, lift, *stored = load(
+        own, (node_inverse, node_lift, *stored), ((0, levels - 1), 0) + (slice(None),) * len(stored)
+    )
+    sols = stored + sols[-1:]
     mine, other = call(
         descent_kernel,
         [(half, "vmem"), (half, "vmem")],
         [(jnp.stack(bits), "smem"), (own, "vmem"), (partner, "vmem"), (inverse, "vmem"), (lift, "vmem")]
         + [(sol, "vmem") for sol in sols]
         + [(coef, "vmem") for coef in coefs],
-        vmem=16,
+        vmem=8,
     )
     other = partner_of(other, 0)
     (back,) = call(

time: 123 us -> 119 us (0.967)
  Pallas kernels: 37.3 us -> 35.4 us
    pallas_call x15, Pallas kernels: 37.3 us -> 35.4 us  [call(): pl.pallas_call(kernel, out_shape=[pltpu.HBM(out.shape, out.dtype) if spac...]
  transfers between devices with their start and end apart: 7 -> 7, of which waited for: 6 -> 6; matrix products, arithmetic and copies ran while one was open for 0% -> 0% of each run, Pallas kernels for 7% -> 9%
where the time goes in v4:
time: 119 us
  waiting for transfers between devices  39.1 us (33%)
  Pallas kernels  35.4 us (30%)
  blocking collectives  32.3 us (27%)
  starting transfers between devices  12 us (10%)
    pallas_call x15, Pallas kernels, call(): pl.pallas_call(kernel, out_shape=[pltpu.HBM(out.shape, out.dtype) if spac...  35.4 us
    all_to_all x1, blocking collectives, exchange(): lax.all_to_all(blocks, ('row', 'col'), split_axis=0, concat_axis=0, tiled...  32.3 us
    all_to_all x1, waiting for transfers between devices, exchange(): lax.all_to_all(blocks, ('row', 'col'), split_axis=0, concat_axis=0, tiled...  26.1 us
    ppermute x6, waiting for transfers between devices, from_partner(): lax.ppermute(shard, axis, [(i, i ^ 1 << apart) for i in range(lax.axis_si...  13 us
    all_to_all x1, starting transfers between devices, exchange(): lax.all_to_all(blocks, ('row', 'col'), split_axis=0, concat_axis=0, tiled...  7.3 us
    ppermute x6, starting transfers between devices, from_partner(): lax.ppermute(shard, axis, [(i, i ^ 1 << apart) for i in range(lax.axis_si...  4.67 us
  transfers between devices with their start and end apart: 7, of which 6 were waited for; matrix products, arithmetic and copies ran while one was open for 0% of the time, Pallas kernels for 9%

profile of v4, /device:TPU:0, one launch (start us, length us, event | category | flops | bytes accessed | tf_op | source)
XLA Modules:
  0.0 119.0 jit_solution(8062759566143726629)
XLA Ops:
  0.0 3.6 %shard_map.82 = (bf16[32,136,128]{2,1,0:T(8,128)(2,1)}, f32[8,128]{1,0:T(8,128)S(1)}) custom-call(s32[1]{0:T(128)} %bitcast.5.me_ref, s32[1,1024]{1,0:T(1,128)} %bitcast.9, bf16[1024,256]{1,0:T(8,128)(2,1)} %rows_hbm.1), custom_call_target="tpu_custom_call" | custom-call | tf_op jit(solution)/shard_map/pallas_call | solution.py:342
  3.6 7.3 %all-to-all-start = ((bf16[32,136,128]{2,1,0:T(8,128)(2,1)}), bf16[32,136,128]{2,1,0:T(8,128)(2,1)S(1)}, u32[]{:S(2)}, u32[]{:S(2)}) async-start(bf16[32,136,128]{2,1,0:T(8,128)(2,1)} %get-tuple-element.37), calls=%async_computation | async-start | bytes 2228224 | tf_op jit(solution)/shard_map/all_to_all | solution.py:392
  10.9 1.6 %shard_map.83.basis_ref = bf16[2,256,1024]{2,1,0:T(8,128)(2,1)S(1)} custom-call(f32[8,128]{1,0:T(8,128)S(1)} %get-tuple-element.38.after_ref.slot_ref, bf16[1,2,1024,256]{3,2,1,0:T(8,128)(2,1)} %refs_0_.6), custom_call_target="tpu_custom_call" | custom-call | tf_op jit(solution)/shard_map/pallas_call | solution.py:342
  12.5 26.1 %all-to-all-done.got_ref = bf16[32,136,128]{2,1,0:T(8,128)(2,1)S(1)} async-done(((bf16[32,136,128]{2,1,0:T(8,128)(2,1)}), bf16[32,136,128]{2,1,0:T(8,128)(2,1)S(1)}, u32[]{:S(2)}, u32[]{:S(2)}) %all-to-all-start) | async-done | bytes 1114144 | tf_op jit(solution)/shard_map/all_to_all | solution.py:392
  38.5 5.7 %shard_map.84 = (f32[1024,256]{1,0:T(8,128)}, f32[256,128]{1,0:T(8,128)S(1)}, f32[256,128]{1,0:T(8,128)S(1)}, f32[16,128]{1,0:T(8,128)S(1)}) custom-call(s32[1]{0:T(128)} %bitcast.bit_ref, bf16[32,136,128]{2,1,0:T(8,128)(2,1)S(1)} %all-to-all-done.got_ref, bf16[1,2,1024,1024]{3,2,1,0:T(8,128)(2,1)} %inverse_hbm.1, bf16[2,256,1024]{2,1,0:T(8,128)(2,1)S(1)} %shard_map.83.basis_ref), custom_call_target="tpu_custom_call" | custom-call | tf_op jit(solution)/shard_map/pallas_call | solution.py:342
  44.2 0.1 collective-permute-start
  44.3 1.6 %shard_map.85 = (bf16[2,512,512]{2,1,0:T(8,128)(2,1)S(1)}, bf16[2,256,512]{2,1,0:T(8,128)(2,1)S(1)}) custom-call(f32[256,128]{1,0:T(8,128)S(1)} %get-tuple-element.39.after_ref.own_ref, bf16[1,5,2,512,512]{4,3,2,1,0:T(8,128)(2,1)} %refs_0_.11, bf16[1,4,2,512,256]{4,3,2,1,0:T(8,128)(2,1)} %refs_1_.8), custom_call_target="tpu_custom_call" | custom-call | tf_op jit(solution)/shard_map/pallas_call | solution.py:342
  45.9 0.0 collective-permute-done.partner_ref
  45.9 1.0 shard_map.86
  46.9 1.5 %collective-permute-start.1 = (f32[256,128]{1,0:T(8,128)S(1)}, f32[256,128]{1,0:T(8,128)S(1)}, u32[]{:S(2)}, u32[]{:S(2)}) collective-permute-start(f32[256,128]{1,0:T(8,128)S(1)} %get-tuple-element.43.after_ref.own_ref.refs_4_), channel_id=1, source_target_pairs={{0,2},{1,3},{2,0},{3,1},{4,6},{5,7},{6,4},{7,5},{8,10},{9,11},{10,... | collective-permute-start | bytes 393224 | tf_op jit(solution)/shard_map/ppermute | solution.py:366
  48.4 1.7 %shard_map.87 = (bf16[2,512,512]{2,1,0:T(8,128)(2,1)S(1)}, bf16[2,256,512]{2,1,0:T(8,128)(2,1)S(1)}, f32[512,128]{1,0:T(8,128)}) custom-call(f32[256,128]{1,0:T(8,128)S(1)} %get-tuple-element.43.after_ref.own_ref.refs_4_, bf16[1,5,2,512,512]{4,3,2,1,0:T(8,128)(2,1)} %refs_0_.11, bf16[1,4,2,512,256]{4,3,2,1,0:T(8,128)(2,1)} %refs_1_.8, ...), custom_call_target="tpu_custom_call" | custom-call | tf_op jit(solution)/shard_map/pallas_call | solution.py:342
  50.1 2.8 %collective-permute-done.1.partner_ref = f32[256,128]{1,0:T(8,128)S(1)} collective-permute-done((f32[256,128]{1,0:T(8,128)S(1)}, f32[256,128]{1,0:T(8,128)S(1)}, u32[]{:S(2)}, u32[]{:S(2)}) %collective-permute-start.1) | collective-permute-done | bytes 131104 | tf_op jit(solution)/shard_map/ppermute | solution.py:366
  52.9 1.0 shard_map.88
  53.9 1.5 %collective-permute-start.2 = (f32[256,128]{1,0:T(8,128)S(1)}, f32[256,128]{1,0:T(8,128)S(1)}, u32[]{:S(2)}, u32[]{:S(2)}) collective-permute-start(f32[256,128]{1,0:T(8,128)S(1)} %get-tuple-element.47.after_ref.own_ref.refs_5_), channel_id=1, source_target_pairs={{0,4},{4,0},{8,12},{12,8},{16,20},{20,16},{24,28},{28,24},{1,5},{5... | collective-permute-start | bytes 393224 | tf_op jit(solution)/shard_map/ppermute | solution.py:366
  55.4 1.7 %shard_map.89 = (bf16[2,512,512]{2,1,0:T(8,128)(2,1)S(1)}, bf16[2,256,512]{2,1,0:T(8,128)(2,1)S(1)}, f32[512,128]{1,0:T(8,128)}) custom-call(f32[256,128]{1,0:T(8,128)S(1)} %get-tuple-element.47.after_ref.own_ref.refs_5_, bf16[1,5,2,512,512]{4,3,2,1,0:T(8,128)(2,1)} %refs_0_.11, bf16[1,4,2,512,256]{4,3,2,1,0:T(8,128)(2,1)} %refs_1_.8, ...), custom_call_target="tpu_custom_call" | custom-call | tf_op jit(solution)/shard_map/pallas_call | solution.py:342
  57.1 2.0 %collective-permute-done.2.partner_ref = f32[256,128]{1,0:T(8,128)S(1)} collective-permute-done((f32[256,128]{1,0:T(8,128)S(1)}, f32[256,128]{1,0:T(8,128)S(1)}, u32[]{:S(2)}, u32[]{:S(2)}) %collective-permute-start.2) | collective-permute-done | bytes 131104 | tf_op jit(solution)/shard_map/ppermute | solution.py:366
  59.1 1.0 shard_map.90
  60.1 0.5 collective-permute-start.3
  60.7 1.7 %shard_map.91 = (bf16[2,512,512]{2,1,0:T(8,128)(2,1)S(1)}, bf16[2,256,512]{2,1,0:T(8,128)(2,1)S(1)}, f32[512,128]{1,0:T(8,128)}) custom-call(f32[256,128]{1,0:T(8,128)S(1)} %get-tuple-element.51.after_ref.own_ref.refs_6_, bf16[1,5,2,512,512]{4,3,2,1,0:T(8,128)(2,1)} %refs_0_.11, bf16[1,4,2,512,256]{4,3,2,1,0:T(8,128)(2,1)} %refs_1_.8, ...), custom_call_target="tpu_custom_call" | custom-call | tf_op jit(solution)/shard_map/pallas_call | solution.py:342
  62.3 2.8 %collective-permute-done.3.partner_ref = f32[256,128]{1,0:T(8,128)S(1)} collective-permute-done((f32[256,128]{1,0:T(8,128)S(1)}, f32[256,128]{1,0:T(8,128)S(1)}, u32[]{:S(2)}, u32[]{:S(2)}) %collective-permute-start.3) | collective-permute-done | bytes 131104 | tf_op jit(solution)/shard_map/ppermute | solution.py:366
  65.2 1.0 shard_map.92
  66.2 0.9 collective-permute-start.4
  67.1 0.1 stack.20.bits_ref
  67.2 2.1 %shard_map.93 = (bf16[2,512,512]{2,1,0:T(8,128)(2,1)S(1)}, bf16[4,2,512,256]{3,2,1,0:T(8,128)(2,1)S(1)}, f32[512,128]{1,0:T(8,128)S(1)}, f32[512,128]{1,0:T(8,128)S(1)}, f32[512,128]{1,0:T(8,128)S(1)}) custom-call(f32[256,128]{1,0:T(8,128)S(1)} %get-tuple-element.55.after_ref.own_ref.refs_7_, bf16[1,5,2,512,512]{4,3,2,1,0:T(8,128)(2,1)} %refs_0_.11, ...), custom_call_target="tpu_custom_call" | custom-call | tf_op jit(solution)/shard_map/pallas_call | solution.py:342
  69.3 4.1 %collective-permute-done.4.partner_ref = f32[256,128]{1,0:T(8,128)S(1)} collective-permute-done((f32[256,128]{1,0:T(8,128)S(1)}, f32[256,128]{1,0:T(8,128)S(1)}, u32[]{:S(2)}, u32[]{:S(2)}) %collective-permute-start.4) | collective-permute-done | bytes 131104 | tf_op jit(solution)/shard_map/ppermute | solution.py:366
  73.4 2.4 %shard_map.94 = (f32[256,128]{1,0:T(8,128)S(1)}, f32[256,128]{1,0:T(8,128)S(1)}) custom-call(s32[5]{0:T(128)S(1)} %stack.20.bits_ref, f32[256,128]{1,0:T(8,128)S(1)} %get-tuple-element.55.after_ref.own_ref.refs_7_, f32[256,128]{1,0:T(8,128)S(1)} %collective-permute-done.4.partner_ref, bf16[2,512,512]{2,1,0:T(8,128)(2,1)S(1)} %get-tuple-element.59.inverse_ref, ...), custom_call_target="tpu_custom_call" | custom-call | tf_op jit(solution)/shard_map/pallas_call | solution.py:342
  75.9 0.1 collective-permute-start.5
  75.9 1.3 %collective-permute-done.5.others_ref = f32[256,128]{1,0:T(8,128)S(1)} collective-permute-done((f32[256,128]{1,0:T(8,128)S(1)}, f32[256,128]{1,0:T(8,128)S(1)}, u32[]{:S(2)}, u32[]{:S(2)}) %collective-permute-start.5) | collective-permute-done | bytes 131104 | tf_op jit(solution)/shard_map/ppermute | solution.py:366
  77.3 5.9 %shard_map.95 = s16[32,136,128]{2,1,0:T(8,128)(2,1)S(1)} custom-call(s32[1]{0:T(128)} %bitcast.bit_ref, f32[256,128]{1,0:T(8,128)S(1)} %get-tuple-element.65.mine_ref, f32[256,128]{1,0:T(8,128)S(1)} %collective-permute-done.5.others_ref, f32[256,128]{1,0:T(8,128)S(1)} %get-tuple-element.39.after_ref.own_ref, f32[256,128]{1,0:T(8,128)S(1)} %get-tuple-element.40.other_ref, ...), custom_call_target="tpu_custom_call" | custom-call | tf_op jit(solution)/shard_map/pallas_call | solution.py:342
  83.2 32.3 %all_to_all.10.got_ref = s16[32,136,128]{2,1,0:T(8,128)(2,1)S(1)} all-to-all(s16[32,136,128]{2,1,0:T(8,128)(2,1)S(1)} %shard_map.95), channel_id=1, replica_groups=mesh['row'=8,'col'=4] {'row','col'}, dimensions={0} | all-to-all | bytes 2228224 | tf_op jit(solution)/shard_map/all_to_all | solution.py:392
  115.5 3.5 %shard_map.96 = f32[1024,256]{1,0:T(8,128)} custom-call(s16[32,136,128]{2,1,0:T(8,128)(2,1)S(1)} %all_to_all.10.got_ref, f32[8,128]{1,0:T(8,128)S(1)} %get-tuple-element.38.after_ref.slot_ref), custom_call_target="tpu_custom_call" | custom-call | tf_op jit(solution)/shard_map/pallas_call | solution.py:342
Async XLA Ops:
  3.6 35.0 %all-to-all-start = ((bf16[32,136,128]{2,1,0:T(8,128)(2,1)}), bf16[32,136,128]{2,1,0:T(8,128)(2,1)S(1)}, u32[]{:S(2)}, u32[]{:S(2)}) async-start(bf16[32,136,128]{2,1,0:T(8,128)(2,1)} %get-tuple-element.37), calls=%async_computation | async-start | bytes 2228224 | tf_op jit(solution)/shard_map/all_to_all | solution.py:392
  44.2 1.7 %collective-permute-start = (f32[256,128]{1,0:T(8,128)S(1)}, f32[256,128]{1,0:T(8,128)S(1)}, u32[]{:S(2)}, u32[]{:S(2)}) collective-permute-start(f32[256,128]{1,0:T(8,128)S(1)} %get-tuple-element.40.other_ref), channel_id=1, source_target_pairs={{0,1},{1,0},{2,3},{3,2},{4,5},{5,4},{6,7},{7,6},{8,9},{9,8},{10,11... | collective-permute-start | bytes 393224 | tf_op jit(solution)/shard_map/ppermute | solution.py:366
  46.9 6.0 %collective-permute-start.1 = (f32[256,128]{1,0:T(8,128)S(1)}, f32[256,128]{1,0:T(8,128)S(1)}, u32[]{:S(2)}, u32[]{:S(2)}) collective-permute-start(f32[256,128]{1,0:T(8,128)S(1)} %get-tuple-element.43.after_ref.own_ref.refs_4_), channel_id=1, source_target_pairs={{0,2},{1,3},{2,0},{3,1},{4,6},{5,7},{6,4},{7,5},{8,10},{9,11},{10,... | collective-permute-start | bytes 393224 | tf_op jit(solution)/shard_map/ppermute | solution.py:366
  53.9 5.2 %collective-permute-start.2 = (f32[256,128]{1,0:T(8,128)S(1)}, f32[256,128]{1,0:T(8,128)S(1)}, u32[]{:S(2)}, u32[]{:S(2)}) collective-permute-start(f32[256,128]{1,0:T(8,128)S(1)} %get-tuple-element.47.after_ref.own_ref.refs_5_), channel_id=1, source_target_pairs={{0,4},{4,0},{8,12},{12,8},{16,20},{20,16},{24,28},{28,24},{1,5},{5... | collective-permute-start | bytes 393224 | tf_op jit(solution)/shard_map/ppermute | solution.py:366
  60.1 5.0 %collective-permute-start.3 = (f32[256,128]{1,0:T(8,128)S(1)}, f32[256,128]{1,0:T(8,128)S(1)}, u32[]{:S(2)}, u32[]{:S(2)}) collective-permute-start(f32[256,128]{1,0:T(8,128)S(1)} %get-tuple-element.51.after_ref.own_ref.refs_6_), channel_id=1, source_target_pairs={{0,8},{4,12},{8,0},{12,4},{16,24},{20,28},{24,16},{28,20},{1,9},{5... | collective-permute-start | bytes 393224 | tf_op jit(solution)/shard_map/ppermute | solution.py:366
  66.2 7.3 %collective-permute-start.4 = (f32[256,128]{1,0:T(8,128)S(1)}, f32[256,128]{1,0:T(8,128)S(1)}, u32[]{:S(2)}, u32[]{:S(2)}) collective-permute-start(f32[256,128]{1,0:T(8,128)S(1)} %get-tuple-element.55.after_ref.own_ref.refs_7_), channel_id=1, source_target_pairs={{0,16},{4,20},{8,24},{12,28},{16,0},{20,4},{24,8},{28,12},{1,17},{... | collective-permute-start | bytes 393224 | tf_op jit(solution)/shard_map/ppermute | solution.py:366
  75.9 1.4 %collective-permute-start.5 = (f32[256,128]{1,0:T(8,128)S(1)}, f32[256,128]{1,0:T(8,128)S(1)}, u32[]{:S(2)}, u32[]{:S(2)}) collective-permute-start(f32[256,128]{1,0:T(8,128)S(1)} %get-tuple-element.66), channel_id=1, source_target_pairs={{0,1},{1,0},{2,3},{3,2},{4,5},{5,4},{6,7},{7,6},{8,9},{9,8},{10,11... | collective-permute-start | bytes 393224 | tf_op jit(solution)/shard_map/ppermute | solution.py:366

commit v5 on v4

v5 whole, which is shorter than its diff:
```python
import functools

import jax
import jax.numpy as jnp
from jax import lax
from jax.experimental import pallas as pl
from jax.experimental.pallas import tpu as pltpu
from jax.sharding import PartitionSpec as P

LANES = 128
EXTRA = 8
CODE_BASE = 32
SCALE_STEPS = 64
HEADROOM = 1.002
ROUNDER = 1.5 * 2.0**23
TAIL = 16
STEP = 256
PIECES = 4
BF16 = jnp.bfloat16
F32 = jnp.float32


def whole_matmul(a, b):
    return lax.dot_general(a, b, (((1,), (0,)), ((), ())), preferred_element_type=F32)


def matmul(a, b):
    pieces = [whole_matmul(a[at : at + STEP], b) for at in range(0, a.shape[0], STEP)]
    return pieces[0] if len(pieces) == 1 else jnp.concatenate(pieces, axis=0)


def matmul_nt(a, b):
    return lax.dot_general(a, b, (((1,), (1,)), ((), ())), preferred_element_type=F32)


def iota(shape, dim):
    return lax.broadcasted_iota(jnp.int32, shape, dim)


def rotated(x):
    if x.shape[1] == LANES:
        turned = pltpu.roll(x, LANES // 2, 1)
        return jnp.where(iota(x.shape, 1) < LANES // 2, -turned, turned)
    return jnp.concatenate([-x[:, LANES:], x[:, :LANES]], axis=1)


def swapped(first, second):
    low = iota(first.shape, 1) < LANES // 2
    return (
        jnp.where(low, first, pltpu.roll(second, LANES // 2, 1)),
        jnp.where(low, pltpu.roll(first, LANES // 2, 1), second),
    )


def two_parts(x):
    high = x.astype(BF16)
    low = (x - high.astype(F32)).astype(BF16)
    return jnp.concatenate([high, low], axis=1)


def folded(both):
    width = both.shape[1] // 2
    return both[:, :width] + both[:, width:]


def apply_complex(real, imag, x):
    return folded(matmul(real, two_parts(x)) + matmul(imag, two_parts(rotated(x))))


def unit_of(code):
    return jnp.exp2(code * (1.0 / SCALE_STEPS) - 15.0) * HEADROOM


def inverse_unit_of(code):
    return jnp.exp2(15.0 - code * (1.0 / SCALE_STEPS)) * (1.0 / HEADROOM)


def rounded(x):
    return (x + ROUNDER) - ROUNDER


def to_int16(x):
    return x.astype(jnp.int32).astype(jnp.int16)


def from_int16(x):
    return x.astype(jnp.int32).astype(F32)


def encoded(x):
    code = scale_code(x)
    level = rounded(x * inverse_unit_of(code))
    return to_int16(jnp.concatenate([level, jnp.broadcast_to(code, (TAIL, LANES))], axis=0))


def decoded(levels):
    values = from_int16(levels)
    return values[:-TAIL] * unit_of(values[-TAIL : 1 - TAIL])


def scale_code(x):
    largest = jnp.max(jnp.abs(x), axis=0, keepdims=True)
    return jnp.ceil(jnp.log2(jnp.maximum(largest, 2.0**-110)) * SCALE_STEPS)


def fetch(source, target, sem):
    copy = pltpu.make_async_copy(source, target, sem)
    copy.start()
    return copy


def wide_one_hot(columns, blocks):
    lane = iota((LANES, LANES), 1).astype(F32)
    one, zero = jnp.ones((), BF16), jnp.zeros((), BF16)
    names = []
    for entry in columns:
        block = jnp.floor(entry * (1.0 / LANES))
        names.append(jnp.where(lane == entry - block * LANES, block, -1.0))
    names = jnp.concatenate(names, axis=0).astype(BF16)
    return jnp.concatenate([jnp.where(names == jnp.array(g, BF16), one, zero) for g in range(blocks)], axis=1)


def row_blocks(x):
    return jnp.concatenate([x[:, at : at + LANES] for at in range(0, x.shape[1], LANES)], axis=0)


def ranks(hits):
    rows, width = hits.shape
    upper = (iota((LANES, LANES), 0) < iota((LANES, LANES), 1)).astype(F32).astype(BF16)
    pieces = jnp.concatenate(
        [hits[:, at : at + LANES] for at in range(0, width, LANES)], axis=0
    ).astype(BF16)
    inside = matmul(pieces, upper)
    totals = matmul(pieces, jnp.ones((LANES, LANES), BF16))
    ahead = jnp.zeros((rows, LANES), F32)
    parts = []
    for k in range(width // LANES):
        parts.append(inside[k * rows : (k + 1) * rows] + ahead)
        ahead = ahead + totals[k * rows : (k + 1) * rows]
    return jnp.concatenate(parts, axis=1)


def pack_kernel(
    me_ref, order_hbm, rows_hbm, send_hbm, slot_ref, order_ref, rows_ref, chosen_ref, send_ref, sem, *,
    devices, capacity,
):
    order_copy = fetch(order_hbm, order_ref, sem.at[0])
    rows_copy = fetch(rows_hbm, rows_ref, sem.at[1])
    leaf_rows = rows_ref.shape[0]
    order_copy.wait()
    order = order_ref[...]
    target = order // leaf_rows
    position = order - target * leaf_rows
    hits = (iota((devices, leaf_rows), 0) == target).astype(F32)
    rank = jnp.sum(hits * ranks(hits), axis=0, keepdims=True).astype(jnp.int32)
    slot_ref[...] = row_blocks((target * capacity + rank).astype(F32))
    group = LANES // capacity
    lane = rank + lax.rem(me_ref[0], group) * capacity
    high = position // CODE_BASE
    low = position - high * CODE_BASE
    codes = jnp.concatenate([hits * (high + 1).astype(F32), hits * low.astype(F32)], axis=0)
    places = (iota((LANES, leaf_rows), 0) == lane).astype(F32).astype(BF16)
    spread = matmul_nt(codes.astype(BF16), places)
    extra = (devices, EXTRA, LANES)
    send_ref[:, 2 * capacity :, :] = jnp.where(
        iota(extra, 1) < EXTRA // 2,
        jnp.broadcast_to(spread[:devices].reshape(devices, 1, LANES), extra),
        jnp.broadcast_to(spread[devices:].reshape(devices, 1, LANES), extra),
    ).astype(BF16)
    in_slot = (iota((capacity, leaf_rows), 0) == rank).astype(F32).astype(BF16)
    hits = hits.astype(BF16)
    for t in range(devices):
        chosen_ref[t * capacity : (t + 1) * capacity, :] = in_slot * hits[t : t + 1, :]
    rows_copy.wait()
    count = devices // PIECES
    copies = []
    for piece in range(PIECES):
        blocks = pl.ds(piece * count, count)
        sent = matmul(chosen_ref[pl.ds(piece * count * capacity, count * capacity), :], rows_ref[...])
        sent = sent.astype(BF16)
        send_ref[blocks, :capacity, :] = sent[:, :LANES].reshape(count, capacity, LANES)
        send_ref[blocks, capacity : 2 * capacity, :] = sent[:, LANES:].reshape(count, capacity, LANES)
        copies.append(fetch(send_ref.at[blocks], send_hbm.at[blocks], sem.at[2 + piece]))
    for copy in copies:
        copy.wait()


def codes_of(got_ref, devices, capacity):
    group = LANES // capacity
    extra = got_ref[:, 2 * capacity :, :].astype(F32)
    return [sum(extra[k + g] for g in range(group)) for k in range(0, devices, group)]


def load_kernel(after_ref, *refs, picks, turned, stores, rows_of, groups, kept):
    refs = list(refs)

    def take(count):
        taken = refs[:count]
        del refs[:count]
        return taken

    count = len(picks)
    plain = count - turned
    gathers = 1 if rows_of else 0
    sources, stored, given = take(count), take(stores), take(2 * gathers)
    targets, held, gathered = take(count), take(stores), take(gathers)
    scratch, chosen, landed = take(turned), take(gathers), take(rows_of == "lift")
    work, (sem,) = take(gathers and not kept), refs
    landing = targets[:plain] + scratch
    if landed:
        lift_copy = fetch(given[1].at[0], landed[0], sem.at[count + stores])
    copies = [
        fetch(source.at[pick], target, sem.at[k])
        for k, (source, target, pick) in enumerate(zip(sources, landing, picks))
    ]
    copies += [fetch(stored[k], held[k], sem.at[count + k]) for k in range(stores)]
    if rows_of:
        out_ref = gathered[0] if kept else work[0]
        (chosen_ref,) = chosen
        chosen_ref[...] = wide_one_hot(place_columns(given[0], groups), chosen_ref.shape[1] // LANES)
        if landed:
            lift_copy.wait()
            width = landed[0].shape[2]
            for part in range(2):
                columns = slice(part * width, (part + 1) * width)
                out_ref[:, columns] = matmul(chosen_ref[...], landed[0][part]).astype(BF16)
        else:
            out_ref[...] = folded(matmul(chosen_ref[...], given[1][...]))
        if not kept:
            copies.append(fetch(out_ref, gathered[0], sem.at[count + stores + 1]))
    for k in range(turned):
        copies[plain + k].wait()
        for part in range(2):
            targets[plain + k][part] = jnp.transpose(scratch[k][part])
    for k, copy in enumerate(copies):
        if not plain <= k < count:
            copy.wait()


def place_columns(place_ref, groups):
    turned = jnp.transpose(place_ref[...])
    return [
        (turned[:, k * EXTRA : k * EXTRA + 1] - 1.0) * CODE_BASE
        + turned[:, k * EXTRA + EXTRA // 2 : k * EXTRA + EXTRA // 2 + 1]
        for k in range(*groups)
    ]


def place_kernel(
    got_ref, inverse_hbm, placed_ref, place_ref, inverse_ref, chosen_ref, rows_ref, sem, *, devices, capacity
):
    inverse_copy = fetch(inverse_hbm.at[0], inverse_ref, sem.at[0])
    leaf_rows = placed_ref.shape[0]
    codes = codes_of(got_ref, devices, capacity)
    place_ref[...] = jnp.concatenate(codes, axis=0)
    code = iota((CODE_BASE, LANES), 0).astype(F32)
    is_low = jnp.concatenate(
        [(code == one[EXTRA // 2 : EXTRA // 2 + 1]).astype(F32) for one in codes], axis=1
    ).astype(BF16)
    is_high = jnp.concatenate([(code == one[:1] - 1.0).astype(F32) for one in codes], axis=1).astype(BF16)
    for h in range(leaf_rows // CODE_BASE):
        chosen_ref[h * CODE_BASE : (h + 1) * CODE_BASE, :] = is_low * is_high[h : h + 1, :]
    slots = devices * capacity
    rows_ref[:, :LANES] = got_ref[:, :capacity, :].reshape(slots, LANES)
    rows_ref[:, LANES:] = got_ref[:, capacity : 2 * capacity, :].reshape(slots, LANES)
    placed_ref[...] = matmul(chosen_ref[...], rows_ref[...]).astype(BF16)
    inverse_copy.wait()


def leaf_kernel(placed_ref, inverse_ref, parts_ref):
    placed = placed_ref[...]
    parts_ref[...] = two_parts(matmul(inverse_ref[0], placed) + matmul(inverse_ref[1], rotated(placed)))


def coef_kernel(bit_ref, parts_ref, basis_ref, own_ref, other_ref):
    width = parts_ref.shape[1] // 2
    parts = parts_ref[...]
    turned = jnp.concatenate([rotated(parts[:, :width]), rotated(parts[:, width:])], axis=1)
    coef = folded(matmul(basis_ref[0], parts) + matmul(basis_ref[1], turned))
    first, second = swapped(coef[:, :LANES], coef[:, LANES:])
    odd = bit_ref[0] == 1
    own_ref[...] = jnp.where(odd, second, first)
    other_ref[...] = jnp.where(odd, first, second)


def node_rhs(upper, own, partner):
    is_upper = upper == 1
    return jnp.concatenate(
        [jnp.where(is_upper, partner, own), jnp.where(is_upper, own, partner)], axis=0
    )


def node_kernel(bit_ref, own_ref, partner_ref, inverse_ref, basis_ref, sol_ref, coef_ref, code_ref):
    partner = partner_ref[...]
    rhs = node_rhs(bit_ref[0], own_ref[...], partner if partner.dtype == F32 else decoded(partner))
    sol = apply_complex(inverse_ref[0], inverse_ref[1], rhs)
    sol_ref[...] = sol
    coef = apply_complex(basis_ref[0], basis_ref[1], sol)
    coef_ref[...] = coef
    code_ref[...] = encoded(coef)


def fetch_pieces(pieces, target, sem):
    copies, at = [], 0
    for k, piece in enumerate(pieces):
        copies.append(fetch(piece, target.at[pl.ds(at, piece.shape[0])], sem.at[k]))
        at += piece.shape[0]
    return copies


def descent_kernel(bits_ref, own_ref, partner_ref, inverse_ref, lift_hbm, *refs):
    levels = bits_ref.shape[0]
    below = levels - 1
    sols, coefs = refs[:below], refs[below : 2 * below]
    gathered = refs[2 * below : -5]
    mine_ref, other_ref, moved_ref, lift_ref, sem = refs[-5:]
    lift_copies = [
        fetch(lift_hbm.at[0, k], lift_ref.at[k], sem.at[len(gathered) + k]) for k in range(below - 1, -1, -1)
    ]
    rank = own_ref.shape[0]
    copies = fetch_pieces(gathered, moved_ref, sem)

    def half(bit):
        return pl.ds(pl.multiple_of(bit * rank, rank), rank)

    rhs = node_rhs(bits_ref[below], own_ref[...], decoded(partner_ref[...]))
    rows = half(bits_ref[below])
    down = apply_complex(inverse_ref[0, rows, :], inverse_ref[1, rows, :], rhs)
    for k in range(below - 1, 0, -1):
        gap = coefs[k][...] - down
        rows = half(bits_ref[k])
        lift_copies[below - 1 - k].wait()
        down = sols[k][rows, :] - apply_complex(lift_ref[k, 0, rows, :], lift_ref[k, 1, rows, :], gap)
    gap = coefs[0][...] - down
    lift_copies[-1].wait()
    down = sols[0][...] - apply_complex(lift_ref[0, 0], lift_ref[0, 1], gap)
    swap = bits_ref[0] == 1
    mine_ref[...] = jnp.where(swap, down[rank:], down[:rank])
    other_ref[...] = jnp.where(swap, down[:rank], down[rank:])
    for copy in copies:
        copy.wait()


def finish_kernel(
    bit_ref, mine_ref, others_ref, own_ref, other_ref, *refs, devices, capacity
):
    *pieces, send_ref = refs
    moved, pieces = pieces[:2], pieces[2:]
    swap = bit_ref[0] == 1
    mine = own_ref[...] - mine_ref[...]
    other = other_ref[...] - others_ref[...]
    first, second = swapped(jnp.where(swap, other, mine), jnp.where(swap, mine, other))
    gap = jnp.concatenate([first, second], axis=1)
    rank, width = gap.shape
    moved = jnp.concatenate([piece[...] for piece in moved], axis=0)
    change = matmul(moved[:, :rank], two_parts(gap)) + matmul(moved[:, rank:], two_parts(rotated(gap)))
    sol = jnp.concatenate([piece[...] for piece in pieces], axis=0) - folded(change)
    code = scale_code(sol)
    level = to_int16(rounded(sol * inverse_unit_of(code)))
    send_ref[:, :capacity, :] = level[:, :LANES].reshape(devices, capacity, LANES)
    send_ref[:, capacity : 2 * capacity, :] = level[:, LANES:].reshape(devices, capacity, LANES)
    extra = (EXTRA, LANES)
    extra = jnp.where(
        iota(extra, 0) < EXTRA // 2,
        jnp.broadcast_to(code[:, :LANES], extra),
        jnp.broadcast_to(code[:, LANES:], extra),
    )
    extra = to_int16(extra)
    send_ref[:, 2 * capacity :, :] = jnp.broadcast_to(
        extra.reshape(1, EXTRA, LANES), (devices, EXTRA, LANES)
    )


def unpack_kernel(got_ref, slot_ref, out_ref, *, devices, capacity):
    slots = devices * capacity
    turned = jnp.transpose(slot_ref[...])
    chosen = wide_one_hot([turned[:, k : k + 1] for k in range(turned.shape[1])], slots // LANES)
    extra = from_int16(got_ref[:, 2 * capacity :, :])
    halves = []
    for half in range(2):
        level = from_int16(got_ref[:, half * capacity : (half + 1) * capacity, :])
        unit = unit_of(extra[:, half * (EXTRA // 2) : half * (EXTRA // 2) + 1, :])
        halves.append((level * unit).reshape(slots, LANES))
    parts = two_parts(jnp.concatenate(halves, axis=1))
    out_ref[...] = folded(whole_matmul(chosen, parts))


def call(kernel, outs, operands, scratch=(), vmem=24):
    specs = {
        "smem": pl.BlockSpec(memory_space=pltpu.SMEM),
        "vmem": pl.BlockSpec(memory_space=pltpu.VMEM),
        "hbm": pl.BlockSpec(memory_space=pl.ANY),
        "any": pl.BlockSpec(memory_space=pl.ANY),
    }
    results = pl.pallas_call(
        kernel,
        out_shape=[pltpu.HBM(out.shape, out.dtype) if space == "hbm" else out for out, space in outs],
        in_specs=[specs[space] for _, space in operands],
        out_specs=[specs[space] for _, space in outs],
        scratch_shapes=[
            pltpu.SemaphoreType.DMA((one,)) if isinstance(one, int) else pltpu.VMEM(one.shape, one.dtype)
            for one in scratch
        ],
        compiler_params=pltpu.CompilerParams(vmem_limit_bytes=vmem * 2**20),
    )(
        *[
            pltpu.with_memory_space_constraint(array, pltpu.HBM) if space == "hbm" else array
            for array, space in operands
        ]
    )
    return results


def shape(dims, dtype=F32):
    return jax.ShapeDtypeStruct(dims, dtype)


def from_partner(shard, axis, apart):
    return lax.ppermute(shard, axis, [(i, i ^ 1 << apart) for i in range(lax.axis_size(axis))])


def tree_bit(height, col_levels):
    if height < col_levels:
        return lax.axis_index("col") >> height & 1
    return lax.axis_index("row") >> height - col_levels & 1


def per_device(
    right_sides, tree_order, leaf_inverse, leaf_basis, leaf_lift, node_inverse, node_basis, node_lift
):
    row_count = lax.axis_size("row")
    col_count = lax.axis_size("col")
    devices = row_count * col_count
    col_levels = col_count.bit_length() - 1
    levels = col_levels + row_count.bit_length() - 1
    leaf_rows, width = right_sides.shape
    rank = leaf_basis.shape[3]
    capacity = 2 * leaf_rows // min(devices, leaf_rows // 8)
    block = (devices, 2 * capacity + EXTRA, LANES)
    sizes = dict(devices=devices, capacity=capacity)
    me = (lax.axis_index("row") * col_count + lax.axis_index("col")).astype(jnp.int32)
    bits = [tree_bit(height, col_levels).astype(jnp.int32) for height in range(levels)]

    def exchange(blocks):
        return lax.all_to_all(blocks, ("row", "col"), split_axis=0, concat_axis=0, tiled=True)

    def partner_of(shard, height):
        if height < col_levels:
            return from_partner(shard, "col", height)
        return from_partner(shard, "row", height - col_levels)

    send, slot = call(
        functools.partial(pack_kernel, **sizes),
        [(shape(block, BF16), "hbm"), (shape((leaf_rows // LANES, LANES)), "vmem")],
        [(me.reshape(1), "smem"), (tree_order.reshape(1, leaf_rows), "hbm"), (right_sides, "hbm")],
        [
            shape((1, leaf_rows), jnp.int32),
            shape(right_sides.shape, BF16),
            shape((devices * capacity, leaf_rows), BF16),
            shape(block, BF16),
            2 + PIECES,
        ],
    )
    slots = devices * capacity
    total = slots // LANES
    gathers = {
        levels - 3: ("sol", (0, total // 2), False),
        levels - 2: ("sol", (total // 2, total), False),
        levels - 1: ("lift", (0, 3 * total // 8), False),
        levels: ("lift", (3 * total // 8, total), True),
    }

    def load(after, weights, picks, turned=0, stores=(), gather=("", (0, 0), False)):
        shapes = [jax.eval_shape(lambda w, pick=pick: w[pick], w) for w, pick in zip(weights, picks)]
        plain = len(weights) - turned
        outs = [shape(one.shape, one.dtype) for one in shapes[:plain]]
        outs += [shape((2, one.shape[2], one.shape[1]), one.dtype) for one in shapes[plain:]]
        rows_of, groups, kept = gather
        rows = (groups[1] - groups[0]) * LANES
        taken = {
            "": [],
            "sol": [shape((rows, width))],
            "lift": [shape((rows, 2 * rank), BF16)],
        }[rows_of]
        given = {"": [], "sol": [(place, "vmem"), (parts, "vmem")], "lift": [(place, "vmem"), (leaf_lift, "hbm")]}
        work = [shape((rows, leaf_rows), BF16)] if rows_of else []
        work += [shape(leaf_lift.shape[1:], BF16)] if rows_of == "lift" else []
        work += [] if kept else taken
        return call(
            functools.partial(
                load_kernel,
                picks=picks,
                turned=turned,
                stores=len(stores),
                rows_of=rows_of,
                groups=groups,
                kept=kept,
            ),
            [(out, "vmem") for out in outs]
            + [(shape(one.shape), "hbm") for one in stores]
            + [(one, "vmem" if kept else "hbm") for one in taken],
            [(after, "any")]
            + [(weight, "hbm") for weight in weights]
            + [(one, "any") for one in stores]
            + given[rows_of],
            [shape(one.shape, one.dtype) for one in shapes[plain:]]
            + work
            + [len(weights) + len(stores) + 2 * bool(rows_of)],
            vmem=14 if rows_of else 6,
        )

    place = parts = None
    got = exchange(send)
    (leaf_basis,) = load(slot, (leaf_basis,), (0,), turned=1)
    half = shape((rank, LANES))
    placed, place, inverse = call(
        functools.partial(place_kernel, **sizes),
        [
            (shape((leaf_rows, width), BF16), "vmem"),
            (shape((slots // LANES * EXTRA, LANES)), "vmem"),
            (shape(leaf_inverse.shape[1:], BF16), "vmem"),
        ],
        [(got, "vmem"), (leaf_inverse, "hbm")],
        [shape((leaf_rows, slots), BF16), shape((slots, width), BF16), 1],
    )
    (parts,) = call(
        leaf_kernel,
        [(shape((leaf_rows, 2 * width), BF16), "vmem")],
        [(placed, "vmem"), (inverse, "vmem")],
    )
    own, other = call(
        coef_kernel,
        [(half, "vmem"), (half, "vmem")],
        [(bits[0].reshape(1), "smem"), (parts, "vmem"), (leaf_basis, "vmem")],
    )
    leaf_own, leaf_other = own, other
    whole = shape((2 * rank, LANES))
    sols, stored, coefs, gathered = [], [], [], []
    no_gather = ("", (0, 0), False)
    for height in range(1, levels):
        partner = partner_of(other if height == 1 else code, height - 1)
        pick = (0, height - 1)
        inverse, basis, *kept = load(
            own, (node_inverse, node_basis), (pick, pick), 1, sols[-1:], gathers.get(height, no_gather)
        )
        stored += kept[: len(sols[-1:])]
        gathered += kept[len(sols[-1:]) :]
        sol, own, code = call(
            node_kernel,
            [(whole, "vmem"), (half, "vmem"), (shape((rank + TAIL, LANES), jnp.int16), "vmem")],
            [
                (bits[height - 1].reshape(1), "smem"),
                (own, "vmem"),
                (partner, "vmem"),
                (inverse, "vmem"),
                (basis, "vmem"),
            ],
            vmem=8,
        )
        sols.append(sol)
        coefs.append(own)
    partner = partner_of(code, levels - 1)
    inverse, *kept = load(
        own,
        (node_inverse, *stored),
        ((0, levels - 1),) + (slice(None),) * len(stored),
        gather=gathers[levels],
    )
    sols = kept[: len(stored)] + sols[-1:]
    gathered += kept[len(stored) :]
    mine, other, moved = call(
        descent_kernel,
        [
            (half, "vmem"),
            (half, "vmem"),
            (shape(gathered[2].shape, BF16), "vmem"),
        ],
        [(jnp.stack(bits), "smem"), (own, "vmem"), (partner, "vmem"), (inverse, "vmem"), (node_lift, "hbm")]
        + [(sol, "vmem") for sol in sols]
        + [(coef, "vmem") for coef in coefs]
        + [(one, "hbm") for one in gathered[2:-1]],
        [shape(node_lift.shape[1:], BF16), len(gathered) - 3 + levels - 1],
        vmem=12,
    )
    other_sent = other
    other = partner_of(other_sent, 0)
    bases = load(other_sent, gathered[:2], (slice(None),) * 2)
    (back,) = call(
        functools.partial(finish_kernel, **sizes),
        [(shape(block, jnp.int16), "vmem")],
        [
            (bits[0].reshape(1), "smem"),
            (mine, "vmem"),
            (other, "vmem"),
            (leaf_own, "vmem"),
            (leaf_other, "vmem"),
            (moved, "vmem"),
            (gathered[-1], "vmem"),
        ]
        + [(one, "vmem") for one in bases],
    )
    returned = exchange(back)
    (result,) = call(
        functools.partial(unpack_kernel, **sizes),
        [(shape((leaf_rows, width)), "vmem")],
        [(returned, "vmem"), (slot, "vmem")],
    )
    return result


def solution(mesh):
    in_specs = (
        P(("row", "col"), None),
        P(("row", "col")),
        P(("row", "col"), None, None, None),
        P(("row", "col"), None, None, None),
        P(("row", "col"), None, None, None),
        P(("row", "col"), None, None, None, None),
        P(("row", "col"), None, None, None, None),
        P(("row", "col"), None, None, None, None),
    )
    out_specs = P(("row", "col"), None)
    return jax.shard_map(
        per_device, mesh=mesh, in_specs=in_specs, out_specs=out_specs, check_vma=False
    )
```

time: 119 us -> 112 us (0.941)
  waiting for transfers between devices: 39.1 us -> 29.1 us
    ppermute x6, waiting for transfers between devices: 13 us -> 3.09 us  [from_partner(): lax.ppermute(shard, axis, [(i, i ^ 1 << apart) for i in range(lax.axis_si...]
    pallas_call x15 -> x18, Pallas kernels: 35.4 us -> 36.4 us  [call(): pl.pallas_call(kernel, out_shape=[pltpu.HBM(out.shape, out.dtype) if spac...]
  transfers between devices with their start and end apart: 7 -> 7, of which waited for: 6 -> 5; matrix products, arithmetic and copies ran while one was open for 0% -> 0% of each run, Pallas kernels for 9% -> 14%
where the time goes in v5:
time: 112 us; the launch traced here: 111 us
  Pallas kernels  36.4 us (32%)
  blocking collectives  32.9 us (29%)
  waiting for transfers between devices  29.1 us (26%)
  starting transfers between devices  12.5 us (11%)
    pallas_call x18, Pallas kernels, call(): pl.pallas_call(kernel, out_shape=[pltpu.HBM(out.shape, out.dtype) if spac...  36.4 us
    all_to_all x1, blocking collectives, exchange(): lax.all_to_all(blocks, ('row', 'col'), split_axis=0, concat_axis=0, tiled...  32.9 us
    all_to_all x1, waiting for transfers between devices, exchange(): lax.all_to_all(blocks, ('row', 'col'), split_axis=0, concat_axis=0, tiled...  26.1 us
    all_to_all x1, starting transfers between devices, exchange(): lax.all_to_all(blocks, ('row', 'col'), split_axis=0, concat_axis=0, tiled...  7.3 us
    ppermute x6, starting transfers between devices, from_partner(): lax.ppermute(shard, axis, [(i, i ^ 1 << apart) for i in range(lax.axis_si...  5.2 us
    ppermute x6, waiting for transfers between devices, from_partner(): lax.ppermute(shard, axis, [(i, i ^ 1 << apart) for i in range(lax.axis_si...  3.09 us
  transfers between devices with their start and end apart: 7, of which 5 were waited for; matrix products, arithmetic and copies ran while one was open for 0% of the time, Pallas kernels for 14%

profile of v5, /device:TPU:0, one launch (start us, length us, event | category | flops | bytes accessed | tf_op | source)
XLA Modules:
  0.0 111.2 jit_solution(3387239764786532225)
XLA Ops:
  0.0 3.2 %shard_map.82 = (bf16[32,136,128]{2,1,0:T(8,128)(2,1)}, f32[8,128]{1,0:T(8,128)S(1)}) custom-call(s32[1]{0:T(128)} %bitcast.5.me_ref, s32[1,1024]{1,0:T(1,128)} %bitcast.7, bf16[1024,256]{1,0:T(8,128)(2,1)} %rows_hbm.1), custom_call_target="tpu_custom_call" | custom-call | tf_op jit(solution)/shard_map/pallas_call | solution.py:395
  3.2 7.3 %all-to-all-start = ((bf16[32,136,128]{2,1,0:T(8,128)(2,1)}), bf16[32,136,128]{2,1,0:T(8,128)(2,1)S(1)}, u32[]{:S(2)}, u32[]{:S(2)}) async-start(bf16[32,136,128]{2,1,0:T(8,128)(2,1)} %get-tuple-element.48), calls=%async_computation | async-start | bytes 2228224 | tf_op jit(solution)/shard_map/all_to_all | solution.py:445
  10.6 1.6 %shard_map.85.basis_ref = bf16[2,256,1024]{2,1,0:T(8,128)(2,1)S(1)} custom-call(f32[8,128]{1,0:T(8,128)S(1)} %get-tuple-element.51.after_ref.slot_ref, bf16[1,2,1024,256]{3,2,1,0:T(8,128)(2,1)} %refs_0_.6), custom_call_target="tpu_custom_call" | custom-call | tf_op jit(solution)/shard_map/pallas_call | solution.py:395
  12.2 26.1 %all-to-all-done.got_ref = bf16[32,136,128]{2,1,0:T(8,128)(2,1)S(1)} async-done(((bf16[32,136,128]{2,1,0:T(8,128)(2,1)}), bf16[32,136,128]{2,1,0:T(8,128)(2,1)S(1)}, u32[]{:S(2)}, u32[]{:S(2)}) %all-to-all-start) | async-done | bytes 1114144 | tf_op jit(solution)/shard_map/all_to_all | solution.py:445
  38.2 2.3 %shard_map.83 = (bf16[1024,256]{1,0:T(8,128)(2,1)S(1)}, f32[128,128]{1,0:T(8,128)S(1)}, bf16[2,1024,1024]{2,1,0:T(8,128)(2,1)S(1)}) custom-call(bf16[32,136,128]{2,1,0:T(8,128)(2,1)S(1)} %all-to-all-done.got_ref, bf16[1,2,1024,1024]{3,2,1,0:T(8,128)(2,1)} %inverse_hbm.1), custom_call_target="tpu_custom_call" | custom-call | tf_op jit(solution)/shard_map/pallas_call | solution.py:395
  40.5 1.3 %shard_map.84.parts_ref.refs_4_ = bf16[1024,512]{1,0:T(8,128)(2,1)S(1)} custom-call(bf16[1024,256]{1,0:T(8,128)(2,1)S(1)} %get-tuple-element.49.placed_ref, bf16[2,1024,1024]{2,1,0:T(8,128)(2,1)S(1)} %get-tuple-element.50.inverse_ref), custom_call_target="tpu_custom_call" | custom-call | tf_op jit(solution)/shard_map/pallas_call | solution.py:395
  41.8 0.8 shard_map.86
  42.6 0.1 collective-permute-start
  42.7 1.6 %shard_map.87 = (bf16[2,512,512]{2,1,0:T(8,128)(2,1)S(1)}, bf16[2,256,512]{2,1,0:T(8,128)(2,1)S(1)}) custom-call(f32[256,128]{1,0:T(8,128)S(1)} %get-tuple-element.52.after_ref.own_ref, bf16[1,5,2,512,512]{4,3,2,1,0:T(8,128)(2,1)} %refs_0_.11, bf16[1,4,2,512,256]{4,3,2,1,0:T(8,128)(2,1)} %refs_1_.7), custom_call_target="tpu_custom_call" | custom-call | tf_op jit(solution)/shard_map/pallas_call | solution.py:395
  44.2 0.0 collective-permute-done.partner_ref
  44.3 1.0 shard_map.88
  45.3 1.5 %collective-permute-start.1 = (s16[272,128]{1,0:T(8,128)(2,1)S(1)}, s16[272,128]{1,0:T(8,128)(2,1)S(1)}, u32[]{:S(2)}, u32[]{:S(2)}) collective-permute-start(s16[272,128]{1,0:T(8,128)(2,1)S(1)} %get-tuple-element.57), channel_id=1, source_target_pairs={{0,2},{1,3},{2,0},{3,1},{4,6},{5,7},{6,4},{7,5},{8,10},{9,11},{10,... | collective-permute-start | bytes 208904 | tf_op jit(solution)/shard_map/ppermute | solution.py:419
  46.8 2.5 %shard_map.89 = (bf16[2,512,512]{2,1,0:T(8,128)(2,1)S(1)}, bf16[2,256,512]{2,1,0:T(8,128)(2,1)S(1)}, f32[512,128]{1,0:T(8,128)}, f32[1024,256]{1,0:T(8,128)}) custom-call(f32[256,128]{1,0:T(8,128)S(1)} %get-tuple-element.56.after_ref.own_ref.refs_4_, bf16[1,5,2,512,512]{4,3,2,1,0:T(8,128)(2,1)} %refs_0_.11, bf16[1,4,2,512,256]{4,3,2,1,0:T(8,128)(2,1)} %refs_1_.7, ...), custom_call_target="tpu_custom_call" | custom-call | tf_op jit(solution)/shard_map/pallas_call | solution.py:395
  49.4 0.6 collective-permute-done.1.partner_ref
  49.9 1.0 shard_map.90
  51.0 1.5 %collective-permute-start.2 = (s16[272,128]{1,0:T(8,128)(2,1)S(1)}, s16[272,128]{1,0:T(8,128)(2,1)S(1)}, u32[]{:S(2)}, u32[]{:S(2)}) collective-permute-start(s16[272,128]{1,0:T(8,128)(2,1)S(1)} %get-tuple-element.63), channel_id=1, source_target_pairs={{0,4},{4,0},{8,12},{12,8},{16,20},{20,16},{24,28},{28,24},{1,5},{5... | collective-permute-start | bytes 208904 | tf_op jit(solution)/shard_map/ppermute | solution.py:419
  52.5 2.6 %shard_map.91 = (bf16[2,512,512]{2,1,0:T(8,128)(2,1)S(1)}, bf16[2,256,512]{2,1,0:T(8,128)(2,1)S(1)}, f32[512,128]{1,0:T(8,128)}, f32[1024,256]{1,0:T(8,128)}) custom-call(f32[256,128]{1,0:T(8,128)S(1)} %get-tuple-element.62.after_ref.own_ref.refs_5_, bf16[1,5,2,512,512]{4,3,2,1,0:T(8,128)(2,1)} %refs_0_.11, bf16[1,4,2,512,256]{4,3,2,1,0:T(8,128)(2,1)} %refs_1_.7, ...), custom_call_target="tpu_custom_call" | custom-call | tf_op jit(solution)/shard_map/pallas_call | solution.py:395
  55.1 0.3 collective-permute-done.2.partner_ref
  55.3 1.0 shard_map.92
  56.4 0.7 collective-permute-start.3
  57.1 3.3 %shard_map.93 = (bf16[2,512,512]{2,1,0:T(8,128)(2,1)S(1)}, bf16[2,256,512]{2,1,0:T(8,128)(2,1)S(1)}, f32[512,128]{1,0:T(8,128)}, bf16[768,512]{1,0:T(8,128)(2,1)}) custom-call(f32[256,128]{1,0:T(8,128)S(1)} %get-tuple-element.67.after_ref.own_ref.refs_6_, bf16[1,5,2,512,512]{4,3,2,1,0:T(8,128)(2,1)} %refs_0_.11, bf16[1,4,2,512,256]{4,3,2,1,0:T(8,128)(2,1)} %refs_1_.7, ...), custom_call_target="tpu_custom_call" | custom-call | tf_op jit(solution)/shard_map/pallas_call | solution.py:395
  60.4 0.4 collective-permute-done.3.partner_ref
  60.8 1.0 shard_map.94
  61.8 1.3 %collective-permute-start.4 = (s16[272,128]{1,0:T(8,128)(2,1)S(1)}, s16[272,128]{1,0:T(8,128)(2,1)S(1)}, u32[]{:S(2)}, u32[]{:S(2)}) collective-permute-start(s16[272,128]{1,0:T(8,128)(2,1)S(1)} %get-tuple-element.73), channel_id=1, source_target_pairs={{0,16},{4,20},{8,24},{12,28},{16,0},{20,4},{24,8},{28,12},{1,17},{... | collective-permute-start | bytes 208904 | tf_op jit(solution)/shard_map/ppermute | solution.py:419
  63.1 0.1 stack.20.bits_ref
  63.2 2.8 %shard_map.95 = (bf16[2,512,512]{2,1,0:T(8,128)(2,1)S(1)}, f32[512,128]{1,0:T(8,128)S(1)}, f32[512,128]{1,0:T(8,128)S(1)}, f32[512,128]{1,0:T(8,128)S(1)}, bf16[1280,512]{1,0:T(8,128)(2,1)S(1)}) custom-call(f32[256,128]{1,0:T(8,128)S(1)} %get-tuple-element.72.after_ref.own_ref.refs_7_, bf16[1,5,2,512,512]{4,3,2,1,0:T(8,128)(2,1)} %refs_0_.11, ...), custom_call_target="tpu_custom_call" | custom-call | tf_op jit(solution)/shard_map/pallas_call | solution.py:395
  66.0 1.8 %collective-permute-done.4.partner_ref = s16[272,128]{1,0:T(8,128)(2,1)S(1)} collective-permute-done((s16[272,128]{1,0:T(8,128)(2,1)S(1)}, s16[272,128]{1,0:T(8,128)(2,1)S(1)}, u32[]{:S(2)}, u32[]{:S(2)}) %collective-permute-start.4) | collective-permute-done | bytes 69664 | tf_op jit(solution)/shard_map/ppermute | solution.py:419
  67.8 3.3 %shard_map.96 = (f32[256,128]{1,0:T(8,128)S(1)}, f32[256,128]{1,0:T(8,128)S(1)}, bf16[768,512]{1,0:T(8,128)(2,1)S(1)}) custom-call(s32[5]{0:T(128)S(1)} %stack.20.bits_ref, f32[256,128]{1,0:T(8,128)S(1)} %get-tuple-element.72.after_ref.own_ref.refs_7_, s16[272,128]{1,0:T(8,128)(2,1)S(1)} %collective-permute-done.4.partner_ref, ...), custom_call_target="tpu_custom_call" | custom-call | tf_op jit(solution)/shard_map/pallas_call | solution.py:395
  71.1 0.1 collective-permute-start.5
  71.2 1.6 %shard_map.97 = (f32[1024,256]{1,0:T(8,128)S(1)}, f32[1024,256]{1,0:T(8,128)S(1)}) custom-call(f32[256,128]{1,0:T(8,128)S(1)} %get-tuple-element.84.after_ref, f32[1024,256]{1,0:T(8,128)} %get-tuple-element.87.refs_0_, f32[1024,256]{1,0:T(8,128)} %get-tuple-element.88.refs_1_), custom_call_target="tpu_custom_call" | custom-call | tf_op jit(solution)/shard_map/pallas_call | solution.py:395
  72.8 0.0 collective-permute-done.5.others_ref
  72.8 2.1 %shard_map.98 = s16[32,136,128]{2,1,0:T(8,128)(2,1)S(1)} custom-call(s32[1]{0:T(128)} %bitcast.bit_ref, f32[256,128]{1,0:T(8,128)S(1)} %get-tuple-element.83.mine_ref, f32[256,128]{1,0:T(8,128)S(1)} %collective-permute-done.5.others_ref, f32[256,128]{1,0:T(8,128)S(1)} %get-tuple-element.52.after_ref.own_ref, f32[256,128]{1,0:T(8,128)S(1)} %get-tuple-element.53.other_ref, ...), custom_call_target="tpu_custom_call" | custom-call | tf_op jit(solution)/shard_map/pallas_call | solution.py:395
  74.9 32.9 %all_to_all.10.got_ref = s16[32,136,128]{2,1,0:T(8,128)(2,1)S(1)} all-to-all(s16[32,136,128]{2,1,0:T(8,128)(2,1)S(1)} %shard_map.98), channel_id=1, replica_groups=mesh['row'=8,'col'=4] {'row','col'}, dimensions={0} | all-to-all | bytes 2228224 | tf_op jit(solution)/shard_map/all_to_all | solution.py:445
  107.8 3.5 %shard_map.99 = f32[1024,256]{1,0:T(8,128)} custom-call(s16[32,136,128]{2,1,0:T(8,128)(2,1)S(1)} %all_to_all.10.got_ref, f32[8,128]{1,0:T(8,128)S(1)} %get-tuple-element.51.after_ref.slot_ref), custom_call_target="tpu_custom_call" | custom-call | tf_op jit(solution)/shard_map/pallas_call | solution.py:395
Async XLA Ops:
  3.2 35.0 %all-to-all-start = ((bf16[32,136,128]{2,1,0:T(8,128)(2,1)}), bf16[32,136,128]{2,1,0:T(8,128)(2,1)S(1)}, u32[]{:S(2)}, u32[]{:S(2)}) async-start(bf16[32,136,128]{2,1,0:T(8,128)(2,1)} %get-tuple-element.48), calls=%async_computation | async-start | bytes 2228224 | tf_op jit(solution)/shard_map/all_to_all | solution.py:445
  42.6 1.7 %collective-permute-start = (f32[256,128]{1,0:T(8,128)S(1)}, f32[256,128]{1,0:T(8,128)S(1)}, u32[]{:S(2)}, u32[]{:S(2)}) collective-permute-start(f32[256,128]{1,0:T(8,128)S(1)} %get-tuple-element.53.other_ref), channel_id=1, source_target_pairs={{0,1},{1,0},{2,3},{3,2},{4,5},{5,4},{6,7},{7,6},{8,9},{9,8},{10,11... | collective-permute-start | bytes 393224 | tf_op jit(solution)/shard_map/ppermute | solution.py:419
  45.3 4.6 %collective-permute-start.1 = (s16[272,128]{1,0:T(8,128)(2,1)S(1)}, s16[272,128]{1,0:T(8,128)(2,1)S(1)}, u32[]{:S(2)}, u32[]{:S(2)}) collective-permute-start(s16[272,128]{1,0:T(8,128)(2,1)S(1)} %get-tuple-element.57), channel_id=1, source_target_pairs={{0,2},{1,3},{2,0},{3,1},{4,6},{5,7},{6,4},{7,5},{8,10},{9,11},{10,... | collective-permute-start | bytes 208904 | tf_op jit(solution)/shard_map/ppermute | solution.py:419
  51.0 4.4 %collective-permute-start.2 = (s16[272,128]{1,0:T(8,128)(2,1)S(1)}, s16[272,128]{1,0:T(8,128)(2,1)S(1)}, u32[]{:S(2)}, u32[]{:S(2)}) collective-permute-start(s16[272,128]{1,0:T(8,128)(2,1)S(1)} %get-tuple-element.63), channel_id=1, source_target_pairs={{0,4},{4,0},{8,12},{12,8},{16,20},{20,16},{24,28},{28,24},{1,5},{5... | collective-permute-start | bytes 208904 | tf_op jit(solution)/shard_map/ppermute | solution.py:419
  56.4 4.4 %collective-permute-start.3 = (s16[272,128]{1,0:T(8,128)(2,1)S(1)}, s16[272,128]{1,0:T(8,128)(2,1)S(1)}, u32[]{:S(2)}, u32[]{:S(2)}) collective-permute-start(s16[272,128]{1,0:T(8,128)(2,1)S(1)} %get-tuple-element.68), channel_id=1, source_target_pairs={{0,8},{4,12},{8,0},{12,4},{16,24},{20,28},{24,16},{28,20},{1,9},{5... | collective-permute-start | bytes 208904 | tf_op jit(solution)/shard_map/ppermute | solution.py:419
  61.8 6.0 %collective-permute-start.4 = (s16[272,128]{1,0:T(8,128)(2,1)S(1)}, s16[272,128]{1,0:T(8,128)(2,1)S(1)}, u32[]{:S(2)}, u32[]{:S(2)}) collective-permute-start(s16[272,128]{1,0:T(8,128)(2,1)S(1)} %get-tuple-element.73), channel_id=1, source_target_pairs={{0,16},{4,20},{8,24},{12,28},{16,0},{20,4},{24,8},{28,12},{1,17},{... | collective-permute-start | bytes 208904 | tf_op jit(solution)/shard_map/ppermute | solution.py:419
  71.1 1.7 %collective-permute-start.5 = (f32[256,128]{1,0:T(8,128)S(1)}, f32[256,128]{1,0:T(8,128)S(1)}, u32[]{:S(2)}, u32[]{:S(2)}) collective-permute-start(f32[256,128]{1,0:T(8,128)S(1)} %get-tuple-element.84.after_ref), channel_id=1, source_target_pairs={{0,1},{1,0},{2,3},{3,2},{4,5},{5,4},{6,7},{7,6},{8,9},{9,8},{10,11... | collective-permute-start | bytes 393224 | tf_op jit(solution)/shard_map/ppermute | solution.py:419

commit v6 on v5

--- a/solution.py
+++ b/solution.py
@@ -31,6 +31,11 @@
 
 def matmul_nt(a, b):
     return lax.dot_general(a, b, (((1,), (1,)), ((), ())), preferred_element_type=F32)
+
+
+def tree_bits(levels):
+    index = lax.axis_index("row") * lax.axis_size("col") + lax.axis_index("col")
+    return [index >> height & 1 for height in range(levels)]
 
 
 def iota(shape, dim):
@@ -141,7 +146,7 @@
 
 
 def pack_kernel(
-    me_ref, order_hbm, rows_hbm, send_hbm, slot_ref, order_ref, rows_ref, chosen_ref, send_ref, sem, *,
+    order_hbm, rows_hbm, send_ref, slot_ref, order_ref, rows_ref, chosen_ref, sem, *,
     devices, capacity,
 ):
     order_copy = fetch(order_hbm, order_ref, sem.at[0])
@@ -155,7 +160,7 @@
     rank = jnp.sum(hits * ranks(hits), axis=0, keepdims=True).astype(jnp.int32)
     slot_ref[...] = row_blocks((target * capacity + rank).astype(F32))
     group = LANES // capacity
-    lane = rank + lax.rem(me_ref[0], group) * capacity
+    lane = rank + lax.rem(lax.axis_index("row") * lax.axis_size("col") + lax.axis_index("col"), group) * capacity
     high = position // CODE_BASE
     low = position - high * CODE_BASE
     codes = jnp.concatenate([hits * (high + 1).astype(F32), hits * low.astype(F32)], axis=0)
@@ -173,16 +178,12 @@
         chosen_ref[t * capacity : (t + 1) * capacity, :] = in_slot * hits[t : t + 1, :]
     rows_copy.wait()
     count = devices // PIECES
-    copies = []
     for piece in range(PIECES):
         blocks = pl.ds(piece * count, count)
         sent = matmul(chosen_ref[pl.ds(piece * count * capacity, count * capacity), :], rows_ref[...])
         sent = sent.astype(BF16)
         send_ref[blocks, :capacity, :] = sent[:, :LANES].reshape(count, capacity, LANES)
         send_ref[blocks, capacity : 2 * capacity, :] = sent[:, LANES:].reshape(count, capacity, LANES)
-        copies.append(fetch(send_ref.at[blocks], send_hbm.at[blocks], sem.at[2 + piece]))
-    for copy in copies:
-        copy.wait()
 
 
 def codes_of(got_ref, devices, capacity):
@@ -191,7 +192,7 @@
     return [sum(extra[k + g] for g in range(group)) for k in range(0, devices, group)]
 
 
-def load_kernel(after_ref, *refs, picks, turned, stores, rows_of, groups, kept):
+def load_kernel(after_ref, *refs, picks, turned, stores, rows_of, groups, kept, levels):
     refs = list(refs)
 
     def take(count):
@@ -209,8 +210,17 @@
     landing = targets[:plain] + scratch
     if landed:
         lift_copy = fetch(given[1].at[0], landed[0], sem.at[count + stores])
+
+    bits = tree_bits(levels) if any(isinstance(one, tuple) for pick in picks for one in pick) else []
+
+    def part(pick, rows):
+        return tuple(
+            pl.ds(pl.multiple_of(bits[one[1]] * rows, rows), rows) if isinstance(one, tuple) else one
+            for one in pick
+        )
+
     copies = [
-        fetch(source.at[pick], target, sem.at[k])
+        fetch(source.at[part(pick, target.shape[-2])], target, sem.at[k])
         for k, (source, target, pick) in enumerate(zip(sources, landing, picks))
     ]
     copies += [fetch(stored[k], held[k], sem.at[count + k]) for k in range(stores)]
@@ -247,8 +257,10 @@
 
 
 def place_kernel(
-    got_ref, inverse_hbm, placed_ref, place_ref, inverse_ref, chosen_ref, rows_ref, sem, *, devices, capacity
+    got_ref, inverse_hbm, basis_hbm, placed_ref, place_ref, inverse_ref, turned_ref,
+    chosen_ref, rows_ref, basis_ref, sem, *, devices, capacity,
 ):
+    basis_copy = fetch(basis_hbm.at[0], basis_ref, sem.at[1])
     inverse_copy = fetch(inverse_hbm.at[0], inverse_ref, sem.at[0])
     leaf_rows = placed_ref.shape[0]
     codes = codes_of(got_ref, devices, capacity)
@@ -264,6 +276,9 @@
     rows_ref[:, :LANES] = got_ref[:, :capacity, :].reshape(slots, LANES)
     rows_ref[:, LANES:] = got_ref[:, capacity : 2 * capacity, :].reshape(slots, LANES)
     placed_ref[...] = matmul(chosen_ref[...], rows_ref[...]).astype(BF16)
+    basis_copy.wait()
+    for part in range(2):
+        turned_ref[part] = jnp.transpose(basis_ref[part])
     inverse_copy.wait()
 
 
@@ -272,13 +287,13 @@
     parts_ref[...] = two_parts(matmul(inverse_ref[0], placed) + matmul(inverse_ref[1], rotated(placed)))
 
 
-def coef_kernel(bit_ref, parts_ref, basis_ref, own_ref, other_ref):
+def coef_kernel(parts_ref, basis_ref, own_ref, other_ref):
     width = parts_ref.shape[1] // 2
     parts = parts_ref[...]
     turned = jnp.concatenate([rotated(parts[:, :width]), rotated(parts[:, width:])], axis=1)
     coef = folded(matmul(basis_ref[0], parts) + matmul(basis_ref[1], turned))
     first, second = swapped(coef[:, :LANES], coef[:, LANES:])
-    odd = bit_ref[0] == 1
+    odd = tree_bits(1)[0] == 1
     own_ref[...] = jnp.where(odd, second, first)
     other_ref[...] = jnp.where(odd, first, second)
 
@@ -290,9 +305,9 @@
     )
 
 
-def node_kernel(bit_ref, own_ref, partner_ref, inverse_ref, basis_ref, sol_ref, coef_ref, code_ref):
+def node_kernel(own_ref, partner_ref, inverse_ref, basis_ref, sol_ref, coef_ref, code_ref, *, height):
     partner = partner_ref[...]
-    rhs = node_rhs(bit_ref[0], own_ref[...], partner if partner.dtype == F32 else decoded(partner))
+    rhs = node_rhs(tree_bits(height)[-1], own_ref[...], partner if partner.dtype == F32 else decoded(partner))
     sol = apply_complex(inverse_ref[0], inverse_ref[1], rhs)
     sol_ref[...] = sol
     coef = apply_complex(basis_ref[0], basis_ref[1], sol)
@@ -300,53 +315,34 @@
     code_ref[...] = encoded(coef)
 
 
-def fetch_pieces(pieces, target, sem):
-    copies, at = [], 0
-    for k, piece in enumerate(pieces):
-        copies.append(fetch(piece, target.at[pl.ds(at, piece.shape[0])], sem.at[k]))
-        at += piece.shape[0]
-    return copies
-
-
-def descent_kernel(bits_ref, own_ref, partner_ref, inverse_ref, lift_hbm, *refs):
-    levels = bits_ref.shape[0]
+def descent_kernel(own_ref, partner_ref, inverse_ref, *refs, levels):
     below = levels - 1
-    sols, coefs = refs[:below], refs[below : 2 * below]
-    gathered = refs[2 * below : -5]
-    mine_ref, other_ref, moved_ref, lift_ref, sem = refs[-5:]
-    lift_copies = [
-        fetch(lift_hbm.at[0, k], lift_ref.at[k], sem.at[len(gathered) + k]) for k in range(below - 1, -1, -1)
-    ]
+    bits = tree_bits(levels)
+    lifts, sols, coefs = refs[:below], refs[below : 2 * below], refs[2 * below : 3 * below]
+    moved_hbm, mine_ref, other_ref, moved_ref, sem = refs[3 * below :]
+    moved_copy = fetch(moved_hbm, moved_ref, sem.at[0])
     rank = own_ref.shape[0]
-    copies = fetch_pieces(gathered, moved_ref, sem)
-
-    def half(bit):
-        return pl.ds(pl.multiple_of(bit * rank, rank), rank)
-
-    rhs = node_rhs(bits_ref[below], own_ref[...], decoded(partner_ref[...]))
-    rows = half(bits_ref[below])
-    down = apply_complex(inverse_ref[0, rows, :], inverse_ref[1, rows, :], rhs)
-    for k in range(below - 1, 0, -1):
+    rhs = node_rhs(bits[below], own_ref[...], decoded(partner_ref[...]))
+    down = apply_complex(inverse_ref[0], inverse_ref[1], rhs)
+    for k in range(below - 1, -1, -1):
         gap = coefs[k][...] - down
-        rows = half(bits_ref[k])
-        lift_copies[below - 1 - k].wait()
-        down = sols[k][rows, :] - apply_complex(lift_ref[k, 0, rows, :], lift_ref[k, 1, rows, :], gap)
-    gap = coefs[0][...] - down
-    lift_copies[-1].wait()
-    down = sols[0][...] - apply_complex(lift_ref[0, 0], lift_ref[0, 1], gap)
-    swap = bits_ref[0] == 1
+        if k == below - 1:
+            sol = sols[k][pl.ds(pl.multiple_of(bits[k] * rank, rank), rank), :]
+        else:
+            sol = sols[k][...]
+        down = sol - apply_complex(lifts[k][0], lifts[k][1], gap)
+    swap = bits[0] == 1
     mine_ref[...] = jnp.where(swap, down[rank:], down[:rank])
     other_ref[...] = jnp.where(swap, down[:rank], down[rank:])
-    for copy in copies:
-        copy.wait()
+    moved_copy.wait()
 
 
 def finish_kernel(
-    bit_ref, mine_ref, others_ref, own_ref, other_ref, *refs, devices, capacity
+    mine_ref, others_ref, own_ref, other_ref, *refs, devices, capacity
 ):
     *pieces, send_ref = refs
     moved, pieces = pieces[:2], pieces[2:]
-    swap = bit_ref[0] == 1
+    swap = tree_bits(1)[0] == 1
     mine = own_ref[...] - mine_ref[...]
     other = other_ref[...] - others_ref[...]
     first, second = swapped(jnp.where(swap, other, mine), jnp.where(swap, mine, other))
@@ -387,7 +383,6 @@
 
 def call(kernel, outs, operands, scratch=(), vmem=24):
     specs = {
-        "smem": pl.BlockSpec(memory_space=pltpu.SMEM),
         "vmem": pl.BlockSpec(memory_space=pltpu.VMEM),
         "hbm": pl.BlockSpec(memory_space=pl.ANY),
         "any": pl.BlockSpec(memory_space=pl.ANY),
@@ -419,12 +414,6 @@
     return lax.ppermute(shard, axis, [(i, i ^ 1 << apart) for i in range(lax.axis_size(axis))])
 
 
-def tree_bit(height, col_levels):
-    if height < col_levels:
-        return lax.axis_index("col") >> height & 1
-    return lax.axis_index("row") >> height - col_levels & 1
-
-
 def per_device(
     right_sides, tree_order, leaf_inverse, leaf_basis, leaf_lift, node_inverse, node_basis, node_lift
 ):
@@ -438,9 +427,6 @@
     capacity = 2 * leaf_rows // min(devices, leaf_rows // 8)
     block = (devices, 2 * capacity + EXTRA, LANES)
     sizes = dict(devices=devices, capacity=capacity)
-    me = (lax.axis_index("row") * col_count + lax.axis_index("col")).astype(jnp.int32)
-    bits = [tree_bit(height, col_levels).astype(jnp.int32) for height in range(levels)]
-
     def exchange(blocks):
         return lax.all_to_all(blocks, ("row", "col"), split_axis=0, concat_axis=0, tiled=True)
 
@@ -451,14 +437,13 @@
 
     send, slot = call(
         functools.partial(pack_kernel, **sizes),
-        [(shape(block, BF16), "hbm"), (shape((leaf_rows // LANES, LANES)), "vmem")],
-        [(me.reshape(1), "smem"), (tree_order.reshape(1, leaf_rows), "hbm"), (right_sides, "hbm")],
+        [(shape(block, BF16), "vmem"), (shape((leaf_rows // LANES, LANES)), "vmem")],
+        [(tree_order.reshape(1, leaf_rows), "hbm"), (right_sides, "hbm")],
         [
             shape((1, leaf_rows), jnp.int32),
             shape(right_sides.shape, BF16),
             shape((devices * capacity, leaf_rows), BF16),
-            shape(block, BF16),
-            2 + PIECES,
+            2,
         ],
     )
     slots = devices * capacity
@@ -471,7 +456,12 @@
     }
 
     def load(after, weights, picks, turned=0, stores=(), gather=("", (0, 0), False)):
-        shapes = [jax.eval_shape(lambda w, pick=pick: w[pick], w) for w, pick in zip(weights, picks)]
+        shapes = [
+            jax.eval_shape(
+                lambda w, pick=pick: w[tuple(slice(0, rank) if isinstance(p, tuple) else p for p in pick)], w
+            )
+            for w, pick in zip(weights, picks)
+        ]
         plain = len(weights) - turned
         outs = [shape(one.shape, one.dtype) for one in shapes[:plain]]
         outs += [shape((2, one.shape[2], one.shape[1]), one.dtype) for one in shapes[plain:]]
@@ -495,6 +485,7 @@
                 rows_of=rows_of,
                 groups=groups,
                 kept=kept,
+                levels=levels,
             ),
             [(out, "vmem") for out in outs]
             + [(shape(one.shape), "hbm") for one in stores]
@@ -511,17 +502,22 @@
 
     place = parts = None
     got = exchange(send)
-    (leaf_basis,) = load(slot, (leaf_basis,), (0,), turned=1)
     half = shape((rank, LANES))
-    placed, place, inverse = call(
+    placed, place, inverse, basis = call(
         functools.partial(place_kernel, **sizes),
         [
             (shape((leaf_rows, width), BF16), "vmem"),
             (shape((slots // LANES * EXTRA, LANES)), "vmem"),
             (shape(leaf_inverse.shape[1:], BF16), "vmem"),
+            (shape((2, rank, leaf_rows), BF16), "vmem"),
         ],
-        [(got, "vmem"), (leaf_inverse, "hbm")],
-        [shape((leaf_rows, slots), BF16), shape((slots, width), BF16), 1],
+        [(got, "vmem"), (leaf_inverse, "hbm"), (leaf_basis, "hbm")],
+        [
+            shape((leaf_rows, slots), BF16),
+            shape((slots, width), BF16),
+            shape(leaf_basis.shape[1:], BF16),
+            2,
+        ],
     )
     (parts,) = call(
         leaf_kernel,
@@ -531,7 +527,7 @@
     own, other = call(
         coef_kernel,
         [(half, "vmem"), (half, "vmem")],
-        [(bits[0].reshape(1), "smem"), (parts, "vmem"), (leaf_basis, "vmem")],
+        [(parts, "vmem"), (basis, "vmem")],
     )
     leaf_own, leaf_other = own, other
     whole = shape((2 * rank, LANES))
@@ -546,10 +542,9 @@
         stored += kept[: len(sols[-1:])]
         gathered += kept[len(sols[-1:]) :]
         sol, own, code = call(
-            node_kernel,
+            functools.partial(node_kernel, height=height),
             [(whole, "vmem"), (half, "vmem"), (shape((rank + TAIL, LANES), jnp.int16), "vmem")],
             [
-                (bits[height - 1].reshape(1), "smem"),
                 (own, "vmem"),
                 (partner, "vmem"),
                 (inverse, "vmem"),
@@ -560,36 +555,42 @@
         sols.append(sol)
         coefs.append(own)
     partner = partner_of(code, levels - 1)
-    inverse, *kept = load(
+    loaded = load(
         own,
-        (node_inverse, *stored),
-        ((0, levels - 1),) + (slice(None),) * len(stored),
+        (node_inverse, *(node_lift for _ in coefs), *stored),
+        (
+            (0, levels - 1, slice(None), ("half", levels - 1)),
+            (0, 0),
+            *((0, k, slice(None), ("half", k)) for k in range(1, levels - 1)),
+            (),
+            *((("half", k),) for k in range(1, levels - 2)),
+        ),
         gather=gathers[levels],
     )
-    sols = kept[: len(stored)] + sols[-1:]
-    gathered += kept[len(stored) :]
+    inverse, lifts, sols = loaded[0], loaded[1:levels], [*loaded[levels:-1], sols[-1]]
+    gathered.append(loaded[-1])
     mine, other, moved = call(
-        descent_kernel,
+        functools.partial(descent_kernel, levels=levels),
         [
             (half, "vmem"),
             (half, "vmem"),
             (shape(gathered[2].shape, BF16), "vmem"),
         ],
-        [(jnp.stack(bits), "smem"), (own, "vmem"), (partner, "vmem"), (inverse, "vmem"), (node_lift, "hbm")]
+        [(own, "vmem"), (partner, "vmem"), (inverse, "vmem")]
+        + [(lift, "vmem") for lift in lifts]
         + [(sol, "vmem") for sol in sols]
         + [(coef, "vmem") for coef in coefs]
         + [(one, "hbm") for one in gathered[2:-1]],
-        [shape(node_lift.shape[1:], BF16), len(gathered) - 3 + levels - 1],
-        vmem=12,
+        [1],
+        vmem=8,
     )
     other_sent = other
     other = partner_of(other_sent, 0)
-    bases = load(other_sent, gathered[:2], (slice(None),) * 2)
+    bases = load(other_sent, gathered[:2], ((),) * 2)
     (back,) = call(
         functools.partial(finish_kernel, **sizes),
         [(shape(block, jnp.int16), "vmem")],
         [
-            (bits[0].reshape(1), "smem"),
             (mine, "vmem"),
             (other, "vmem"),
             (leaf_own, "vmem"),

time: 112 us -> 110 us (0.982)
  blocking collectives: 32.9 us -> 67.6 us
  waiting for transfers between devices: 29.1 us -> 5.3 us
  starting transfers between devices: 12.5 us -> 3.06 us
  Pallas kernels: 36.4 us -> 33.1 us
    all_to_all x1 -> x2, blocking collectives: 32.9 us -> 67.6 us  [exchange(): lax.all_to_all(blocks, ('row', 'col'), split_axis=0, concat_axis=0, tiled...]
    all_to_all x1 -> x0, waiting for transfers between devices: 26.1 us -> none  [exchange(): lax.all_to_all(blocks, ('row', 'col'), split_axis=0, concat_axis=0, tiled...]
    all_to_all x1 -> x0, starting transfers between devices: 7.3 us -> none  [exchange(): lax.all_to_all(blocks, ('row', 'col'), split_axis=0, concat_axis=0, tiled...]
    pallas_call x18 -> x17, Pallas kernels: 36.4 us -> 33.1 us  [call(): pl.pallas_call(kernel, out_shape=[pltpu.HBM(out.shape, out.dtype) if spac...]
    ppermute x6, waiting for transfers between devices: 3.09 us -> 5.3 us  [from_partner(): lax.ppermute(shard, axis, [(i, i ^ 1 << apart) for i in range(lax.axis_si...]
    ppermute x6, starting transfers between devices: 5.2 us -> 3.06 us  [from_partner(): lax.ppermute(shard, axis, [(i, i ^ 1 << apart) for i in range(lax.axis_si...]
  transfers between devices with their start and end apart: 7 -> 6, of which waited for: 5 -> 4; matrix products, arithmetic and copies ran while one was open for 0% -> 0% of each run, Pallas kernels for 14% -> 13%
where the time goes in v6:
time: 110 us; the launch traced here: 109 us
  blocking collectives  67.6 us (61%)
  Pallas kernels  33.1 us (30%)
  waiting for transfers between devices  5.3 us (5%)
  starting transfers between devices  3.06 us (3%)
    all_to_all x2, blocking collectives, exchange(): lax.all_to_all(blocks, ('row', 'col'), split_axis=0, concat_axis=0, tiled...  67.6 us
    pallas_call x17, Pallas kernels, call(): pl.pallas_call(kernel, out_shape=[pltpu.HBM(out.shape, out.dtype) if spac...  33.1 us
    ppermute x6, waiting for transfers between devices, from_partner(): lax.ppermute(shard, axis, [(i, i ^ 1 << apart) for i in range(lax.axis_si...  5.3 us
    ppermute x6, starting transfers between devices, from_partner(): lax.ppermute(shard, axis, [(i, i ^ 1 << apart) for i in range(lax.axis_si...  3.06 us
  transfers between devices with their start and end apart: 6, of which 4 were waited for; matrix products, arithmetic and copies ran while one was open for 0% of the time, Pallas kernels for 13%

profile of v6, /device:TPU:0, one launch (start us, length us, event | category | flops | bytes accessed | tf_op | source)
XLA Modules:
  0.0 109.3 jit_solution(17738405783182414006)
XLA Ops:
  0.0 2.5 %shard_map.82 = (bf16[32,136,128]{2,1,0:T(8,128)(2,1)S(1)}, f32[8,128]{1,0:T(8,128)S(1)}) custom-call(s32[1,1024]{1,0:T(1,128)} %bitcast.1, bf16[1024,256]{1,0:T(8,128)(2,1)} %rows_hbm.1), custom_call_target="tpu_custom_call" | custom-call | tf_op jit(solution)/shard_map/pallas_call | solution.py:390
  2.5 36.5 %all_to_all.10.got_ref = bf16[32,136,128]{2,1,0:T(8,128)(2,1)S(1)} all-to-all(bf16[32,136,128]{2,1,0:T(8,128)(2,1)S(1)} %get-tuple-element.53), channel_id=1, replica_groups=mesh['row'=8,'col'=4] {'row','col'}, dimensions={0} | all-to-all | bytes 2228224 | tf_op jit(solution)/shard_map/all_to_all | solution.py:431
  39.0 2.6 %shard_map.83 = (bf16[1024,256]{1,0:T(8,128)(2,1)S(1)}, f32[128,128]{1,0:T(8,128)S(1)}, bf16[2,1024,1024]{2,1,0:T(8,128)(2,1)S(1)}, bf16[2,256,1024]{2,1,0:T(8,128)(2,1)S(1)}) custom-call(bf16[32,136,128]{2,1,0:T(8,128)(2,1)S(1)} %all_to_all.10.got_ref, bf16[1,2,1024,1024]{3,2,1,0:T(8,128)(2,1)} %inverse_hbm.1, bf16[1,2,1024,256]{3,2,1,0:T(8,128)(2,1)} %basis_hbm.1), custom_call_target="tpu_custom_call" | custom-call | tf_op jit(solution)/shard_map/pallas_call | solution.py:390
  41.6 1.3 %shard_map.84.parts_ref.refs_4_ = bf16[1024,512]{1,0:T(8,128)(2,1)S(1)} custom-call(bf16[1024,256]{1,0:T(8,128)(2,1)S(1)} %get-tuple-element.54.placed_ref, bf16[2,1024,1024]{2,1,0:T(8,128)(2,1)S(1)} %get-tuple-element.55.inverse_ref), custom_call_target="tpu_custom_call" | custom-call | tf_op jit(solution)/shard_map/pallas_call | solution.py:390
  42.9 0.8 shard_map.85
  43.7 0.1 collective-permute-start
  43.8 1.6 %shard_map.86 = (bf16[2,512,512]{2,1,0:T(8,128)(2,1)S(1)}, bf16[2,256,512]{2,1,0:T(8,128)(2,1)S(1)}) custom-call(f32[256,128]{1,0:T(8,128)S(1)} %get-tuple-element.57.after_ref.own_ref, bf16[1,5,2,512,512]{4,3,2,1,0:T(8,128)(2,1)} %refs_0_.9, bf16[1,4,2,512,256]{4,3,2,1,0:T(8,128)(2,1)} %refs_1_.8), custom_call_target="tpu_custom_call" | custom-call | tf_op jit(solution)/shard_map/pallas_call | solution.py:390
  45.3 0.0 collective-permute-done.partner_ref
  45.3 1.0 shard_map.87
  46.4 0.6 collective-permute-start.1
  47.0 2.5 %shard_map.88 = (bf16[2,512,512]{2,1,0:T(8,128)(2,1)S(1)}, bf16[2,256,512]{2,1,0:T(8,128)(2,1)S(1)}, f32[512,128]{1,0:T(8,128)}, f32[1024,256]{1,0:T(8,128)}) custom-call(f32[256,128]{1,0:T(8,128)S(1)} %get-tuple-element.61.after_ref.own_ref.refs_8_, bf16[1,5,2,512,512]{4,3,2,1,0:T(8,128)(2,1)} %refs_0_.9, bf16[1,4,2,512,256]{4,3,2,1,0:T(8,128)(2,1)} %refs_1_.8, ...), custom_call_target="tpu_custom_call" | custom-call | tf_op jit(solution)/shard_map/pallas_call | solution.py:390
  49.5 1.5 %collective-permute-done.1.partner_ref = s16[272,128]{1,0:T(8,128)(2,1)S(1)} collective-permute-done((s16[272,128]{1,0:T(8,128)(2,1)S(1)}, s16[272,128]{1,0:T(8,128)(2,1)S(1)}, u32[]{:S(2)}, u32[]{:S(2)}) %collective-permute-start.1) | collective-permute-done | bytes 69664 | tf_op jit(solution)/shard_map/ppermute | solution.py:414
  51.0 1.0 shard_map.89
  52.0 0.7 collective-permute-start.2
  52.7 2.5 %shard_map.90 = (bf16[2,512,512]{2,1,0:T(8,128)(2,1)S(1)}, bf16[2,256,512]{2,1,0:T(8,128)(2,1)S(1)}, f32[512,128]{1,0:T(8,128)}, f32[1024,256]{1,0:T(8,128)}) custom-call(f32[256,128]{1,0:T(8,128)S(1)} %get-tuple-element.67.after_ref.own_ref.refs_9_, bf16[1,5,2,512,512]{4,3,2,1,0:T(8,128)(2,1)} %refs_0_.9, bf16[1,4,2,512,256]{4,3,2,1,0:T(8,128)(2,1)} %refs_1_.8, ...), custom_call_target="tpu_custom_call" | custom-call | tf_op jit(solution)/shard_map/pallas_call | solution.py:390
  55.3 1.2 %collective-permute-done.2.partner_ref = s16[272,128]{1,0:T(8,128)(2,1)S(1)} collective-permute-done((s16[272,128]{1,0:T(8,128)(2,1)S(1)}, s16[272,128]{1,0:T(8,128)(2,1)S(1)}, u32[]{:S(2)}, u32[]{:S(2)}) %collective-permute-start.2) | collective-permute-done | bytes 69664 | tf_op jit(solution)/shard_map/ppermute | solution.py:414
  56.4 1.0 shard_map.91
  57.5 0.7 collective-permute-start.3
  58.1 3.3 %shard_map.92 = (bf16[2,512,512]{2,1,0:T(8,128)(2,1)S(1)}, bf16[2,256,512]{2,1,0:T(8,128)(2,1)S(1)}, f32[512,128]{1,0:T(8,128)}, bf16[768,512]{1,0:T(8,128)(2,1)}) custom-call(f32[256,128]{1,0:T(8,128)S(1)} %get-tuple-element.72.after_ref.own_ref.refs_10_, bf16[1,5,2,512,512]{4,3,2,1,0:T(8,128)(2,1)} %refs_0_.9, bf16[1,4,2,512,256]{4,3,2,1,0:T(8,128)(2,1)} %refs_1_.8, ...), custom_call_target="tpu_custom_call" | custom-call | tf_op jit(solution)/shard_map/pallas_call | solution.py:390
  61.4 0.4 collective-permute-done.3.partner_ref
  61.8 1.0 shard_map.93
  62.9 1.0 collective-permute-start.4
  63.8 2.8 %shard_map.94 = (bf16[2,256,512]{2,1,0:T(8,128)(2,1)S(1)}, bf16[2,512,256]{2,1,0:T(8,128)(2,1)S(1)}, bf16[2,256,256]{2,1,0:T(8,128)(2,1)S(1)}, bf16[2,256,256]{2...) custom-call(f32[256,128]{1,0:T(8,128)S(1)} %get-tuple-element.77.aft, ...), custom_call_target="tpu_custom_call" | custom-call | tf_op jit(solution)/shard_map/pallas_call | solution.py:390
  66.7 2.2 %collective-permute-done.4.partner_ref = s16[272,128]{1,0:T(8,128)(2,1)S(1)} collective-permute-done((s16[272,128]{1,0:T(8,128)(2,1)S(1)}, s16[272,128]{1,0:T(8,128)(2,1)S(1)}, u32[]{:S(2)}, u32[]{:S(2)}) %collective-permute-start.4) | collective-permute-done | bytes 69664 | tf_op jit(solution)/shard_map/ppermute | solution.py:414
  68.9 2.0 %shard_map.95 = (f32[256,128]{1,0:T(8,128)S(1)}, f32[256,128]{1,0:T(8,128)S(1)}, bf16[768,512]{1,0:T(8,128)(2,1)S(1)}) custom-call(f32[256,128]{1,0:T(8,128)S(1)} %get-tuple-element.77.after_ref.own_ref.refs_11_, s16[272,128]{1,0:T(8,128)(2,1)S(1)} %collective-permute-done.4.partner_ref, bf16[2,256,512]{2,1,0:T(8,128)(2,1)S(1)} %get-tuple-element.82.inverse_ref, ...), custom_call_target="tpu_custom_call" | custom-call | tf_op jit(solution)/shard_map/pallas_call | solution.py:390
  70.9 0.1 collective-permute-start.5
  71.0 1.6 %shard_map.96 = (f32[1024,256]{1,0:T(8,128)S(1)}, f32[1024,256]{1,0:T(8,128)S(1)}) custom-call(f32[256,128]{1,0:T(8,128)S(1)} %get-tuple-element.93.after_ref, f32[1024,256]{1,0:T(8,128)} %get-tuple-element.96.refs_0_, f32[1024,256]{1,0:T(8,128)} %get-tuple-element.97.refs_1_), custom_call_target="tpu_custom_call" | custom-call | tf_op jit(solution)/shard_map/pallas_call | solution.py:390
  72.5 0.0 collective-permute-done.5.others_ref
  72.6 2.1 %shard_map.97 = s16[32,136,128]{2,1,0:T(8,128)(2,1)S(1)} custom-call(f32[256,128]{1,0:T(8,128)S(1)} %get-tuple-element.92.mine_ref, f32[256,128]{1,0:T(8,128)S(1)} %collective-permute-done.5.others_ref, f32[256,128]{1,0:T(8,128)S(1)} %get-tuple-element.57.after_ref.own_ref, f32[256,128]{1,0:T(8,128)S(1)} %get-tuple-element.58.other_ref, ...), custom_call_target="tpu_custom_call" | custom-call | tf_op jit(solution)/shard_map/pallas_call | solution.py:390
  74.6 31.2 %all_to_all.11.got_ref = s16[32,136,128]{2,1,0:T(8,128)(2,1)S(1)} all-to-all(s16[32,136,128]{2,1,0:T(8,128)(2,1)S(1)} %shard_map.97), channel_id=1, replica_groups=mesh['row'=8,'col'=4] {'row','col'}, dimensions={0} | all-to-all | bytes 2228224 | tf_op jit(solution)/shard_map/all_to_all | solution.py:431
  105.8 3.4 %shard_map.98 = f32[1024,256]{1,0:T(8,128)} custom-call(s16[32,136,128]{2,1,0:T(8,128)(2,1)S(1)} %all_to_all.11.got_ref, f32[8,128]{1,0:T(8,128)S(1)} %get-tuple-element.100.slot_ref), custom_call_target="tpu_custom_call" | custom-call | tf_op jit(solution)/shard_map/pallas_call | solution.py:390
Async XLA Ops:
  43.7 1.7 %collective-permute-start = (f32[256,128]{1,0:T(8,128)S(1)}, f32[256,128]{1,0:T(8,128)S(1)}, u32[]{:S(2)}, u32[]{:S(2)}) collective-permute-start(f32[256,128]{1,0:T(8,128)S(1)} %get-tuple-element.58.other_ref), channel_id=1, source_target_pairs={{0,1},{1,0},{2,3},{3,2},{4,5},{5,4},{6,7},{7,6},{8,9},{9,8},{10,11... | collective-permute-start | bytes 393224 | tf_op jit(solution)/shard_map/ppermute | solution.py:414
  46.4 4.6 %collective-permute-start.1 = (s16[272,128]{1,0:T(8,128)(2,1)S(1)}, s16[272,128]{1,0:T(8,128)(2,1)S(1)}, u32[]{:S(2)}, u32[]{:S(2)}) collective-permute-start(s16[272,128]{1,0:T(8,128)(2,1)S(1)} %get-tuple-element.62), channel_id=1, source_target_pairs={{0,2},{1,3},{2,0},{3,1},{4,6},{5,7},{6,4},{7,5},{8,10},{9,11},{10,... | collective-permute-start | bytes 208904 | tf_op jit(solution)/shard_map/ppermute | solution.py:414
  52.0 4.4 %collective-permute-start.2 = (s16[272,128]{1,0:T(8,128)(2,1)S(1)}, s16[272,128]{1,0:T(8,128)(2,1)S(1)}, u32[]{:S(2)}, u32[]{:S(2)}) collective-permute-start(s16[272,128]{1,0:T(8,128)(2,1)S(1)} %get-tuple-element.68), channel_id=1, source_target_pairs={{0,4},{4,0},{8,12},{12,8},{16,20},{20,16},{24,28},{28,24},{1,5},{5... | collective-permute-start | bytes 208904 | tf_op jit(solution)/shard_map/ppermute | solution.py:414
  57.5 4.4 %collective-permute-start.3 = (s16[272,128]{1,0:T(8,128)(2,1)S(1)}, s16[272,128]{1,0:T(8,128)(2,1)S(1)}, u32[]{:S(2)}, u32[]{:S(2)}) collective-permute-start(s16[272,128]{1,0:T(8,128)(2,1)S(1)} %get-tuple-element.73), channel_id=1, source_target_pairs={{0,8},{4,12},{8,0},{12,4},{16,24},{20,28},{24,16},{28,20},{1,9},{5... | collective-permute-start | bytes 208904 | tf_op jit(solution)/shard_map/ppermute | solution.py:414
  62.9 6.0 %collective-permute-start.4 = (s16[272,128]{1,0:T(8,128)(2,1)S(1)}, s16[272,128]{1,0:T(8,128)(2,1)S(1)}, u32[]{:S(2)}, u32[]{:S(2)}) collective-permute-start(s16[272,128]{1,0:T(8,128)(2,1)S(1)} %get-tuple-element.78), channel_id=1, source_target_pairs={{0,16},{4,20},{8,24},{12,28},{16,0},{20,4},{24,8},{28,12},{1,17},{... | collective-permute-start | bytes 208904 | tf_op jit(solution)/shard_map/ppermute | solution.py:414
  70.9 1.7 %collective-permute-start.5 = (f32[256,128]{1,0:T(8,128)S(1)}, f32[256,128]{1,0:T(8,128)S(1)}, u32[]{:S(2)}, u32[]{:S(2)}) collective-permute-start(f32[256,128]{1,0:T(8,128)S(1)} %get-tuple-element.93.after_ref), channel_id=1, source_target_pairs={{0,1},{1,0},{2,3},{3,2},{4,5},{5,4},{6,7},{7,6},{8,9},{9,8},{10,11... | collective-permute-start | bytes 393224 | tf_op jit(solution)/shard_map/ppermute | solution.py:414

commit v7 on v6

--- a/solution.py
+++ b/solution.py
@@ -16,6 +16,8 @@
 TAIL = 16
 STEP = 256
 PIECES = 4
+NODE_STEP = 128
+FINISH_PIECES = 8
 BF16 = jnp.bfloat16
 F32 = jnp.float32
 
@@ -24,8 +26,8 @@
     return lax.dot_general(a, b, (((1,), (0,)), ((), ())), preferred_element_type=F32)
 
 
-def matmul(a, b):
-    pieces = [whole_matmul(a[at : at + STEP], b) for at in range(0, a.shape[0], STEP)]
+def matmul(a, b, step=STEP):
+    pieces = [whole_matmul(a[at : at + step], b) for at in range(0, a.shape[0], step)]
     return pieces[0] if len(pieces) == 1 else jnp.concatenate(pieces, axis=0)
 
 
@@ -68,8 +70,9 @@
     return both[:, :width] + both[:, width:]
 
 
-def apply_complex(real, imag, x):
-    return folded(matmul(real, two_parts(x)) + matmul(imag, two_parts(rotated(x))))
+def apply_complex(real, imag, x, step=STEP):
+    both = jnp.concatenate([two_parts(x), two_parts(rotated(x))], axis=0)
+    return folded(matmul(jnp.concatenate([real, imag], axis=1), both, step))
 
 
 def unit_of(code):
@@ -146,11 +149,14 @@
 
 
 def pack_kernel(
-    order_hbm, rows_hbm, send_ref, slot_ref, order_ref, rows_ref, chosen_ref, sem, *,
+    order_hbm, rows_hbm, inverse_hbm, basis_hbm, send_ref, slot_ref, real_ref, basis_ref,
+    order_ref, rows_ref, chosen_ref, sem, *,
     devices, capacity,
 ):
     order_copy = fetch(order_hbm, order_ref, sem.at[0])
     rows_copy = fetch(rows_hbm, rows_ref, sem.at[1])
+    basis_copy = fetch(basis_hbm.at[0], basis_ref, sem.at[2])
+    real_copy = fetch(inverse_hbm.at[0, 0], real_ref, sem.at[3])
     leaf_rows = rows_ref.shape[0]
     order_copy.wait()
     order = order_ref[...]
@@ -184,6 +190,8 @@
         sent = sent.astype(BF16)
         send_ref[blocks, :capacity, :] = sent[:, :LANES].reshape(count, capacity, LANES)
         send_ref[blocks, capacity : 2 * capacity, :] = sent[:, LANES:].reshape(count, capacity, LANES)
+    basis_copy.wait()
+    real_copy.wait()
 
 
 def codes_of(got_ref, devices, capacity):
@@ -257,11 +265,10 @@
 
 
 def place_kernel(
-    got_ref, inverse_hbm, basis_hbm, placed_ref, place_ref, inverse_ref, turned_ref,
-    chosen_ref, rows_ref, basis_ref, sem, *, devices, capacity,
+    got_ref, inverse_hbm, basis_ref, placed_ref, place_ref, imag_ref, turned_ref, chosen_ref, rows_ref, sem, *,
+    devices, capacity,
 ):
-    basis_copy = fetch(basis_hbm.at[0], basis_ref, sem.at[1])
-    inverse_copy = fetch(inverse_hbm.at[0], inverse_ref, sem.at[0])
+    imag_copy = fetch(inverse_hbm.at[0, 1], imag_ref, sem.at[0])
     leaf_rows = placed_ref.shape[0]
     codes = codes_of(got_ref, devices, capacity)
     place_ref[...] = jnp.concatenate(codes, axis=0)
@@ -276,15 +283,14 @@
     rows_ref[:, :LANES] = got_ref[:, :capacity, :].reshape(slots, LANES)
     rows_ref[:, LANES:] = got_ref[:, capacity : 2 * capacity, :].reshape(slots, LANES)
     placed_ref[...] = matmul(chosen_ref[...], rows_ref[...]).astype(BF16)
-    basis_copy.wait()
     for part in range(2):
         turned_ref[part] = jnp.transpose(basis_ref[part])
-    inverse_copy.wait()
-
-
-def leaf_kernel(placed_ref, inverse_ref, parts_ref):
+    imag_copy.wait()
+
+
+def leaf_kernel(placed_ref, real_ref, imag_ref, parts_ref):
     placed = placed_ref[...]
-    parts_ref[...] = two_parts(matmul(inverse_ref[0], placed) + matmul(inverse_ref[1], rotated(placed)))
+    parts_ref[...] = two_parts(matmul(real_ref[...], placed) + matmul(imag_ref[...], rotated(placed)))
 
 
 def coef_kernel(parts_ref, basis_ref, own_ref, other_ref):
@@ -308,9 +314,9 @@
 def node_kernel(own_ref, partner_ref, inverse_ref, basis_ref, sol_ref, coef_ref, code_ref, *, height):
     partner = partner_ref[...]
     rhs = node_rhs(tree_bits(height)[-1], own_ref[...], partner if partner.dtype == F32 else decoded(partner))
-    sol = apply_complex(inverse_ref[0], inverse_ref[1], rhs)
+    sol = apply_complex(inverse_ref[0], inverse_ref[1], rhs, NODE_STEP)
     sol_ref[...] = sol
-    coef = apply_complex(basis_ref[0], basis_ref[1], sol)
+    coef = apply_complex(basis_ref[0], basis_ref[1], sol, NODE_STEP)
     coef_ref[...] = coef
     code_ref[...] = encoded(coef)
 
@@ -337,6 +343,16 @@
     moved_copy.wait()
 
 
+def rows_of(refs, rows):
+    parts, at = [], 0
+    for ref in refs:
+        first, last = max(rows.start - at, 0), min(rows.stop - at, ref.shape[0])
+        if first < last:
+            parts.append(ref[first:last, :])
+        at += ref.shape[0]
+    return parts[0] if len(parts) == 1 else jnp.concatenate(parts, axis=0)
+
+
 def finish_kernel(
     mine_ref, others_ref, own_ref, other_ref, *refs, devices, capacity
 ):
@@ -348,26 +364,28 @@
     first, second = swapped(jnp.where(swap, other, mine), jnp.where(swap, mine, other))
     gap = jnp.concatenate([first, second], axis=1)
     rank, width = gap.shape
-    moved = jnp.concatenate([piece[...] for piece in moved], axis=0)
-    change = matmul(moved[:, :rank], two_parts(gap)) + matmul(moved[:, rank:], two_parts(rotated(gap)))
-    sol = jnp.concatenate([piece[...] for piece in pieces], axis=0) - folded(change)
-    code = scale_code(sol)
-    level = to_int16(rounded(sol * inverse_unit_of(code)))
-    send_ref[:, :capacity, :] = level[:, :LANES].reshape(devices, capacity, LANES)
-    send_ref[:, capacity : 2 * capacity, :] = level[:, LANES:].reshape(devices, capacity, LANES)
-    extra = (EXTRA, LANES)
-    extra = jnp.where(
-        iota(extra, 0) < EXTRA // 2,
-        jnp.broadcast_to(code[:, :LANES], extra),
-        jnp.broadcast_to(code[:, LANES:], extra),
-    )
-    extra = to_int16(extra)
-    send_ref[:, 2 * capacity :, :] = jnp.broadcast_to(
-        extra.reshape(1, EXTRA, LANES), (devices, EXTRA, LANES)
-    )
-
-
-def unpack_kernel(got_ref, slot_ref, out_ref, *, devices, capacity):
+    parts = jnp.concatenate([two_parts(gap), two_parts(rotated(gap))], axis=0)
+    count = devices // FINISH_PIECES
+    for at in range(0, devices, count):
+        rows = slice(at * capacity, (at + count) * capacity)
+        sol = rows_of(pieces, rows) - folded(matmul(rows_of(moved, rows), parts))
+        code = scale_code(sol)
+        level = to_int16(rounded(sol * inverse_unit_of(code)))
+        blocks = slice(at, at + count)
+        send_ref[blocks, :capacity, :] = level[:, :LANES].reshape(count, capacity, LANES)
+        send_ref[blocks, capacity : 2 * capacity, :] = level[:, LANES:].reshape(count, capacity, LANES)
+        extra = (EXTRA, LANES)
+        extra = jnp.where(
+            iota(extra, 0) < EXTRA // 2,
+            jnp.broadcast_to(code[:, :LANES], extra),
+            jnp.broadcast_to(code[:, LANES:], extra),
+        )
+        send_ref[blocks, 2 * capacity :, :] = jnp.broadcast_to(
+            to_int16(extra).reshape(1, EXTRA, LANES), (count, EXTRA, LANES)
+        )
+
+
+def unpack_kernel(got_ref, slot_ref, out_hbm, out_ref, sem, *, devices, capacity):
     slots = devices * capacity
     turned = jnp.transpose(slot_ref[...])
     chosen = wide_one_hot([turned[:, k : k + 1] for k in range(turned.shape[1])], slots // LANES)
@@ -378,7 +396,14 @@
         unit = unit_of(extra[:, half * (EXTRA // 2) : half * (EXTRA // 2) + 1, :])
         halves.append((level * unit).reshape(slots, LANES))
     parts = two_parts(jnp.concatenate(halves, axis=1))
-    out_ref[...] = folded(whole_matmul(chosen, parts))
+    count = out_ref.shape[0] // PIECES
+    copies = []
+    for piece in range(PIECES):
+        rows = pl.ds(piece * count, count)
+        out_ref[rows, :] = folded(whole_matmul(chosen[piece * count : (piece + 1) * count], parts))
+        copies.append(fetch(out_ref.at[rows], out_hbm.at[rows], sem.at[piece]))
+    for copy in copies:
+        copy.wait()
 
 
 def call(kernel, outs, operands, scratch=(), vmem=24):
@@ -435,15 +460,21 @@
             return from_partner(shard, "col", height)
         return from_partner(shard, "row", height - col_levels)
 
-    send, slot = call(
+    send, slot, real, basis = call(
         functools.partial(pack_kernel, **sizes),
-        [(shape(block, BF16), "vmem"), (shape((leaf_rows // LANES, LANES)), "vmem")],
-        [(tree_order.reshape(1, leaf_rows), "hbm"), (right_sides, "hbm")],
+        [
+            (shape(block, BF16), "vmem"),
+            (shape((leaf_rows // LANES, LANES)), "vmem"),
+            (shape(leaf_inverse.shape[2:], BF16), "vmem"),
+            (shape(leaf_basis.shape[1:], BF16), "vmem"),
+        ],
+        [(tree_order.reshape(1, leaf_rows), "hbm"), (right_sides, "hbm")]
+        + [(leaf_inverse, "hbm"), (leaf_basis, "hbm")],
         [
             shape((1, leaf_rows), jnp.int32),
             shape(right_sides.shape, BF16),
             shape((devices * capacity, leaf_rows), BF16),
-            2,
+            4,
         ],
     )
     slots = devices * capacity
@@ -503,26 +534,21 @@
     place = parts = None
     got = exchange(send)
     half = shape((rank, LANES))
-    placed, place, inverse, basis = call(
+    placed, place, imag, basis = call(
         functools.partial(place_kernel, **sizes),
         [
             (shape((leaf_rows, width), BF16), "vmem"),
             (shape((slots // LANES * EXTRA, LANES)), "vmem"),
-            (shape(leaf_inverse.shape[1:], BF16), "vmem"),
+            (shape(leaf_inverse.shape[2:], BF16), "vmem"),
             (shape((2, rank, leaf_rows), BF16), "vmem"),
         ],
-        [(got, "vmem"), (leaf_inverse, "hbm"), (leaf_basis, "hbm")],
-        [
-            shape((leaf_rows, slots), BF16),
-            shape((slots, width), BF16),
-            shape(leaf_basis.shape[1:], BF16),
-            2,
-        ],
+        [(got, "vmem"), (leaf_inverse, "hbm"), (basis, "vmem")],
+        [shape((leaf_rows, slots), BF16), shape((slots, width), BF16), 1],
     )
     (parts,) = call(
         leaf_kernel,
         [(shape((leaf_rows, 2 * width), BF16), "vmem")],
-        [(placed, "vmem"), (inverse, "vmem")],
+        [(placed, "vmem"), (real, "vmem"), (imag, "vmem")],
     )
     own, other = call(
         coef_kernel,
@@ -603,8 +629,9 @@
     returned = exchange(back)
     (result,) = call(
         functools.partial(unpack_kernel, **sizes),
-        [(shape((leaf_rows, width)), "vmem")],
+        [(shape((leaf_rows, width)), "hbm")],
         [(returned, "vmem"), (slot, "vmem")],
+        [shape((leaf_rows, width)), PIECES],
     )
     return result
 

time: 110 us -> 107 us (0.973)
  Pallas kernels: 33.1 us -> 30.4 us
    pallas_call x17, Pallas kernels: 33.1 us -> 30.4 us  [call(): pl.pallas_call(kernel, out_shape=[pltpu.HBM(out.shape, out.dtype) if spac...]
where the time goes in v7:
time: 107 us
  blocking collectives  67.6 us (63%)
  Pallas kernels  30.4 us (28%)
  waiting for transfers between devices  5.27 us (5%)
  starting transfers between devices  3.09 us (3%)
    all_to_all x2, blocking collectives, exchange(): lax.all_to_all(blocks, ('row', 'col'), split_axis=0, concat_axis=0, tiled...  67.6 us
    pallas_call x17, Pallas kernels, call(): pl.pallas_call(kernel, out_shape=[pltpu.HBM(out.shape, out.dtype) if spac...  30.4 us
    ppermute x6, waiting for transfers between devices, from_partner(): lax.ppermute(shard, axis, [(i, i ^ 1 << apart) for i in range(lax.axis_si...  5.27 us
    ppermute x6, starting transfers between devices, from_partner(): lax.ppermute(shard, axis, [(i, i ^ 1 << apart) for i in range(lax.axis_si...  3.09 us
  transfers between devices with their start and end apart: 6, of which 4 were waited for; matrix products, arithmetic and copies ran while one was open for 0% of the time, Pallas kernels for 13%

profile of v7, /device:TPU:0, one launch (start us, length us, event | category | flops | bytes accessed | tf_op | source)
XLA Modules:
  0.0 106.8 jit_solution(13295439127100480962)
XLA Ops:
  0.0 2.5 %shard_map.82 = (bf16[32,136,128]{2,1,0:T(8,128)(2,1)S(1)}, f32[8,128]{1,0:T(8,128)S(1)}, bf16[1024,1024]{1,0:T(8,128)(2,1)S(1)}, bf16[2,1024,256]{2,1,0:T(8,128)(2,1)S(1)}) custom-call(s32[1,1024]{1,0:T(1,128)} %bitcast.1, bf16[1024,256]{1,0:T(8,128)(2,1)} %rows_hbm.1, bf16[1,2,1024,1024]{3,2,1,0:T(8,128)(2,1)} %inverse_hbm.3, ...), custom_call_target="tpu_custom_call" | custom-call | tf_op jit(solution)/shard_map/pallas_call | solution.py:415
  2.5 36.5 %all_to_all.10.got_ref = bf16[32,136,128]{2,1,0:T(8,128)(2,1)S(1)} all-to-all(bf16[32,136,128]{2,1,0:T(8,128)(2,1)S(1)} %get-tuple-element.55), channel_id=1, replica_groups=mesh['row'=8,'col'=4] {'row','col'}, dimensions={0} | all-to-all | bytes 2228224 | tf_op jit(solution)/shard_map/all_to_all | solution.py:456
  39.0 1.7 %shard_map.83 = (bf16[1024,256]{1,0:T(8,128)(2,1)S(1)}, f32[128,128]{1,0:T(8,128)S(1)}, bf16[1024,1024]{1,0:T(8,128)(2,1)S(1)}, bf16[2,256,1024]{2,1,0:T(8,128)(2,1)S(1)}) custom-call(bf16[32,136,128]{2,1,0:T(8,128)(2,1)S(1)} %all_to_all.10.got_ref, bf16[1,2,1024,1024]{3,2,1,0:T(8,128)(2,1)} %inverse_hbm.3, bf16[2,1024,256]{2,1,0:T(8,128)(2,1)S(1)} %get-tuple-element.56.basis_ref), custom_call_target="tpu_custom_call" | custom-call | tf_op jit(solution)/shard_map/pallas_call | solution.py:415
  40.7 1.3 %shard_map.84.parts_ref.refs_4_ = bf16[1024,512]{1,0:T(8,128)(2,1)S(1)} custom-call(bf16[1024,256]{1,0:T(8,128)(2,1)S(1)} %get-tuple-element.57.placed_ref, bf16[1024,1024]{1,0:T(8,128)(2,1)S(1)} %get-tuple-element.58.real_ref, bf16[1024,1024]{1,0:T(8,128)(2,1)S(1)} %get-tuple-element.59.imag_ref), custom_call_target="tpu_custom_call" | custom-call | tf_op jit(solution)/shard_map/pallas_call | solution.py:415
  42.0 0.8 shard_map.85
  42.8 0.1 collective-permute-start
  42.8 1.6 %shard_map.86 = (bf16[2,512,512]{2,1,0:T(8,128)(2,1)S(1)}, bf16[2,256,512]{2,1,0:T(8,128)(2,1)S(1)}) custom-call(f32[256,128]{1,0:T(8,128)S(1)} %get-tuple-element.61.after_ref.own_ref, bf16[1,5,2,512,512]{4,3,2,1,0:T(8,128)(2,1)} %refs_0_.9, bf16[1,4,2,512,256]{4,3,2,1,0:T(8,128)(2,1)} %refs_1_.8), custom_call_target="tpu_custom_call" | custom-call | tf_op jit(solution)/shard_map/pallas_call | solution.py:415
  44.4 0.0 collective-permute-done.partner_ref
  44.4 0.8 shard_map.87
  45.2 0.7 collective-permute-start.1
  45.9 2.5 %shard_map.88 = (bf16[2,512,512]{2,1,0:T(8,128)(2,1)S(1)}, bf16[2,256,512]{2,1,0:T(8,128)(2,1)S(1)}, f32[512,128]{1,0:T(8,128)}, f32[1024,256]{1,0:T(8,128)}) custom-call(f32[256,128]{1,0:T(8,128)S(1)} %get-tuple-element.65.after_ref.own_ref.refs_8_, bf16[1,5,2,512,512]{4,3,2,1,0:T(8,128)(2,1)} %refs_0_.9, bf16[1,4,2,512,256]{4,3,2,1,0:T(8,128)(2,1)} %refs_1_.8, ...), custom_call_target="tpu_custom_call" | custom-call | tf_op jit(solution)/shard_map/pallas_call | solution.py:415
  48.4 1.4 %collective-permute-done.1.partner_ref = s16[272,128]{1,0:T(8,128)(2,1)S(1)} collective-permute-done((s16[272,128]{1,0:T(8,128)(2,1)S(1)}, s16[272,128]{1,0:T(8,128)(2,1)S(1)}, u32[]{:S(2)}, u32[]{:S(2)}) %collective-permute-start.1) | collective-permute-done | bytes 69664 | tf_op jit(solution)/shard_map/ppermute | solution.py:439
  49.9 0.8 shard_map.89
  50.7 0.7 collective-permute-start.2
  51.3 2.5 %shard_map.90 = (bf16[2,512,512]{2,1,0:T(8,128)(2,1)S(1)}, bf16[2,256,512]{2,1,0:T(8,128)(2,1)S(1)}, f32[512,128]{1,0:T(8,128)}, f32[1024,256]{1,0:T(8,128)}) custom-call(f32[256,128]{1,0:T(8,128)S(1)} %get-tuple-element.71.after_ref.own_ref.refs_9_, bf16[1,5,2,512,512]{4,3,2,1,0:T(8,128)(2,1)} %refs_0_.9, bf16[1,4,2,512,256]{4,3,2,1,0:T(8,128)(2,1)} %refs_1_.8, ...), custom_call_target="tpu_custom_call" | custom-call | tf_op jit(solution)/shard_map/pallas_call | solution.py:415
  53.9 1.2 %collective-permute-done.2.partner_ref = s16[272,128]{1,0:T(8,128)(2,1)S(1)} collective-permute-done((s16[272,128]{1,0:T(8,128)(2,1)S(1)}, s16[272,128]{1,0:T(8,128)(2,1)S(1)}, u32[]{:S(2)}, u32[]{:S(2)}) %collective-permute-start.2) | collective-permute-done | bytes 69664 | tf_op jit(solution)/shard_map/ppermute | solution.py:439
  55.0 0.8 shard_map.91
  55.8 0.7 collective-permute-start.3
  56.5 3.3 %shard_map.92 = (bf16[2,512,512]{2,1,0:T(8,128)(2,1)S(1)}, bf16[2,256,512]{2,1,0:T(8,128)(2,1)S(1)}, f32[512,128]{1,0:T(8,128)}, bf16[768,512]{1,0:T(8,128)(2,1)}) custom-call(f32[256,128]{1,0:T(8,128)S(1)} %get-tuple-element.76.after_ref.own_ref.refs_10_, bf16[1,5,2,512,512]{4,3,2,1,0:T(8,128)(2,1)} %refs_0_.9, bf16[1,4,2,512,256]{4,3,2,1,0:T(8,128)(2,1)} %refs_1_.8, ...), custom_call_target="tpu_custom_call" | custom-call | tf_op jit(solution)/shard_map/pallas_call | solution.py:415
  59.8 0.4 collective-permute-done.3.partner_ref
  60.2 0.8 shard_map.93
  61.0 1.0 collective-permute-start.4
  62.0 2.8 %shard_map.94 = (bf16[2,256,512]{2,1,0:T(8,128)(2,1)S(1)}, bf16[2,512,256]{2,1,0:T(8,128)(2,1)S(1)}, bf16[2,256,256]{2,1,0:T(8,128)(2,1)S(1)}, bf16[2,256,256]{2...) custom-call(f32[256,128]{1,0:T(8,128)S(1)} %get-tuple-element.81.aft, ...), custom_call_target="tpu_custom_call" | custom-call | tf_op jit(solution)/shard_map/pallas_call | solution.py:415
  64.8 2.2 %collective-permute-done.4.partner_ref = s16[272,128]{1,0:T(8,128)(2,1)S(1)} collective-permute-done((s16[272,128]{1,0:T(8,128)(2,1)S(1)}, s16[272,128]{1,0:T(8,128)(2,1)S(1)}, u32[]{:S(2)}, u32[]{:S(2)}) %collective-permute-start.4) | collective-permute-done | bytes 69664 | tf_op jit(solution)/shard_map/ppermute | solution.py:439
  67.0 1.5 %shard_map.95 = (f32[256,128]{1,0:T(8,128)S(1)}, f32[256,128]{1,0:T(8,128)S(1)}, bf16[768,512]{1,0:T(8,128)(2,1)S(1)}) custom-call(f32[256,128]{1,0:T(8,128)S(1)} %get-tuple-element.81.after_ref.own_ref.refs_11_, s16[272,128]{1,0:T(8,128)(2,1)S(1)} %collective-permute-done.4.partner_ref, bf16[2,256,512]{2,1,0:T(8,128)(2,1)S(1)} %get-tuple-element.86.inverse_ref, ...), custom_call_target="tpu_custom_call" | custom-call | tf_op jit(solution)/shard_map/pallas_call | solution.py:415
  68.5 0.1 collective-permute-start.5
  68.6 1.6 %shard_map.96 = (f32[1024,256]{1,0:T(8,128)S(1)}, f32[1024,256]{1,0:T(8,128)S(1)}) custom-call(f32[256,128]{1,0:T(8,128)S(1)} %get-tuple-element.97.after_ref, f32[1024,256]{1,0:T(8,128)} %get-tuple-element.100.refs_0_, f32[1024,256]{1,0:T(8,128)} %get-tuple-element.101.refs_1_), custom_call_target="tpu_custom_call" | custom-call | tf_op jit(solution)/shard_map/pallas_call | solution.py:415
  70.2 0.0 collective-permute-done.5.others_ref
  70.2 1.9 %shard_map.97 = s16[32,136,128]{2,1,0:T(8,128)(2,1)S(1)} custom-call(f32[256,128]{1,0:T(8,128)S(1)} %get-tuple-element.96.mine_ref, f32[256,128]{1,0:T(8,128)S(1)} %collective-permute-done.5.others_ref, f32[256,128]{1,0:T(8,128)S(1)} %get-tuple-element.61.after_ref.own_ref, f32[256,128]{1,0:T(8,128)S(1)} %get-tuple-element.62.other_ref, ...), custom_call_target="tpu_custom_call" | custom-call | tf_op jit(solution)/shard_map/pallas_call | solution.py:415
  72.1 31.2 %all_to_all.11.got_ref = s16[32,136,128]{2,1,0:T(8,128)(2,1)S(1)} all-to-all(s16[32,136,128]{2,1,0:T(8,128)(2,1)S(1)} %shard_map.97), channel_id=1, replica_groups=mesh['row'=8,'col'=4] {'row','col'}, dimensions={0} | all-to-all | bytes 2228224 | tf_op jit(solution)/shard_map/all_to_all | solution.py:456
  103.2 3.4 %shard_map.98 = f32[1024,256]{1,0:T(8,128)} custom-call(s16[32,136,128]{2,1,0:T(8,128)(2,1)S(1)} %all_to_all.11.got_ref, f32[8,128]{1,0:T(8,128)S(1)} %get-tuple-element.104.slot_ref), custom_call_target="tpu_custom_call" | custom-call | tf_op jit(solution)/shard_map/pallas_call | solution.py:415
Async XLA Ops:
  42.8 1.7 %collective-permute-start = (f32[256,128]{1,0:T(8,128)S(1)}, f32[256,128]{1,0:T(8,128)S(1)}, u32[]{:S(2)}, u32[]{:S(2)}) collective-permute-start(f32[256,128]{1,0:T(8,128)S(1)} %get-tuple-element.62.other_ref), channel_id=1, source_target_pairs={{0,1},{1,0},{2,3},{3,2},{4,5},{5,4},{6,7},{7,6},{8,9},{9,8},{10,11... | collective-permute-start | bytes 393224 | tf_op jit(solution)/shard_map/ppermute | solution.py:439
  45.2 4.6 %collective-permute-start.1 = (s16[272,128]{1,0:T(8,128)(2,1)S(1)}, s16[272,128]{1,0:T(8,128)(2,1)S(1)}, u32[]{:S(2)}, u32[]{:S(2)}) collective-permute-start(s16[272,128]{1,0:T(8,128)(2,1)S(1)} %get-tuple-element.66), channel_id=1, source_target_pairs={{0,2},{1,3},{2,0},{3,1},{4,6},{5,7},{6,4},{7,5},{8,10},{9,11},{10,... | collective-permute-start | bytes 208904 | tf_op jit(solution)/shard_map/ppermute | solution.py:439
  50.7 4.4 %collective-permute-start.2 = (s16[272,128]{1,0:T(8,128)(2,1)S(1)}, s16[272,128]{1,0:T(8,128)(2,1)S(1)}, u32[]{:S(2)}, u32[]{:S(2)}) collective-permute-start(s16[272,128]{1,0:T(8,128)(2,1)S(1)} %get-tuple-element.72), channel_id=1, source_target_pairs={{0,4},{4,0},{8,12},{12,8},{16,20},{20,16},{24,28},{28,24},{1,5},{5... | collective-permute-start | bytes 208904 | tf_op jit(solution)/shard_map/ppermute | solution.py:439
  55.8 4.4 %collective-permute-start.3 = (s16[272,128]{1,0:T(8,128)(2,1)S(1)}, s16[272,128]{1,0:T(8,128)(2,1)S(1)}, u32[]{:S(2)}, u32[]{:S(2)}) collective-permute-start(s16[272,128]{1,0:T(8,128)(2,1)S(1)} %get-tuple-element.77), channel_id=1, source_target_pairs={{0,8},{4,12},{8,0},{12,4},{16,24},{20,28},{24,16},{28,20},{1,9},{5... | collective-permute-start | bytes 208904 | tf_op jit(solution)/shard_map/ppermute | solution.py:439
  61.0 6.0 %collective-permute-start.4 = (s16[272,128]{1,0:T(8,128)(2,1)S(1)}, s16[272,128]{1,0:T(8,128)(2,1)S(1)}, u32[]{:S(2)}, u32[]{:S(2)}) collective-permute-start(s16[272,128]{1,0:T(8,128)(2,1)S(1)} %get-tuple-element.82), channel_id=1, source_target_pairs={{0,16},{4,20},{8,24},{12,28},{16,0},{20,4},{24,8},{28,12},{1,17},{... | collective-permute-start | bytes 208904 | tf_op jit(solution)/shard_map/ppermute | solution.py:439
  68.5 1.7 %collective-permute-start.5 = (f32[256,128]{1,0:T(8,128)S(1)}, f32[256,128]{1,0:T(8,128)S(1)}, u32[]{:S(2)}, u32[]{:S(2)}) collective-permute-start(f32[256,128]{1,0:T(8,128)S(1)} %get-tuple-element.97.after_ref), channel_id=1, source_target_pairs={{0,1},{1,0},{2,3},{3,2},{4,5},{5,4},{6,7},{7,6},{8,9},{9,8},{10,11... | collective-permute-start | bytes 393224 | tf_op jit(solution)/shard_map/ppermute | solution.py:439

commit v8 on v7

--- a/solution.py
+++ b/solution.py
@@ -20,6 +20,7 @@
 FINISH_PIECES = 8
 BF16 = jnp.bfloat16
 F32 = jnp.float32
+F8 = jnp.float8_e4m3fn
 
 
 def whole_matmul(a, b):
@@ -200,7 +201,7 @@
     return [sum(extra[k + g] for g in range(group)) for k in range(0, devices, group)]
 
 
-def load_kernel(after_ref, *refs, picks, turned, stores, rows_of, groups, kept, levels):
+def load_kernel(after_ref, *refs, picks, turned, stores, rows_of, groups, kept, levels, height):
     refs = list(refs)
 
     def take(count):
@@ -212,7 +213,7 @@
     plain = count - turned
     gathers = 1 if rows_of else 0
     sources, stored, given = take(count), take(stores), take(2 * gathers)
-    targets, held, gathered = take(count), take(stores), take(gathers)
+    targets, held, gathered, early = take(count), take(stores), take(gathers), take(height > 0)
     scratch, chosen, landed = take(turned), take(gathers), take(rows_of == "lift")
     work, (sem,) = take(gathers and not kept), refs
     landing = targets[:plain] + scratch
@@ -246,13 +247,22 @@
             out_ref[...] = folded(matmul(chosen_ref[...], given[1][...]))
         if not kept:
             copies.append(fetch(out_ref, gathered[0], sem.at[count + stores + 1]))
+    if early:
+        copies[0].wait()
+        early[0][...] = half_product(targets[0], tree_bits(height)[-1], after_ref[...])
     for k in range(turned):
         copies[plain + k].wait()
         for part in range(2):
             targets[plain + k][part] = jnp.transpose(scratch[k][part])
     for k, copy in enumerate(copies):
-        if not plain <= k < count:
+        if not plain <= k < count and not (early and k == 0):
             copy.wait()
+
+
+def half_product(inverse_ref, upper, half):
+    rank = half.shape[0]
+    columns = pl.ds(pl.multiple_of(upper * rank, rank), rank)
+    return apply_complex(inverse_ref[0, :, columns], inverse_ref[1, :, columns], half, NODE_STEP)
 
 
 def place_columns(place_ref, groups):
@@ -288,9 +298,11 @@
     imag_copy.wait()
 
 
-def leaf_kernel(placed_ref, real_ref, imag_ref, parts_ref):
+def leaf_kernel(placed_ref, real_ref, imag_ref, inverse_hbm, parts_ref, inverse_ref, sem):
+    copy = fetch(inverse_hbm.at[0, 0], inverse_ref, sem.at[0])
     placed = placed_ref[...]
     parts_ref[...] = two_parts(matmul(real_ref[...], placed) + matmul(imag_ref[...], rotated(placed)))
+    copy.wait()
 
 
 def coef_kernel(parts_ref, basis_ref, own_ref, other_ref):
@@ -312,9 +324,12 @@
 
 
 def node_kernel(own_ref, partner_ref, inverse_ref, basis_ref, sol_ref, coef_ref, code_ref, *, height):
-    partner = partner_ref[...]
-    rhs = node_rhs(tree_bits(height)[-1], own_ref[...], partner if partner.dtype == F32 else decoded(partner))
-    sol = apply_complex(inverse_ref[0], inverse_ref[1], rhs, NODE_STEP)
+    bit = tree_bits(height)[-1]
+    if height == 1:
+        rhs = node_rhs(bit, own_ref[...], partner_ref[...])
+        sol = apply_complex(inverse_ref[0], inverse_ref[1], rhs, NODE_STEP)
+    else:
+        sol = own_ref[...] + half_product(inverse_ref, 1 - bit, decoded(partner_ref[...]))
     sol_ref[...] = sol
     coef = apply_complex(basis_ref[0], basis_ref[1], sol, NODE_STEP)
     coef_ref[...] = coef
@@ -328,8 +343,7 @@
     moved_hbm, mine_ref, other_ref, moved_ref, sem = refs[3 * below :]
     moved_copy = fetch(moved_hbm, moved_ref, sem.at[0])
     rank = own_ref.shape[0]
-    rhs = node_rhs(bits[below], own_ref[...], decoded(partner_ref[...]))
-    down = apply_complex(inverse_ref[0], inverse_ref[1], rhs)
+    down = own_ref[...] + half_product(inverse_ref, 1 - bits[below], decoded(partner_ref[...]))
     for k in range(below - 1, -1, -1):
         gap = coefs[k][...] - down
         if k == below - 1:
@@ -390,17 +404,25 @@
     turned = jnp.transpose(slot_ref[...])
     chosen = wide_one_hot([turned[:, k : k + 1] for k in range(turned.shape[1])], slots // LANES)
     extra = from_int16(got_ref[:, 2 * capacity :, :])
-    halves = []
+    unit = unit_of(extra)
+    unit = jnp.concatenate([unit[:, :1, :], unit[:, EXTRA // 2 : EXTRA // 2 + 1, :]], axis=2)
+    largest = jnp.max(unit, axis=0)
+    inverse = 1.0 / largest
+    highs, lows = [], []
     for half in range(2):
+        lanes = slice(half * LANES, (half + 1) * LANES)
         level = from_int16(got_ref[:, half * capacity : (half + 1) * capacity, :])
-        unit = unit_of(extra[:, half * (EXTRA // 2) : half * (EXTRA // 2) + 1, :])
-        halves.append((level * unit).reshape(slots, LANES))
-    parts = two_parts(jnp.concatenate(halves, axis=1))
+        value = (level * unit[:, :, lanes]).reshape(slots, LANES)
+        high = value.astype(BF16)
+        highs.append(high)
+        lows.append(((value - high.astype(F32)) * inverse[:, lanes]).astype(F8))
+    high, low = jnp.concatenate(highs, axis=1), jnp.concatenate(lows, axis=1)
     count = out_ref.shape[0] // PIECES
     copies = []
     for piece in range(PIECES):
         rows = pl.ds(piece * count, count)
-        out_ref[rows, :] = folded(whole_matmul(chosen[piece * count : (piece + 1) * count], parts))
+        some = chosen[piece * count : (piece + 1) * count]
+        out_ref[rows, :] = whole_matmul(some, high) + whole_matmul(some.astype(F8), low) * largest
         copies.append(fetch(out_ref.at[rows], out_hbm.at[rows], sem.at[piece]))
     for copy in copies:
         copy.wait()
@@ -486,7 +508,7 @@
         levels: ("lift", (3 * total // 8, total), True),
     }
 
-    def load(after, weights, picks, turned=0, stores=(), gather=("", (0, 0), False)):
+    def load(after, weights, picks, turned=0, stores=(), gather=("", (0, 0), False), height=0):
         shapes = [
             jax.eval_shape(
                 lambda w, pick=pick: w[tuple(slice(0, rank) if isinstance(p, tuple) else p for p in pick)], w
@@ -517,11 +539,13 @@
                 groups=groups,
                 kept=kept,
                 levels=levels,
+                height=height,
             ),
             [(out, "vmem") for out in outs]
             + [(shape(one.shape), "hbm") for one in stores]
-            + [(one, "vmem" if kept else "hbm") for one in taken],
-            [(after, "any")]
+            + [(one, "vmem" if kept else "hbm") for one in taken]
+            + ([(shape((shapes[0].shape[1], LANES)), "vmem")] if height else []),
+            [(after, "vmem" if height else "any")]
             + [(weight, "hbm") for weight in weights]
             + [(one, "any") for one in stores]
             + given[rows_of],
@@ -545,10 +569,11 @@
         [(got, "vmem"), (leaf_inverse, "hbm"), (basis, "vmem")],
         [shape((leaf_rows, slots), BF16), shape((slots, width), BF16), 1],
     )
-    (parts,) = call(
+    parts, lowest = call(
         leaf_kernel,
-        [(shape((leaf_rows, 2 * width), BF16), "vmem")],
-        [(placed, "vmem"), (real, "vmem"), (imag, "vmem")],
+        [(shape((leaf_rows, 2 * width), BF16), "vmem"), (shape(node_inverse.shape[2:], BF16), "vmem")],
+        [(placed, "vmem"), (real, "vmem"), (imag, "vmem"), (node_inverse, "hbm")],
+        [1],
     )
     own, other = call(
         coef_kernel,
@@ -562,16 +587,25 @@
     for height in range(1, levels):
         partner = partner_of(other if height == 1 else code, height - 1)
         pick = (0, height - 1)
-        inverse, basis, *kept = load(
-            own, (node_inverse, node_basis), (pick, pick), 1, sols[-1:], gathers.get(height, no_gather)
+        first = height == 1
+        loaded = load(
+            own,
+            (node_basis,) if first else (node_inverse, node_basis),
+            (pick,) if first else (pick, pick),
+            1,
+            sols[-1:],
+            gathers.get(height, no_gather),
+            0 if first else height,
         )
+        (inverse, basis, *kept) = (lowest, *loaded) if first else loaded
+        early = own if first else kept.pop()
         stored += kept[: len(sols[-1:])]
         gathered += kept[len(sols[-1:]) :]
         sol, own, code = call(
             functools.partial(node_kernel, height=height),
             [(whole, "vmem"), (half, "vmem"), (shape((rank + TAIL, LANES), jnp.int16), "vmem")],
             [
-                (own, "vmem"),
+                (early, "vmem"),
                 (partner, "vmem"),
                 (inverse, "vmem"),
                 (basis, "vmem"),
@@ -592,7 +626,9 @@
             *((("half", k),) for k in range(1, levels - 2)),
         ),
         gather=gathers[levels],
-    )
+        height=levels,
+    )
+    *loaded, early = loaded
     inverse, lifts, sols = loaded[0], loaded[1:levels], [*loaded[levels:-1], sols[-1]]
     gathered.append(loaded[-1])
     mine, other, moved = call(
@@ -602,7 +638,7 @@
             (half, "vmem"),
             (shape(gathered[2].shape, BF16), "vmem"),
         ],
-        [(own, "vmem"), (partner, "vmem"), (inverse, "vmem")]
+        [(early, "vmem"), (partner, "vmem"), (inverse, "vmem")]
         + [(lift, "vmem") for lift in lifts]
         + [(sol, "vmem") for sol in sols]
         + [(coef, "vmem") for coef in coefs]

time: 107 us -> 106 us (level)
  transfers between devices with their start and end apart: 6 -> 6, of which waited for: 4 -> 5; matrix products, arithmetic and copies ran while one was open for 0% -> 0% of each run, Pallas kernels for 13% -> 13%
where the time goes in v8:
time: 106 us
  blocking collectives  67.6 us (64%)
  Pallas kernels  29.8 us (28%)
  waiting for transfers between devices  5.07 us (5%)
  starting transfers between devices  3.02 us (3%)
    all_to_all x2, blocking collectives, exchange(): lax.all_to_all(blocks, ('row', 'col'), split_axis=0, concat_axis=0, tiled...  67.6 us
    pallas_call x17, Pallas kernels, call(): pl.pallas_call(kernel, out_shape=[pltpu.HBM(out.shape, out.dtype) if spac...  29.8 us
    ppermute x6, waiting for transfers between devices, from_partner(): lax.ppermute(shard, axis, [(i, i ^ 1 << apart) for i in range(lax.axis_si...  5.07 us
    ppermute x6, starting transfers between devices, from_partner(): lax.ppermute(shard, axis, [(i, i ^ 1 << apart) for i in range(lax.axis_si...  3.02 us
  transfers between devices with their start and end apart: 6, of which 5 were waited for; matrix products, arithmetic and copies ran while one was open for 0% of the time, Pallas kernels for 13%

profile of v8, /device:TPU:0, one launch (start us, length us, event | category | flops | bytes accessed | tf_op | source)
XLA Modules:
  0.0 105.9 jit_solution(3274154990827034017)
XLA Ops:
  0.0 2.5 %shard_map.82 = (bf16[32,136,128]{2,1,0:T(8,128)(2,1)S(1)}, f32[8,128]{1,0:T(8,128)S(1)}, bf16[1024,1024]{1,0:T(8,128)(2,1)S(1)}, bf16[2,1024,256]{2,1,0:T(8,128)(2,1)S(1)}) custom-call(s32[1,1024]{1,0:T(1,128)} %bitcast.1, bf16[1024,256]{1,0:T(8,128)(2,1)} %rows_hbm.1, bf16[1,2,1024,1024]{3,2,1,0:T(8,128)(2,1)} %inverse_hbm.4, ...), custom_call_target="tpu_custom_call" | custom-call | tf_op jit(solution)/shard_map/pallas_call | solution.py:437
  2.5 36.5 %all_to_all.10.got_ref = bf16[32,136,128]{2,1,0:T(8,128)(2,1)S(1)} all-to-all(bf16[32,136,128]{2,1,0:T(8,128)(2,1)S(1)} %get-tuple-element.59), channel_id=1, replica_groups=mesh['row'=8,'col'=4] {'row','col'}, dimensions={0} | all-to-all | bytes 2228224 | tf_op jit(solution)/shard_map/all_to_all | solution.py:478
  39.0 1.7 %shard_map.83 = (bf16[1024,256]{1,0:T(8,128)(2,1)S(1)}, f32[128,128]{1,0:T(8,128)S(1)}, bf16[1024,1024]{1,0:T(8,128)(2,1)S(1)}, bf16[2,256,1024]{2,1,0:T(8,128)(2,1)S(1)}) custom-call(bf16[32,136,128]{2,1,0:T(8,128)(2,1)S(1)} %all_to_all.10.got_ref, bf16[1,2,1024,1024]{3,2,1,0:T(8,128)(2,1)} %inverse_hbm.4, bf16[2,1024,256]{2,1,0:T(8,128)(2,1)S(1)} %get-tuple-element.60.basis_ref), custom_call_target="tpu_custom_call" | custom-call | tf_op jit(solution)/shard_map/pallas_call | solution.py:437
  40.7 1.3 %shard_map.84 = (bf16[1024,512]{1,0:T(8,128)(2,1)S(1)}, bf16[2,512,512]{2,1,0:T(8,128)(2,1)S(1)}) custom-call(bf16[1024,256]{1,0:T(8,128)(2,1)S(1)} %get-tuple-element.61.placed_ref, bf16[1024,1024]{1,0:T(8,128)(2,1)S(1)} %get-tuple-element.62.real_ref, bf16[1024,1024]{1,0:T(8,128)(2,1)S(1)} %get-tuple-element.63.imag_ref, bf16[1,5,2,512,512]{4,3,2,1,0:T(8,128)(2,1)} %refs_0_.9), custom_call_target="tpu_custom_call" | custom-call | tf_op jit(solution)/shard_map/pallas_call | solution.py:437
  42.0 0.8 shard_map.85
  42.8 0.1 collective-permute-start
  42.9 1.2 %shard_map.86.basis_ref = bf16[2,256,512]{2,1,0:T(8,128)(2,1)S(1)} custom-call(f32[256,128]{1,0:T(8,128)S(1)} %get-tuple-element.66.after_ref.own_ref, bf16[1,4,2,512,256]{4,3,2,1,0:T(8,128)(2,1)} %refs_1_.6), custom_call_target="tpu_custom_call" | custom-call | tf_op jit(solution)/shard_map/pallas_call | solution.py:437
  44.1 0.1 collective-permute-done.partner_ref
  44.2 0.8 shard_map.87
  45.0 0.6 collective-permute-start.1
  45.6 2.5 %shard_map.88 = (bf16[2,512,512]{2,1,0:T(8,128)(2,1)S(1)}, bf16[2,256,512]{2,1,0:T(8,128)(2,1)S(1)}, f32[512,128]{1,0:T(8,128)}, f32[1024,256]{1,0:T(8,128)}, f32[512,128]{1,0:T(8,128)S(1)}) custom-call(f32[256,128]{1,0:T(8,128)S(1)} %get-tuple-element.69.after_ref.refs_8_, bf16[1,5,2,512,512]{4,3,2,1,0:T(8,128)(2,1)} %refs_0_.9, ...), custom_call_target="tpu_custom_call" | custom-call | tf_op jit(solution)/shard_map/pallas_call | solution.py:437
  48.1 1.4 %collective-permute-done.1.partner_ref = s16[272,128]{1,0:T(8,128)(2,1)S(1)} collective-permute-done((s16[272,128]{1,0:T(8,128)(2,1)S(1)}, s16[272,128]{1,0:T(8,128)(2,1)S(1)}, u32[]{:S(2)}, u32[]{:S(2)}) %collective-permute-start.1) | collective-permute-done | bytes 69664 | tf_op jit(solution)/shard_map/ppermute | solution.py:461
  49.6 0.7 shard_map.89
  50.3 0.6 collective-permute-start.2
  50.9 2.5 %shard_map.90 = (bf16[2,512,512]{2,1,0:T(8,128)(2,1)S(1)}, bf16[2,256,512]{2,1,0:T(8,128)(2,1)S(1)}, f32[512,128]{1,0:T(8,128)}, f32[1024,256]{1,0:T(8,128)}, f32[512,128]{1,0:T(8,128)S(1)}) custom-call(f32[256,128]{1,0:T(8,128)S(1)} %get-tuple-element.76.after_ref.refs_9_, bf16[1,5,2,512,512]{4,3,2,1,0:T(8,128)(2,1)} %refs_0_.9, ...), custom_call_target="tpu_custom_call" | custom-call | tf_op jit(solution)/shard_map/pallas_call | solution.py:437
  53.5 1.2 %collective-permute-done.2.partner_ref = s16[272,128]{1,0:T(8,128)(2,1)S(1)} collective-permute-done((s16[272,128]{1,0:T(8,128)(2,1)S(1)}, s16[272,128]{1,0:T(8,128)(2,1)S(1)}, u32[]{:S(2)}, u32[]{:S(2)}) %collective-permute-start.2) | collective-permute-done | bytes 69664 | tf_op jit(solution)/shard_map/ppermute | solution.py:461
  54.7 0.7 shard_map.91
  55.4 0.7 collective-permute-start.3
  56.1 3.3 %shard_map.92 = (bf16[2,512,512]{2,1,0:T(8,128)(2,1)S(1)}, bf16[2,256,512]{2,1,0:T(8,128)(2,1)S(1)}, f32[512,128]{1,0:T(8,128)}, bf16[768,512]{1,0:T(8,128)(2,1)}, f32[512,128]{1,0:T(8,128)S(1)}) custom-call(f32[256,128]{1,0:T(8,128)S(1)} %get-tuple-element.82.after_ref.refs_10_, bf16[1,5,2,512,512]{4,3,2,1,0:T(8,128)(2,1)} %refs_0_.9, ...), custom_call_target="tpu_custom_call" | custom-call | tf_op jit(solution)/shard_map/pallas_call | solution.py:437
  59.3 0.4 collective-permute-done.3.partner_ref
  59.8 0.7 shard_map.93
  60.5 1.0 collective-permute-start.4
  61.4 3.1 %shard_map.94 = (bf16[2,256,512]{2,1,0:T(8,128)(2,1)S(1)}, bf16[2,512,256]{2,1,0:T(8,128)(2,1)S(1)}, bf16[2,256,256]{2,1,0:T(8,128)(2,1)S(1)}, bf16[2,256,256]{2...) custom-call(f32[256,128]{1,0:T(8,128)S(1)} %get-tuple-element.88.aft, ...), custom_call_target="tpu_custom_call" | custom-call | tf_op jit(solution)/shard_map/pallas_call | solution.py:437
  64.6 1.9 %collective-permute-done.4.partner_ref = s16[272,128]{1,0:T(8,128)(2,1)S(1)} collective-permute-done((s16[272,128]{1,0:T(8,128)(2,1)S(1)}, s16[272,128]{1,0:T(8,128)(2,1)S(1)}, u32[]{:S(2)}, u32[]{:S(2)}) %collective-permute-start.4) | collective-permute-done | bytes 69664 | tf_op jit(solution)/shard_map/ppermute | solution.py:461
  66.5 1.5 %shard_map.95 = (f32[256,128]{1,0:T(8,128)S(1)}, f32[256,128]{1,0:T(8,128)S(1)}, bf16[768,512]{1,0:T(8,128)(2,1)S(1)}) custom-call(f32[256,128]{1,0:T(8,128)S(1)} %get-tuple-element.92.own_ref, s16[272,128]{1,0:T(8,128)(2,1)S(1)} %collective-permute-done.4.partner_ref, bf16[2,256,512]{2,1,0:T(8,128)(2,1)S(1)} %get-tuple-element.94.inverse_ref, ...), custom_call_target="tpu_custom_call" | custom-call | tf_op jit(solution)/shard_map/pallas_call | solution.py:437
  68.0 0.1 collective-permute-start.5
  68.1 1.6 %shard_map.96 = (f32[1024,256]{1,0:T(8,128)S(1)}, f32[1024,256]{1,0:T(8,128)S(1)}) custom-call(f32[256,128]{1,0:T(8,128)S(1)} %get-tuple-element.105.after_ref, f32[1024,256]{1,0:T(8,128)} %get-tuple-element.108.refs_0_, f32[1024,256]{1,0:T(8,128)} %get-tuple-element.109.refs_1_), custom_call_target="tpu_custom_call" | custom-call | tf_op jit(solution)/shard_map/pallas_call | solution.py:437
  69.7 0.0 collective-permute-done.5.others_ref
  69.7 1.9 %shard_map.97 = s16[32,136,128]{2,1,0:T(8,128)(2,1)S(1)} custom-call(f32[256,128]{1,0:T(8,128)S(1)} %get-tuple-element.104.mine_ref, f32[256,128]{1,0:T(8,128)S(1)} %collective-permute-done.5.others_ref, f32[256,128]{1,0:T(8,128)S(1)} %get-tuple-element.66.after_ref.own_ref, f32[256,128]{1,0:T(8,128)S(1)} %get-tuple-element.67.other_ref, ...), custom_call_target="tpu_custom_call" | custom-call | tf_op jit(solution)/shard_map/pallas_call | solution.py:437
  71.6 31.2 %all_to_all.11.got_ref = s16[32,136,128]{2,1,0:T(8,128)(2,1)S(1)} all-to-all(s16[32,136,128]{2,1,0:T(8,128)(2,1)S(1)} %shard_map.97), channel_id=1, replica_groups=mesh['row'=8,'col'=4] {'row','col'}, dimensions={0} | all-to-all | bytes 2228224 | tf_op jit(solution)/shard_map/all_to_all | solution.py:478
  102.7 3.0 %shard_map.98 = f32[1024,256]{1,0:T(8,128)} custom-call(s16[32,136,128]{2,1,0:T(8,128)(2,1)S(1)} %all_to_all.11.got_ref, f32[8,128]{1,0:T(8,128)S(1)} %get-tuple-element.112.slot_ref), custom_call_target="tpu_custom_call" | custom-call | tf_op jit(solution)/shard_map/pallas_call | solution.py:437
Async XLA Ops:
  42.8 1.4 %collective-permute-start = (f32[256,128]{1,0:T(8,128)S(1)}, f32[256,128]{1,0:T(8,128)S(1)}, u32[]{:S(2)}, u32[]{:S(2)}) collective-permute-start(f32[256,128]{1,0:T(8,128)S(1)} %get-tuple-element.67.other_ref), channel_id=1, source_target_pairs={{0,1},{1,0},{2,3},{3,2},{4,5},{5,4},{6,7},{7,6},{8,9},{9,8},{10,11... | collective-permute-start | bytes 393224 | tf_op jit(solution)/shard_map/ppermute | solution.py:461
  45.0 4.6 %collective-permute-start.1 = (s16[272,128]{1,0:T(8,128)(2,1)S(1)}, s16[272,128]{1,0:T(8,128)(2,1)S(1)}, u32[]{:S(2)}, u32[]{:S(2)}) collective-permute-start(s16[272,128]{1,0:T(8,128)(2,1)S(1)} %get-tuple-element.73), channel_id=1, source_target_pairs={{0,2},{1,3},{2,0},{3,1},{4,6},{5,7},{6,4},{7,5},{8,10},{9,11},{10,... | collective-permute-start | bytes 208904 | tf_op jit(solution)/shard_map/ppermute | solution.py:461
  50.3 4.4 %collective-permute-start.2 = (s16[272,128]{1,0:T(8,128)(2,1)S(1)}, s16[272,128]{1,0:T(8,128)(2,1)S(1)}, u32[]{:S(2)}, u32[]{:S(2)}) collective-permute-start(s16[272,128]{1,0:T(8,128)(2,1)S(1)} %get-tuple-element.79), channel_id=1, source_target_pairs={{0,4},{4,0},{8,12},{12,8},{16,20},{20,16},{24,28},{28,24},{1,5},{5... | collective-permute-start | bytes 208904 | tf_op jit(solution)/shard_map/ppermute | solution.py:461
  55.4 4.4 %collective-permute-start.3 = (s16[272,128]{1,0:T(8,128)(2,1)S(1)}, s16[272,128]{1,0:T(8,128)(2,1)S(1)}, u32[]{:S(2)}, u32[]{:S(2)}) collective-permute-start(s16[272,128]{1,0:T(8,128)(2,1)S(1)} %get-tuple-element.85), channel_id=1, source_target_pairs={{0,8},{4,12},{8,0},{12,4},{16,24},{20,28},{24,16},{28,20},{1,9},{5... | collective-permute-start | bytes 208904 | tf_op jit(solution)/shard_map/ppermute | solution.py:461
  60.5 6.0 %collective-permute-start.4 = (s16[272,128]{1,0:T(8,128)(2,1)S(1)}, s16[272,128]{1,0:T(8,128)(2,1)S(1)}, u32[]{:S(2)}, u32[]{:S(2)}) collective-permute-start(s16[272,128]{1,0:T(8,128)(2,1)S(1)} %get-tuple-element.93), channel_id=1, source_target_pairs={{0,16},{4,20},{8,24},{12,28},{16,0},{20,4},{24,8},{28,12},{1,17},{... | collective-permute-start | bytes 208904 | tf_op jit(solution)/shard_map/ppermute | solution.py:461
  68.0 1.7 %collective-permute-start.5 = (f32[256,128]{1,0:T(8,128)S(1)}, f32[256,128]{1,0:T(8,128)S(1)}, u32[]{:S(2)}, u32[]{:S(2)}) collective-permute-start(f32[256,128]{1,0:T(8,128)S(1)} %get-tuple-element.105.after_ref), channel_id=1, source_target_pairs={{0,1},{1,0},{2,3},{3,2},{4,5},{5,4},{6,7},{7,6},{8,9},{9,8},{10,11... | collective-permute-start | bytes 393224 | tf_op jit(solution)/shard_map/ppermute | solution.py:461

commit v9 on v8

--- a/solution.py
+++ b/solution.py
@@ -340,8 +340,7 @@
     below = levels - 1
     bits = tree_bits(levels)
     lifts, sols, coefs = refs[:below], refs[below : 2 * below], refs[2 * below : 3 * below]
-    moved_hbm, mine_ref, other_ref, moved_ref, sem = refs[3 * below :]
-    moved_copy = fetch(moved_hbm, moved_ref, sem.at[0])
+    mine_ref, other_ref = refs[3 * below :]
     rank = own_ref.shape[0]
     down = own_ref[...] + half_product(inverse_ref, 1 - bits[below], decoded(partner_ref[...]))
     for k in range(below - 1, -1, -1):
@@ -354,7 +353,6 @@
     swap = bits[0] == 1
     mine_ref[...] = jnp.where(swap, down[rank:], down[:rank])
     other_ref[...] = jnp.where(swap, down[:rank], down[rank:])
-    moved_copy.wait()
 
 
 def rows_of(refs, rows):
@@ -382,7 +380,7 @@
     count = devices // FINISH_PIECES
     for at in range(0, devices, count):
         rows = slice(at * capacity, (at + count) * capacity)
-        sol = rows_of(pieces, rows) - folded(matmul(rows_of(moved, rows), parts))
+        sol = rows_of(pieces, rows) - folded(matmul(rows_of(moved, rows), parts, NODE_STEP))
         code = scale_code(sol)
         level = to_int16(rounded(sol * inverse_unit_of(code)))
         blocks = slice(at, at + count)
@@ -504,7 +502,7 @@
     gathers = {
         levels - 3: ("sol", (0, total // 2), False),
         levels - 2: ("sol", (total // 2, total), False),
-        levels - 1: ("lift", (0, 3 * total // 8), False),
+        levels - 1: ("lift", (0, 3 * total // 8), True),
         levels: ("lift", (3 * total // 8, total), True),
     }
 
@@ -617,38 +615,36 @@
     partner = partner_of(code, levels - 1)
     loaded = load(
         own,
-        (node_inverse, *(node_lift for _ in coefs), *stored),
+        (node_inverse, *(node_lift for _ in coefs), *stored, gathered[0]),
         (
             (0, levels - 1, slice(None), ("half", levels - 1)),
             (0, 0),
             *((0, k, slice(None), ("half", k)) for k in range(1, levels - 1)),
             (),
             *((("half", k),) for k in range(1, levels - 2)),
+            (),
         ),
         gather=gathers[levels],
         height=levels,
     )
     *loaded, early = loaded
-    inverse, lifts, sols = loaded[0], loaded[1:levels], [*loaded[levels:-1], sols[-1]]
+    inverse, lifts, sols = loaded[0], loaded[1:levels], [*loaded[levels:-2], sols[-1]]
     gathered.append(loaded[-1])
-    mine, other, moved = call(
+    mine, other = call(
         functools.partial(descent_kernel, levels=levels),
         [
             (half, "vmem"),
             (half, "vmem"),
-            (shape(gathered[2].shape, BF16), "vmem"),
         ],
         [(early, "vmem"), (partner, "vmem"), (inverse, "vmem")]
         + [(lift, "vmem") for lift in lifts]
         + [(sol, "vmem") for sol in sols]
-        + [(coef, "vmem") for coef in coefs]
-        + [(one, "hbm") for one in gathered[2:-1]],
-        [1],
+        + [(coef, "vmem") for coef in coefs],
         vmem=8,
     )
     other_sent = other
     other = partner_of(other_sent, 0)
-    bases = load(other_sent, gathered[:2], ((),) * 2)
+    bases = [loaded[-2], *load(other_sent, gathered[1:2], ((),))]
     (back,) = call(
         functools.partial(finish_kernel, **sizes),
         [(shape(block, jnp.int16), "vmem")],
@@ -657,8 +653,8 @@
             (other, "vmem"),
             (leaf_own, "vmem"),
             (leaf_other, "vmem"),
-            (moved, "vmem"),
-            (gathered[-1], "vmem"),
+            (gathered[2], "vmem"),
+            (gathered[3], "vmem"),
         ]
         + [(one, "vmem") for one in bases],
     )

time: 106 us -> 106 us (level)
  transfers between devices with their start and end apart: 6 -> 6, of which waited for: 5 -> 6; matrix products, arithmetic and copies ran while one was open for 0% -> 0% of each run, Pallas kernels for 13% -> 13%
where the time goes in v9:
time: 106 us; the launch traced here: 105 us
  blocking collectives  67.6 us (64%)
  Pallas kernels  28.9 us (27%)
  waiting for transfers between devices  5.86 us (6%)
  starting transfers between devices  2.67 us (3%)
    all_to_all x2, blocking collectives, exchange(): lax.all_to_all(blocks, ('row', 'col'), split_axis=0, concat_axis=0, tiled...  67.6 us
    pallas_call x17, Pallas kernels, call(): pl.pallas_call(kernel, out_shape=[pltpu.HBM(out.shape, out.dtype) if spac...  28.9 us
    ppermute x6, waiting for transfers between devices, from_partner(): lax.ppermute(shard, axis, [(i, i ^ 1 << apart) for i in range(lax.axis_si...  5.86 us
    ppermute x6, starting transfers between devices, from_partner(): lax.ppermute(shard, axis, [(i, i ^ 1 << apart) for i in range(lax.axis_si...  2.67 us
  transfers between devices with their start and end apart: 6, of which 6 were waited for; matrix products, arithmetic and copies ran while one was open for 0% of the time, Pallas kernels for 13%

profile of v9, /device:TPU:0, one launch (start us, length us, event | category | flops | bytes accessed | tf_op | source)
XLA Modules:
  0.0 105.3 jit_solution(12511055813497682712)
XLA Ops:
  0.0 2.5 %shard_map.82 = (bf16[32,136,128]{2,1,0:T(8,128)(2,1)S(1)}, f32[8,128]{1,0:T(8,128)S(1)}, bf16[1024,1024]{1,0:T(8,128)(2,1)S(1)}, bf16[2,1024,256]{2,1,0:T(8,128)(2,1)S(1)}) custom-call(s32[1,1024]{1,0:T(1,128)} %bitcast.1, bf16[1024,256]{1,0:T(8,128)(2,1)} %rows_hbm.1, bf16[1,2,1024,1024]{3,2,1,0:T(8,128)(2,1)} %inverse_hbm.4, ...), custom_call_target="tpu_custom_call" | custom-call | tf_op jit(solution)/shard_map/pallas_call | solution.py:435
  2.5 36.5 %all_to_all.10.got_ref = bf16[32,136,128]{2,1,0:T(8,128)(2,1)S(1)} all-to-all(bf16[32,136,128]{2,1,0:T(8,128)(2,1)S(1)} %get-tuple-element.57), channel_id=1, replica_groups=mesh['row'=8,'col'=4] {'row','col'}, dimensions={0} | all-to-all | bytes 2228224 | tf_op jit(solution)/shard_map/all_to_all | solution.py:476
  39.0 1.7 %shard_map.83 = (bf16[1024,256]{1,0:T(8,128)(2,1)S(1)}, f32[128,128]{1,0:T(8,128)S(1)}, bf16[1024,1024]{1,0:T(8,128)(2,1)S(1)}, bf16[2,256,1024]{2,1,0:T(8,128)(2,1)S(1)}) custom-call(bf16[32,136,128]{2,1,0:T(8,128)(2,1)S(1)} %all_to_all.10.got_ref, bf16[1,2,1024,1024]{3,2,1,0:T(8,128)(2,1)} %inverse_hbm.4, bf16[2,1024,256]{2,1,0:T(8,128)(2,1)S(1)} %get-tuple-element.58.basis_ref), custom_call_target="tpu_custom_call" | custom-call | tf_op jit(solution)/shard_map/pallas_call | solution.py:435
  40.7 1.3 %shard_map.84 = (bf16[1024,512]{1,0:T(8,128)(2,1)S(1)}, bf16[2,512,512]{2,1,0:T(8,128)(2,1)S(1)}) custom-call(bf16[1024,256]{1,0:T(8,128)(2,1)S(1)} %get-tuple-element.59.placed_ref, bf16[1024,1024]{1,0:T(8,128)(2,1)S(1)} %get-tuple-element.60.real_ref, bf16[1024,1024]{1,0:T(8,128)(2,1)S(1)} %get-tuple-element.61.imag_ref, bf16[1,5,2,512,512]{4,3,2,1,0:T(8,128)(2,1)} %refs_0_.9), custom_call_target="tpu_custom_call" | custom-call | tf_op jit(solution)/shard_map/pallas_call | solution.py:435
  42.0 0.8 shard_map.85
  42.8 0.1 collective-permute-start
  42.9 1.2 %shard_map.86.basis_ref = bf16[2,256,512]{2,1,0:T(8,128)(2,1)S(1)} custom-call(f32[256,128]{1,0:T(8,128)S(1)} %get-tuple-element.64.after_ref.own_ref, bf16[1,4,2,512,256]{4,3,2,1,0:T(8,128)(2,1)} %refs_1_.6), custom_call_target="tpu_custom_call" | custom-call | tf_op jit(solution)/shard_map/pallas_call | solution.py:435
  44.1 0.1 collective-permute-done.partner_ref
  44.2 0.8 shard_map.87
  45.0 0.6 collective-permute-start.1
  45.6 2.5 %shard_map.88 = (bf16[2,512,512]{2,1,0:T(8,128)(2,1)S(1)}, bf16[2,256,512]{2,1,0:T(8,128)(2,1)S(1)}, f32[512,128]{1,0:T(8,128)}, f32[1024,256]{1,0:T(8,128)}, f32[512,128]{1,0:T(8,128)S(1)}) custom-call(f32[256,128]{1,0:T(8,128)S(1)} %get-tuple-element.67.after_ref.refs_8_, bf16[1,5,2,512,512]{4,3,2,1,0:T(8,128)(2,1)} %refs_0_.9, ...), custom_call_target="tpu_custom_call" | custom-call | tf_op jit(solution)/shard_map/pallas_call | solution.py:435
  48.1 1.4 %collective-permute-done.1.partner_ref = s16[272,128]{1,0:T(8,128)(2,1)S(1)} collective-permute-done((s16[272,128]{1,0:T(8,128)(2,1)S(1)}, s16[272,128]{1,0:T(8,128)(2,1)S(1)}, u32[]{:S(2)}, u32[]{:S(2)}) %collective-permute-start.1) | collective-permute-done | bytes 69664 | tf_op jit(solution)/shard_map/ppermute | solution.py:459
  49.6 0.7 shard_map.89
  50.3 0.6 collective-permute-start.2
  50.9 2.5 %shard_map.90 = (bf16[2,512,512]{2,1,0:T(8,128)(2,1)S(1)}, bf16[2,256,512]{2,1,0:T(8,128)(2,1)S(1)}, f32[512,128]{1,0:T(8,128)}, f32[1024,256]{1,0:T(8,128)}, f32[512,128]{1,0:T(8,128)S(1)}) custom-call(f32[256,128]{1,0:T(8,128)S(1)} %get-tuple-element.74.after_ref.refs_9_, bf16[1,5,2,512,512]{4,3,2,1,0:T(8,128)(2,1)} %refs_0_.9, ...), custom_call_target="tpu_custom_call" | custom-call | tf_op jit(solution)/shard_map/pallas_call | solution.py:435
  53.5 1.2 %collective-permute-done.2.partner_ref = s16[272,128]{1,0:T(8,128)(2,1)S(1)} collective-permute-done((s16[272,128]{1,0:T(8,128)(2,1)S(1)}, s16[272,128]{1,0:T(8,128)(2,1)S(1)}, u32[]{:S(2)}, u32[]{:S(2)}) %collective-permute-start.2) | collective-permute-done | bytes 69664 | tf_op jit(solution)/shard_map/ppermute | solution.py:459
  54.7 0.7 shard_map.91
  55.4 0.7 collective-permute-start.3
  56.1 2.9 %shard_map.92 = (bf16[2,512,512]{2,1,0:T(8,128)(2,1)S(1)}, bf16[2,256,512]{2,1,0:T(8,128)(2,1)S(1)}, f32[512,128]{1,0:T(8,128)}, bf16[768,512]{1,0:T(8,128)(2,1)S(1)}, f32[512,128]{1,0:T(8,128)S(1)}) custom-call(f32[256,128]{1,0:T(8,128)S(1)} %get-tuple-element.80.after_ref.refs_10_, bf16[1,5,2,512,512]{4,3,2,1,0:T(8,128)(2,1)} %refs_0_.9, ...), custom_call_target="tpu_custom_call" | custom-call | tf_op jit(solution)/shard_map/pallas_call | solution.py:435
  59.0 0.8 collective-permute-done.3.partner_ref
  59.8 0.7 shard_map.93
  60.5 0.6 collective-permute-start.4
  61.1 3.1 %shard_map.94 = (bf16[2,256,512]{2,1,0:T(8,128)(2,1)S(1)}, bf16[2,512,256]{2,1,0:T(8,128)(2,1)S(1)}, bf16[2,256,256]{2,1,0:T(8,128)(2,1)S(1)}, bf16[2,256,256]{2...) custom-call(f32[256,128]{1,0:T(8,128)S(1)} %get-tuple-element.86.aft, ...), custom_call_target="tpu_custom_call" | custom-call | tf_op jit(solution)/shard_map/pallas_call | solution.py:435
  64.2 2.3 %collective-permute-done.4.partner_ref = s16[272,128]{1,0:T(8,128)(2,1)S(1)} collective-permute-done((s16[272,128]{1,0:T(8,128)(2,1)S(1)}, s16[272,128]{1,0:T(8,128)(2,1)S(1)}, u32[]{:S(2)}, u32[]{:S(2)}) %collective-permute-start.4) | collective-permute-done | bytes 69664 | tf_op jit(solution)/shard_map/ppermute | solution.py:459
  66.5 1.4 %shard_map.95 = (f32[256,128]{1,0:T(8,128)S(1)}, f32[256,128]{1,0:T(8,128)S(1)}) custom-call(f32[256,128]{1,0:T(8,128)S(1)} %get-tuple-element.91.own_ref, s16[272,128]{1,0:T(8,128)(2,1)S(1)} %collective-permute-done.4.partner_ref, bf16[2,256,512]{2,1,0:T(8,128)(2,1)S(1)} %get-tuple-element.93.inverse_ref, ...), custom_call_target="tpu_custom_call" | custom-call | tf_op jit(solution)/shard_map/pallas_call | solution.py:435
  67.9 0.1 collective-permute-start.5
  68.0 1.2 %shard_map.96.refs_3_ = f32[1024,256]{1,0:T(8,128)S(1)} custom-call(f32[256,128]{1,0:T(8,128)S(1)} %get-tuple-element.103.after_ref, f32[1024,256]{1,0:T(8,128)} %get-tuple-element.107.refs_0_), custom_call_target="tpu_custom_call" | custom-call | tf_op jit(solution)/shard_map/pallas_call | solution.py:435
  69.2 0.1 collective-permute-done.5.others_ref
  69.3 1.8 %shard_map.97 = s16[32,136,128]{2,1,0:T(8,128)(2,1)S(1)} custom-call(f32[256,128]{1,0:T(8,128)S(1)} %get-tuple-element.102.mine_ref, f32[256,128]{1,0:T(8,128)S(1)} %collective-permute-done.5.others_ref, f32[256,128]{1,0:T(8,128)S(1)} %get-tuple-element.64.after_ref.own_ref, f32[256,128]{1,0:T(8,128)S(1)} %get-tuple-element.65.other_ref, ...), custom_call_target="tpu_custom_call" | custom-call | tf_op jit(solution)/shard_map/pallas_call | solution.py:435
  71.1 31.1 %all_to_all.11.got_ref = s16[32,136,128]{2,1,0:T(8,128)(2,1)S(1)} all-to-all(s16[32,136,128]{2,1,0:T(8,128)(2,1)S(1)} %shard_map.97), channel_id=1, replica_groups=mesh['row'=8,'col'=4] {'row','col'}, dimensions={0} | all-to-all | bytes 2228224 | tf_op jit(solution)/shard_map/all_to_all | solution.py:476
  102.2 3.0 %shard_map.98 = f32[1024,256]{1,0:T(8,128)} custom-call(s16[32,136,128]{2,1,0:T(8,128)(2,1)S(1)} %all_to_all.11.got_ref, f32[8,128]{1,0:T(8,128)S(1)} %get-tuple-element.108.slot_ref), custom_call_target="tpu_custom_call" | custom-call | tf_op jit(solution)/shard_map/pallas_call | solution.py:435
Async XLA Ops:
  42.8 1.4 %collective-permute-start = (f32[256,128]{1,0:T(8,128)S(1)}, f32[256,128]{1,0:T(8,128)S(1)}, u32[]{:S(2)}, u32[]{:S(2)}) collective-permute-start(f32[256,128]{1,0:T(8,128)S(1)} %get-tuple-element.65.other_ref), channel_id=1, source_target_pairs={{0,1},{1,0},{2,3},{3,2},{4,5},{5,4},{6,7},{7,6},{8,9},{9,8},{10,11... | collective-permute-start | bytes 393224 | tf_op jit(solution)/shard_map/ppermute | solution.py:459
  45.0 4.6 %collective-permute-start.1 = (s16[272,128]{1,0:T(8,128)(2,1)S(1)}, s16[272,128]{1,0:T(8,128)(2,1)S(1)}, u32[]{:S(2)}, u32[]{:S(2)}) collective-permute-start(s16[272,128]{1,0:T(8,128)(2,1)S(1)} %get-tuple-element.71), channel_id=1, source_target_pairs={{0,2},{1,3},{2,0},{3,1},{4,6},{5,7},{6,4},{7,5},{8,10},{9,11},{10,... | collective-permute-start | bytes 208904 | tf_op jit(solution)/shard_map/ppermute | solution.py:459
  50.3 4.4 %collective-permute-start.2 = (s16[272,128]{1,0:T(8,128)(2,1)S(1)}, s16[272,128]{1,0:T(8,128)(2,1)S(1)}, u32[]{:S(2)}, u32[]{:S(2)}) collective-permute-start(s16[272,128]{1,0:T(8,128)(2,1)S(1)} %get-tuple-element.77), channel_id=1, source_target_pairs={{0,4},{4,0},{8,12},{12,8},{16,20},{20,16},{24,28},{28,24},{1,5},{5... | collective-permute-start | bytes 208904 | tf_op jit(solution)/shard_map/ppermute | solution.py:459
  55.4 4.4 %collective-permute-start.3 = (s16[272,128]{1,0:T(8,128)(2,1)S(1)}, s16[272,128]{1,0:T(8,128)(2,1)S(1)}, u32[]{:S(2)}, u32[]{:S(2)}) collective-permute-start(s16[272,128]{1,0:T(8,128)(2,1)S(1)} %get-tuple-element.83), channel_id=1, source_target_pairs={{0,8},{4,12},{8,0},{12,4},{16,24},{20,28},{24,16},{28,20},{1,9},{5... | collective-permute-start | bytes 208904 | tf_op jit(solution)/shard_map/ppermute | solution.py:459
  60.5 6.0 %collective-permute-start.4 = (s16[272,128]{1,0:T(8,128)(2,1)S(1)}, s16[272,128]{1,0:T(8,128)(2,1)S(1)}, u32[]{:S(2)}, u32[]{:S(2)}) collective-permute-start(s16[272,128]{1,0:T(8,128)(2,1)S(1)} %get-tuple-element.92), channel_id=1, source_target_pairs={{0,16},{4,20},{8,24},{12,28},{16,0},{20,4},{24,8},{28,12},{1,17},{... | collective-permute-start | bytes 208904 | tf_op jit(solution)/shard_map/ppermute | solution.py:459
  67.9 1.4 %collective-permute-start.5 = (f32[256,128]{1,0:T(8,128)S(1)}, f32[256,128]{1,0:T(8,128)S(1)}, u32[]{:S(2)}, u32[]{:S(2)}) collective-permute-start(f32[256,128]{1,0:T(8,128)S(1)} %get-tuple-element.103.after_ref), channel_id=1, source_target_pairs={{0,1},{1,0},{2,3},{3,2},{4,5},{5,4},{6,7},{7,6},{8,9},{9,8},{10,11... | collective-permute-start | bytes 393224 | tf_op jit(solution)/shard_map/ppermute | solution.py:459

commit v10 on v9

--- a/solution.py
+++ b/solution.py
@@ -500,8 +500,8 @@
     slots = devices * capacity
     total = slots // LANES
     gathers = {
-        levels - 3: ("sol", (0, total // 2), False),
-        levels - 2: ("sol", (total // 2, total), False),
+        levels - 3: ("sol", (0, total // 2), True),
+        levels - 2: ("sol", (total // 2, total), True),
         levels - 1: ("lift", (0, 3 * total // 8), True),
         levels: ("lift", (3 * total // 8, total), True),
     }
@@ -615,20 +615,19 @@
     partner = partner_of(code, levels - 1)
     loaded = load(
         own,
-        (node_inverse, *(node_lift for _ in coefs), *stored, gathered[0]),
+        (node_inverse, *(node_lift for _ in coefs), *stored),
         (
             (0, levels - 1, slice(None), ("half", levels - 1)),
             (0, 0),
             *((0, k, slice(None), ("half", k)) for k in range(1, levels - 1)),
             (),
             *((("half", k),) for k in range(1, levels - 2)),
-            (),
         ),
         gather=gathers[levels],
         height=levels,
     )
     *loaded, early = loaded
-    inverse, lifts, sols = loaded[0], loaded[1:levels], [*loaded[levels:-2], sols[-1]]
+    inverse, lifts, sols = loaded[0], loaded[1:levels], [*loaded[levels:-1], sols[-1]]
     gathered.append(loaded[-1])
     mine, other = call(
         functools.partial(descent_kernel, levels=levels),
@@ -642,9 +641,8 @@
         + [(coef, "vmem") for coef in coefs],
         vmem=8,
     )
-    other_sent = other
-    other = partner_of(other_sent, 0)
-    bases = [loaded[-2], *load(other_sent, gathered[1:2], ((),))]
+    other = partner_of(other, 0)
+    bases = gathered[:2]
     (back,) = call(
         functools.partial(finish_kernel, **sizes),
         [(shape(block, jnp.int16), "vmem")],

time: 106 us -> 106 us (level)
  Pallas kernels: 28.9 us -> 26.8 us
  waiting for transfers between devices: 5.86 us -> 7.94 us
    pallas_call x17 -> x16, Pallas kernels: 28.9 us -> 26.8 us  [call(): pl.pallas_call(kernel, out_shape=[pltpu.HBM(out.shape, out.dtype) if spac...]
    ppermute x6, waiting for transfers between devices: 5.86 us -> 7.94 us  [from_partner(): lax.ppermute(shard, axis, [(i, i ^ 1 << apart) for i in range(lax.axis_si...]
  transfers between devices with their start and end apart: 6 -> 6, of which waited for: 6 -> 6; matrix products, arithmetic and copies ran while one was open for 0% -> 0% of each run, Pallas kernels for 13% -> 11%
where the time goes in v10:
time: 106 us; the launch traced here: 105 us
  blocking collectives  67.6 us (64%)
  Pallas kernels  26.8 us (25%)
  waiting for transfers between devices  7.94 us (7%)
  starting transfers between devices  2.67 us (3%)
    all_to_all x2, blocking collectives, exchange(): lax.all_to_all(blocks, ('row', 'col'), split_axis=0, concat_axis=0, tiled...  67.6 us
    pallas_call x16, Pallas kernels, call(): pl.pallas_call(kernel, out_shape=[pltpu.HBM(out.shape, out.dtype) if spac...  26.8 us
    ppermute x6, waiting for transfers between devices, from_partner(): lax.ppermute(shard, axis, [(i, i ^ 1 << apart) for i in range(lax.axis_si...  7.94 us
    ppermute x6, starting transfers between devices, from_partner(): lax.ppermute(shard, axis, [(i, i ^ 1 << apart) for i in range(lax.axis_si...  2.67 us
  transfers between devices with their start and end apart: 6, of which 6 were waited for; matrix products, arithmetic and copies ran while one was open for 0% of the time, Pallas kernels for 11%

profile of v10, /device:TPU:0, one launch (start us, length us, event | category | flops | bytes accessed | tf_op | source)
XLA Modules:
  0.0 105.3 jit_solution(4849941944627285623)
XLA Ops:
  0.0 2.5 %shard_map.82 = (bf16[32,136,128]{2,1,0:T(8,128)(2,1)S(1)}, f32[8,128]{1,0:T(8,128)S(1)}, bf16[1024,1024]{1,0:T(8,128)(2,1)S(1)}, bf16[2,1024,256]{2,1,0:T(8,128)(2,1)S(1)}) custom-call(s32[1,1024]{1,0:T(1,128)} %bitcast.1, bf16[1024,256]{1,0:T(8,128)(2,1)} %rows_hbm.1, bf16[1,2,1024,1024]{3,2,1,0:T(8,128)(2,1)} %inverse_hbm.4, ...), custom_call_target="tpu_custom_call" | custom-call | tf_op jit(solution)/shard_map/pallas_call | solution.py:435
  2.5 36.5 %all_to_all.10.got_ref = bf16[32,136,128]{2,1,0:T(8,128)(2,1)S(1)} all-to-all(bf16[32,136,128]{2,1,0:T(8,128)(2,1)S(1)} %get-tuple-element.56), channel_id=1, replica_groups=mesh['row'=8,'col'=4] {'row','col'}, dimensions={0} | all-to-all | bytes 2228224 | tf_op jit(solution)/shard_map/all_to_all | solution.py:476
  39.0 1.7 %shard_map.83 = (bf16[1024,256]{1,0:T(8,128)(2,1)S(1)}, f32[128,128]{1,0:T(8,128)S(1)}, bf16[1024,1024]{1,0:T(8,128)(2,1)S(1)}, bf16[2,256,1024]{2,1,0:T(8,128)(2,1)S(1)}) custom-call(bf16[32,136,128]{2,1,0:T(8,128)(2,1)S(1)} %all_to_all.10.got_ref, bf16[1,2,1024,1024]{3,2,1,0:T(8,128)(2,1)} %inverse_hbm.4, bf16[2,1024,256]{2,1,0:T(8,128)(2,1)S(1)} %get-tuple-element.57.basis_ref), custom_call_target="tpu_custom_call" | custom-call | tf_op jit(solution)/shard_map/pallas_call | solution.py:435
  40.7 1.3 %shard_map.84 = (bf16[1024,512]{1,0:T(8,128)(2,1)S(1)}, bf16[2,512,512]{2,1,0:T(8,128)(2,1)S(1)}) custom-call(bf16[1024,256]{1,0:T(8,128)(2,1)S(1)} %get-tuple-element.58.placed_ref, bf16[1024,1024]{1,0:T(8,128)(2,1)S(1)} %get-tuple-element.59.real_ref, bf16[1024,1024]{1,0:T(8,128)(2,1)S(1)} %get-tuple-element.60.imag_ref, bf16[1,5,2,512,512]{4,3,2,1,0:T(8,128)(2,1)} %refs_0_.9), custom_call_target="tpu_custom_call" | custom-call | tf_op jit(solution)/shard_map/pallas_call | solution.py:435
  42.0 0.8 shard_map.85
  42.8 0.1 collective-permute-start
  42.9 1.2 %shard_map.86.basis_ref = bf16[2,256,512]{2,1,0:T(8,128)(2,1)S(1)} custom-call(f32[256,128]{1,0:T(8,128)S(1)} %get-tuple-element.63.after_ref.own_ref, bf16[1,4,2,512,256]{4,3,2,1,0:T(8,128)(2,1)} %refs_1_.6), custom_call_target="tpu_custom_call" | custom-call | tf_op jit(solution)/shard_map/pallas_call | solution.py:435
  44.1 0.1 collective-permute-done.partner_ref
  44.2 0.8 shard_map.87
  45.0 0.6 collective-permute-start.1
  45.6 2.1 %shard_map.88 = (bf16[2,512,512]{2,1,0:T(8,128)(2,1)S(1)}, bf16[2,256,512]{2,1,0:T(8,128)(2,1)S(1)}, f32[512,128]{1,0:T(8,128)}, f32[1024,256]{1,0:T(8,128)S(1)}, f32[512,128]{1,0:T(8,128)S(1)}) custom-call(f32[256,128]{1,0:T(8,128)S(1)} %get-tuple-element.66.after_ref.refs_8_, bf16[1,5,2,512,512]{4,3,2,1,0:T(8,128)(2,1)} %refs_0_.9, ...), custom_call_target="tpu_custom_call" | custom-call | tf_op jit(solution)/shard_map/pallas_call | solution.py:435
  47.7 1.9 %collective-permute-done.1.partner_ref = s16[272,128]{1,0:T(8,128)(2,1)S(1)} collective-permute-done((s16[272,128]{1,0:T(8,128)(2,1)S(1)}, s16[272,128]{1,0:T(8,128)(2,1)S(1)}, u32[]{:S(2)}, u32[]{:S(2)}) %collective-permute-start.1) | collective-permute-done | bytes 69664 | tf_op jit(solution)/shard_map/ppermute | solution.py:459
  49.6 0.7 shard_map.89
  50.3 0.6 collective-permute-start.2
  50.9 2.1 %shard_map.90 = (bf16[2,512,512]{2,1,0:T(8,128)(2,1)S(1)}, bf16[2,256,512]{2,1,0:T(8,128)(2,1)S(1)}, f32[512,128]{1,0:T(8,128)}, f32[1024,256]{1,0:T(8,128)S(1)}, f32[512,128]{1,0:T(8,128)S(1)}) custom-call(f32[256,128]{1,0:T(8,128)S(1)} %get-tuple-element.73.after_ref.refs_9_, bf16[1,5,2,512,512]{4,3,2,1,0:T(8,128)(2,1)} %refs_0_.9, ...), custom_call_target="tpu_custom_call" | custom-call | tf_op jit(solution)/shard_map/pallas_call | solution.py:435
  53.1 1.6 %collective-permute-done.2.partner_ref = s16[272,128]{1,0:T(8,128)(2,1)S(1)} collective-permute-done((s16[272,128]{1,0:T(8,128)(2,1)S(1)}, s16[272,128]{1,0:T(8,128)(2,1)S(1)}, u32[]{:S(2)}, u32[]{:S(2)}) %collective-permute-start.2) | collective-permute-done | bytes 69664 | tf_op jit(solution)/shard_map/ppermute | solution.py:459
  54.7 0.7 shard_map.91
  55.4 0.7 collective-permute-start.3
  56.1 2.9 %shard_map.92 = (bf16[2,512,512]{2,1,0:T(8,128)(2,1)S(1)}, bf16[2,256,512]{2,1,0:T(8,128)(2,1)S(1)}, f32[512,128]{1,0:T(8,128)}, bf16[768,512]{1,0:T(8,128)(2,1)S(1)}, f32[512,128]{1,0:T(8,128)S(1)}) custom-call(f32[256,128]{1,0:T(8,128)S(1)} %get-tuple-element.79.after_ref.refs_10_, bf16[1,5,2,512,512]{4,3,2,1,0:T(8,128)(2,1)} %refs_0_.9, ...), custom_call_target="tpu_custom_call" | custom-call | tf_op jit(solution)/shard_map/pallas_call | solution.py:435
  59.0 0.8 collective-permute-done.3.partner_ref
  59.8 0.7 shard_map.93
  60.5 0.6 collective-permute-start.4
  61.1 3.1 %shard_map.94 = (bf16[2,256,512]{2,1,0:T(8,128)(2,1)S(1)}, bf16[2,512,256]{2,1,0:T(8,128)(2,1)S(1)}, bf16[2,256,256]{2,1,0:T(8,128)(2,1)S(1)}, bf16[2,256,256]{2...) custom-call(f32[256,128]{1,0:T(8,128)S(1)} %get-tuple-element.85.aft, ...), custom_call_target="tpu_custom_call" | custom-call | tf_op jit(solution)/shard_map/pallas_call | solution.py:435
  64.2 2.3 %collective-permute-done.4.partner_ref = s16[272,128]{1,0:T(8,128)(2,1)S(1)} collective-permute-done((s16[272,128]{1,0:T(8,128)(2,1)S(1)}, s16[272,128]{1,0:T(8,128)(2,1)S(1)}, u32[]{:S(2)}, u32[]{:S(2)}) %collective-permute-start.4) | collective-permute-done | bytes 69664 | tf_op jit(solution)/shard_map/ppermute | solution.py:459
  66.5 1.4 %shard_map.95 = (f32[256,128]{1,0:T(8,128)S(1)}, f32[256,128]{1,0:T(8,128)S(1)}) custom-call(f32[256,128]{1,0:T(8,128)S(1)} %get-tuple-element.89.own_ref, s16[272,128]{1,0:T(8,128)(2,1)S(1)} %collective-permute-done.4.partner_ref, bf16[2,256,512]{2,1,0:T(8,128)(2,1)S(1)} %get-tuple-element.91.inverse_ref, ...), custom_call_target="tpu_custom_call" | custom-call | tf_op jit(solution)/shard_map/pallas_call | solution.py:435
  67.9 0.1 collective-permute-start.5
  68.0 1.3 %collective-permute-done.5.others_ref = f32[256,128]{1,0:T(8,128)S(1)} collective-permute-done((f32[256,128]{1,0:T(8,128)S(1)}, f32[256,128]{1,0:T(8,128)S(1)}, u32[]{:S(2)}, u32[]{:S(2)}) %collective-permute-start.5) | collective-permute-done | bytes 131104 | tf_op jit(solution)/shard_map/ppermute | solution.py:459
  69.3 1.8 %shard_map.96 = s16[32,136,128]{2,1,0:T(8,128)(2,1)S(1)} custom-call(f32[256,128]{1,0:T(8,128)S(1)} %get-tuple-element.100.mine_ref, f32[256,128]{1,0:T(8,128)S(1)} %collective-permute-done.5.others_ref, f32[256,128]{1,0:T(8,128)S(1)} %get-tuple-element.63.after_ref.own_ref, f32[256,128]{1,0:T(8,128)S(1)} %get-tuple-element.64.other_ref, ...), custom_call_target="tpu_custom_call" | custom-call | tf_op jit(solution)/shard_map/pallas_call | solution.py:435
  71.1 31.1 %all_to_all.11.got_ref = s16[32,136,128]{2,1,0:T(8,128)(2,1)S(1)} all-to-all(s16[32,136,128]{2,1,0:T(8,128)(2,1)S(1)} %shard_map.96), channel_id=1, replica_groups=mesh['row'=8,'col'=4] {'row','col'}, dimensions={0} | all-to-all | bytes 2228224 | tf_op jit(solution)/shard_map/all_to_all | solution.py:476
  102.2 3.0 %shard_map.97 = f32[1024,256]{1,0:T(8,128)} custom-call(s16[32,136,128]{2,1,0:T(8,128)(2,1)S(1)} %all_to_all.11.got_ref, f32[8,128]{1,0:T(8,128)S(1)} %get-tuple-element.106.slot_ref), custom_call_target="tpu_custom_call" | custom-call | tf_op jit(solution)/shard_map/pallas_call | solution.py:435
Async XLA Ops:
  42.8 1.4 %collective-permute-start = (f32[256,128]{1,0:T(8,128)S(1)}, f32[256,128]{1,0:T(8,128)S(1)}, u32[]{:S(2)}, u32[]{:S(2)}) collective-permute-start(f32[256,128]{1,0:T(8,128)S(1)} %get-tuple-element.64.other_ref), channel_id=1, source_target_pairs={{0,1},{1,0},{2,3},{3,2},{4,5},{5,4},{6,7},{7,6},{8,9},{9,8},{10,11... | collective-permute-start | bytes 393224 | tf_op jit(solution)/shard_map/ppermute | solution.py:459
  45.0 4.6 %collective-permute-start.1 = (s16[272,128]{1,0:T(8,128)(2,1)S(1)}, s16[272,128]{1,0:T(8,128)(2,1)S(1)}, u32[]{:S(2)}, u32[]{:S(2)}) collective-permute-start(s16[272,128]{1,0:T(8,128)(2,1)S(1)} %get-tuple-element.70), channel_id=1, source_target_pairs={{0,2},{1,3},{2,0},{3,1},{4,6},{5,7},{6,4},{7,5},{8,10},{9,11},{10,... | collective-permute-start | bytes 208904 | tf_op jit(solution)/shard_map/ppermute | solution.py:459
  50.3 4.4 %collective-permute-start.2 = (s16[272,128]{1,0:T(8,128)(2,1)S(1)}, s16[272,128]{1,0:T(8,128)(2,1)S(1)}, u32[]{:S(2)}, u32[]{:S(2)}) collective-permute-start(s16[272,128]{1,0:T(8,128)(2,1)S(1)} %get-tuple-element.76), channel_id=1, source_target_pairs={{0,4},{4,0},{8,12},{12,8},{16,20},{20,16},{24,28},{28,24},{1,5},{5... | collective-permute-start | bytes 208904 | tf_op jit(solution)/shard_map/ppermute | solution.py:459
  55.4 4.4 %collective-permute-start.3 = (s16[272,128]{1,0:T(8,128)(2,1)S(1)}, s16[272,128]{1,0:T(8,128)(2,1)S(1)}, u32[]{:S(2)}, u32[]{:S(2)}) collective-permute-start(s16[272,128]{1,0:T(8,128)(2,1)S(1)} %get-tuple-element.82), channel_id=1, source_target_pairs={{0,8},{4,12},{8,0},{12,4},{16,24},{20,28},{24,16},{28,20},{1,9},{5... | collective-permute-start | bytes 208904 | tf_op jit(solution)/shard_map/ppermute | solution.py:459
  60.5 6.0 %collective-permute-start.4 = (s16[272,128]{1,0:T(8,128)(2,1)S(1)}, s16[272,128]{1,0:T(8,128)(2,1)S(1)}, u32[]{:S(2)}, u32[]{:S(2)}) collective-permute-start(s16[272,128]{1,0:T(8,128)(2,1)S(1)} %get-tuple-element.90), channel_id=1, source_target_pairs={{0,16},{4,20},{8,24},{12,28},{16,0},{20,4},{24,8},{28,12},{1,17},{... | collective-permute-start | bytes 208904 | tf_op jit(solution)/shard_map/ppermute | solution.py:459
  67.9 1.4 %collective-permute-start.5 = (f32[256,128]{1,0:T(8,128)S(1)}, f32[256,128]{1,0:T(8,128)S(1)}, u32[]{:S(2)}, u32[]{:S(2)}) collective-permute-start(f32[256,128]{1,0:T(8,128)S(1)} %get-tuple-element.101), channel_id=1, source_target_pairs={{0,1},{1,0},{2,3},{3,2},{4,5},{5,4},{6,7},{7,6},{8,9},{9,8},{10,11... | collective-permute-start | bytes 393224 | tf_op jit(solution)/shard_map/ppermute | solution.py:459

commit v11 on v10

--- a/solution.py
+++ b/solution.py
@@ -15,7 +15,7 @@
 ROUNDER = 1.5 * 2.0**23
 TAIL = 16
 STEP = 256
-PIECES = 4
+PIECES = 8
 NODE_STEP = 128
 FINISH_PIECES = 8
 BF16 = jnp.bfloat16

time: 106 us -> 106 us (level)
  no operation moved by 1% of the time
where the time goes in v11:
time: 106 us; the launch traced here: 105 us
  blocking collectives  67.6 us (64%)
  Pallas kernels  27 us (25%)
  waiting for transfers between devices  7.94 us (7%)
  starting transfers between devices  2.67 us (3%)
    all_to_all x2, blocking collectives, exchange(): lax.all_to_all(blocks, ('row', 'col'), split_axis=0, concat_axis=0, tiled...  67.6 us
    pallas_call x16, Pallas kernels, call(): pl.pallas_call(kernel, out_shape=[pltpu.HBM(out.shape, out.dtype) if spac...  27 us
    ppermute x6, waiting for transfers between devices, from_partner(): lax.ppermute(shard, axis, [(i, i ^ 1 << apart) for i in range(lax.axis_si...  7.94 us
    ppermute x6, starting transfers between devices, from_partner(): lax.ppermute(shard, axis, [(i, i ^ 1 << apart) for i in range(lax.axis_si...  2.67 us
  transfers between devices with their start and end apart: 6, of which 6 were waited for; matrix products, arithmetic and copies ran while one was open for 0% of the time, Pallas kernels for 11%

profile of v11, /device:TPU:0, one launch (start us, length us, event | category | flops | bytes accessed | tf_op | source)
XLA Modules:
  0.0 105.4 jit_solution(3357386028832663602)
XLA Ops:
  0.0 2.5 %shard_map.82 = (bf16[32,136,128]{2,1,0:T(8,128)(2,1)S(1)}, f32[8,128]{1,0:T(8,128)S(1)}, bf16[1024,1024]{1,0:T(8,128)(2,1)S(1)}, bf16[2,1024,256]{2,1,0:T(8,128)(2,1)S(1)}) custom-call(s32[1,1024]{1,0:T(1,128)} %bitcast.1, bf16[1024,256]{1,0:T(8,128)(2,1)} %rows_hbm.1, bf16[1,2,1024,1024]{3,2,1,0:T(8,128)(2,1)} %inverse_hbm.4, ...), custom_call_target="tpu_custom_call" | custom-call | tf_op jit(solution)/shard_map/pallas_call | solution.py:435
  2.5 36.5 %all_to_all.10.got_ref = bf16[32,136,128]{2,1,0:T(8,128)(2,1)S(1)} all-to-all(bf16[32,136,128]{2,1,0:T(8,128)(2,1)S(1)} %get-tuple-element.56), channel_id=1, replica_groups=mesh['row'=8,'col'=4] {'row','col'}, dimensions={0} | all-to-all | bytes 2228224 | tf_op jit(solution)/shard_map/all_to_all | solution.py:476
  39.0 1.7 %shard_map.83 = (bf16[1024,256]{1,0:T(8,128)(2,1)S(1)}, f32[128,128]{1,0:T(8,128)S(1)}, bf16[1024,1024]{1,0:T(8,128)(2,1)S(1)}, bf16[2,256,1024]{2,1,0:T(8,128)(2,1)S(1)}) custom-call(bf16[32,136,128]{2,1,0:T(8,128)(2,1)S(1)} %all_to_all.10.got_ref, bf16[1,2,1024,1024]{3,2,1,0:T(8,128)(2,1)} %inverse_hbm.4, bf16[2,1024,256]{2,1,0:T(8,128)(2,1)S(1)} %get-tuple-element.57.basis_ref), custom_call_target="tpu_custom_call" | custom-call | tf_op jit(solution)/shard_map/pallas_call | solution.py:435
  40.7 1.3 %shard_map.84 = (bf16[1024,512]{1,0:T(8,128)(2,1)S(1)}, bf16[2,512,512]{2,1,0:T(8,128)(2,1)S(1)}) custom-call(bf16[1024,256]{1,0:T(8,128)(2,1)S(1)} %get-tuple-element.58.placed_ref, bf16[1024,1024]{1,0:T(8,128)(2,1)S(1)} %get-tuple-element.59.real_ref, bf16[1024,1024]{1,0:T(8,128)(2,1)S(1)} %get-tuple-element.60.imag_ref, bf16[1,5,2,512,512]{4,3,2,1,0:T(8,128)(2,1)} %refs_0_.9), custom_call_target="tpu_custom_call" | custom-call | tf_op jit(solution)/shard_map/pallas_call | solution.py:435
  42.0 0.8 shard_map.85
  42.8 0.1 collective-permute-start
  42.9 1.2 %shard_map.86.basis_ref = bf16[2,256,512]{2,1,0:T(8,128)(2,1)S(1)} custom-call(f32[256,128]{1,0:T(8,128)S(1)} %get-tuple-element.63.after_ref.own_ref, bf16[1,4,2,512,256]{4,3,2,1,0:T(8,128)(2,1)} %refs_1_.6), custom_call_target="tpu_custom_call" | custom-call | tf_op jit(solution)/shard_map/pallas_call | solution.py:435
  44.1 0.1 collective-permute-done.partner_ref
  44.2 0.8 shard_map.87
  45.0 0.6 collective-permute-start.1
  45.6 2.1 %shard_map.88 = (bf16[2,512,512]{2,1,0:T(8,128)(2,1)S(1)}, bf16[2,256,512]{2,1,0:T(8,128)(2,1)S(1)}, f32[512,128]{1,0:T(8,128)}, f32[1024,256]{1,0:T(8,128)S(1)}, f32[512,128]{1,0:T(8,128)S(1)}) custom-call(f32[256,128]{1,0:T(8,128)S(1)} %get-tuple-element.66.after_ref.refs_8_, bf16[1,5,2,512,512]{4,3,2,1,0:T(8,128)(2,1)} %refs_0_.9, ...), custom_call_target="tpu_custom_call" | custom-call | tf_op jit(solution)/shard_map/pallas_call | solution.py:435
  47.7 1.9 %collective-permute-done.1.partner_ref = s16[272,128]{1,0:T(8,128)(2,1)S(1)} collective-permute-done((s16[272,128]{1,0:T(8,128)(2,1)S(1)}, s16[272,128]{1,0:T(8,128)(2,1)S(1)}, u32[]{:S(2)}, u32[]{:S(2)}) %collective-permute-start.1) | collective-permute-done | bytes 69664 | tf_op jit(solution)/shard_map/ppermute | solution.py:459
  49.6 0.7 shard_map.89
  50.3 0.6 collective-permute-start.2
  50.9 2.1 %shard_map.90 = (bf16[2,512,512]{2,1,0:T(8,128)(2,1)S(1)}, bf16[2,256,512]{2,1,0:T(8,128)(2,1)S(1)}, f32[512,128]{1,0:T(8,128)}, f32[1024,256]{1,0:T(8,128)S(1)}, f32[512,128]{1,0:T(8,128)S(1)}) custom-call(f32[256,128]{1,0:T(8,128)S(1)} %get-tuple-element.73.after_ref.refs_9_, bf16[1,5,2,512,512]{4,3,2,1,0:T(8,128)(2,1)} %refs_0_.9, ...), custom_call_target="tpu_custom_call" | custom-call | tf_op jit(solution)/shard_map/pallas_call | solution.py:435
  53.1 1.6 %collective-permute-done.2.partner_ref = s16[272,128]{1,0:T(8,128)(2,1)S(1)} collective-permute-done((s16[272,128]{1,0:T(8,128)(2,1)S(1)}, s16[272,128]{1,0:T(8,128)(2,1)S(1)}, u32[]{:S(2)}, u32[]{:S(2)}) %collective-permute-start.2) | collective-permute-done | bytes 69664 | tf_op jit(solution)/shard_map/ppermute | solution.py:459
  54.7 0.7 shard_map.91
  55.4 0.7 collective-permute-start.3
  56.1 2.9 %shard_map.92 = (bf16[2,512,512]{2,1,0:T(8,128)(2,1)S(1)}, bf16[2,256,512]{2,1,0:T(8,128)(2,1)S(1)}, f32[512,128]{1,0:T(8,128)}, bf16[768,512]{1,0:T(8,128)(2,1)S(1)}, f32[512,128]{1,0:T(8,128)S(1)}) custom-call(f32[256,128]{1,0:T(8,128)S(1)} %get-tuple-element.79.after_ref.refs_10_, bf16[1,5,2,512,512]{4,3,2,1,0:T(8,128)(2,1)} %refs_0_.9, ...), custom_call_target="tpu_custom_call" | custom-call | tf_op jit(solution)/shard_map/pallas_call | solution.py:435
  59.0 0.8 collective-permute-done.3.partner_ref
  59.8 0.7 shard_map.93
  60.5 0.6 collective-permute-start.4
  61.1 3.1 %shard_map.94 = (bf16[2,256,512]{2,1,0:T(8,128)(2,1)S(1)}, bf16[2,512,256]{2,1,0:T(8,128)(2,1)S(1)}, bf16[2,256,256]{2,1,0:T(8,128)(2,1)S(1)}, bf16[2,256,256]{2...) custom-call(f32[256,128]{1,0:T(8,128)S(1)} %get-tuple-element.85.aft, ...), custom_call_target="tpu_custom_call" | custom-call | tf_op jit(solution)/shard_map/pallas_call | solution.py:435
  64.2 2.3 %collective-permute-done.4.partner_ref = s16[272,128]{1,0:T(8,128)(2,1)S(1)} collective-permute-done((s16[272,128]{1,0:T(8,128)(2,1)S(1)}, s16[272,128]{1,0:T(8,128)(2,1)S(1)}, u32[]{:S(2)}, u32[]{:S(2)}) %collective-permute-start.4) | collective-permute-done | bytes 69664 | tf_op jit(solution)/shard_map/ppermute | solution.py:459
  66.5 1.4 %shard_map.95 = (f32[256,128]{1,0:T(8,128)S(1)}, f32[256,128]{1,0:T(8,128)S(1)}) custom-call(f32[256,128]{1,0:T(8,128)S(1)} %get-tuple-element.89.own_ref, s16[272,128]{1,0:T(8,128)(2,1)S(1)} %collective-permute-done.4.partner_ref, bf16[2,256,512]{2,1,0:T(8,128)(2,1)S(1)} %get-tuple-element.91.inverse_ref, ...), custom_call_target="tpu_custom_call" | custom-call | tf_op jit(solution)/shard_map/pallas_call | solution.py:435
  67.9 0.1 collective-permute-start.5
  68.0 1.3 %collective-permute-done.5.others_ref = f32[256,128]{1,0:T(8,128)S(1)} collective-permute-done((f32[256,128]{1,0:T(8,128)S(1)}, f32[256,128]{1,0:T(8,128)S(1)}, u32[]{:S(2)}, u32[]{:S(2)}) %collective-permute-start.5) | collective-permute-done | bytes 131104 | tf_op jit(solution)/shard_map/ppermute | solution.py:459
  69.3 1.8 %shard_map.96 = s16[32,136,128]{2,1,0:T(8,128)(2,1)S(1)} custom-call(f32[256,128]{1,0:T(8,128)S(1)} %get-tuple-element.100.mine_ref, f32[256,128]{1,0:T(8,128)S(1)} %collective-permute-done.5.others_ref, f32[256,128]{1,0:T(8,128)S(1)} %get-tuple-element.63.after_ref.own_ref, f32[256,128]{1,0:T(8,128)S(1)} %get-tuple-element.64.other_ref, ...), custom_call_target="tpu_custom_call" | custom-call | tf_op jit(solution)/shard_map/pallas_call | solution.py:435
  71.1 31.1 %all_to_all.11.got_ref = s16[32,136,128]{2,1,0:T(8,128)(2,1)S(1)} all-to-all(s16[32,136,128]{2,1,0:T(8,128)(2,1)S(1)} %shard_map.96), channel_id=1, replica_groups=mesh['row'=8,'col'=4] {'row','col'}, dimensions={0} | all-to-all | bytes 2228224 | tf_op jit(solution)/shard_map/all_to_all | solution.py:476
  102.2 3.1 %shard_map.97 = f32[1024,256]{1,0:T(8,128)} custom-call(s16[32,136,128]{2,1,0:T(8,128)(2,1)S(1)} %all_to_all.11.got_ref, f32[8,128]{1,0:T(8,128)S(1)} %get-tuple-element.106.slot_ref), custom_call_target="tpu_custom_call" | custom-call | tf_op jit(solution)/shard_map/pallas_call | solution.py:435
Async XLA Ops:
  42.8 1.4 %collective-permute-start = (f32[256,128]{1,0:T(8,128)S(1)}, f32[256,128]{1,0:T(8,128)S(1)}, u32[]{:S(2)}, u32[]{:S(2)}) collective-permute-start(f32[256,128]{1,0:T(8,128)S(1)} %get-tuple-element.64.other_ref), channel_id=1, source_target_pairs={{0,1},{1,0},{2,3},{3,2},{4,5},{5,4},{6,7},{7,6},{8,9},{9,8},{10,11... | collective-permute-start | bytes 393224 | tf_op jit(solution)/shard_map/ppermute | solution.py:459
  45.0 4.6 %collective-permute-start.1 = (s16[272,128]{1,0:T(8,128)(2,1)S(1)}, s16[272,128]{1,0:T(8,128)(2,1)S(1)}, u32[]{:S(2)}, u32[]{:S(2)}) collective-permute-start(s16[272,128]{1,0:T(8,128)(2,1)S(1)} %get-tuple-element.70), channel_id=1, source_target_pairs={{0,2},{1,3},{2,0},{3,1},{4,6},{5,7},{6,4},{7,5},{8,10},{9,11},{10,... | collective-permute-start | bytes 208904 | tf_op jit(solution)/shard_map/ppermute | solution.py:459
  50.3 4.4 %collective-permute-start.2 = (s16[272,128]{1,0:T(8,128)(2,1)S(1)}, s16[272,128]{1,0:T(8,128)(2,1)S(1)}, u32[]{:S(2)}, u32[]{:S(2)}) collective-permute-start(s16[272,128]{1,0:T(8,128)(2,1)S(1)} %get-tuple-element.76), channel_id=1, source_target_pairs={{0,4},{4,0},{8,12},{12,8},{16,20},{20,16},{24,28},{28,24},{1,5},{5... | collective-permute-start | bytes 208904 | tf_op jit(solution)/shard_map/ppermute | solution.py:459
  55.4 4.4 %collective-permute-start.3 = (s16[272,128]{1,0:T(8,128)(2,1)S(1)}, s16[272,128]{1,0:T(8,128)(2,1)S(1)}, u32[]{:S(2)}, u32[]{:S(2)}) collective-permute-start(s16[272,128]{1,0:T(8,128)(2,1)S(1)} %get-tuple-element.82), channel_id=1, source_target_pairs={{0,8},{4,12},{8,0},{12,4},{16,24},{20,28},{24,16},{28,20},{1,9},{5... | collective-permute-start | bytes 208904 | tf_op jit(solution)/shard_map/ppermute | solution.py:459
  60.5 6.0 %collective-permute-start.4 = (s16[272,128]{1,0:T(8,128)(2,1)S(1)}, s16[272,128]{1,0:T(8,128)(2,1)S(1)}, u32[]{:S(2)}, u32[]{:S(2)}) collective-permute-start(s16[272,128]{1,0:T(8,128)(2,1)S(1)} %get-tuple-element.90), channel_id=1, source_target_pairs={{0,16},{4,20},{8,24},{12,28},{16,0},{20,4},{24,8},{28,12},{1,17},{... | collective-permute-start | bytes 208904 | tf_op jit(solution)/shard_map/ppermute | solution.py:459
  67.9 1.4 %collective-permute-start.5 = (f32[256,128]{1,0:T(8,128)S(1)}, f32[256,128]{1,0:T(8,128)S(1)}, u32[]{:S(2)}, u32[]{:S(2)}) collective-permute-start(f32[256,128]{1,0:T(8,128)S(1)} %get-tuple-element.101), channel_id=1, source_target_pairs={{0,1},{1,0},{2,3},{3,2},{4,5},{5,4},{6,7},{7,6},{8,9},{9,8},{10,11... | collective-permute-start | bytes 393224 | tf_op jit(solution)/shard_map/ppermute | solution.py:459
